TPU v7x, 32 devices: a whole 2x2x4 slice. The times are simulated.
32 devices in a mesh: seq: 16 (over z, y, x), head: 2 (over core).
Axes of the slice: x: 2, y: 2, z: 4, core: 2. Of those that a mesh axis runs over, the one named last changes fastest.
Arguments:
- queries: bfloat16 [4096, 384], P('seq', 'head'), may hold values from -15 to 15
- key_states: bfloat16 [4096, 384], P('seq', 'head'), may hold values from -15 to 15
- value_states: bfloat16 [4096, 384], P('seq', 'head'), may hold values from -6 to 6
- pool_weight: float32 [64], replicated, may hold values from -0.75 to 0.75
- out_grad: bfloat16 [4096, 384], P('seq', 'head'), may hold values from -12 to 12
Outputs:
- attended: bfloat16 [4096, 384], P('seq', 'head')
- query_grad: bfloat16 [4096, 384], P('seq', 'head')
- key_grad: bfloat16 [4096, 384], P('seq', 'head')
- value_grad: bfloat16 [4096, 384], P('seq', 'head')
- pool_grad: float32 [64], replicated
All inputs are finite; a program needn't handle non-finite values.
Results may differ from a plain program's by a relative error of at most 0.0045.
The roundings to bfloat16 on the way count: a program that leaves them out, or rounds other values in their place, can miss the bound.
Values may be sent and summed in bfloat16 or wider, within the bound.
No kernel may reach another device: no remote copies, remote signals or barrier semaphores. Data moves between devices by JAX's collectives and lax.ppermute only.
A program may use at most 64 MiB of HBM per device.

v0:
```python
import jax
import jax.numpy as jnp
from jax import lax
from jax.sharding import PartitionSpec as P

HEAD_DIM = 64
BLOCK = 64
SUM_DEV = 4


def extended(x, sides, width):
    for axis, dim in sides:
        devices, length = (lax.axis_size(axis), x.shape[dim])
        up = [(i, (i + 1) % devices) for i in range(devices - 1)]
        down = [(j, i) for i, j in up]
        last = lax.slice_in_dim(x, length - width, length, axis=dim)
        leading = lax.slice_in_dim(x, 0, width, axis=dim)
        before = lax.ppermute(last, axis, up)
        after = lax.ppermute(leading, axis, down)
        x = jnp.concatenate([before, x, after], axis=dim)
    return x


def make_windows(padded, block_count):
    span = block_count * BLOCK
    return jnp.concatenate(
        [
            padded[0:span].reshape(block_count, BLOCK, -1),
            padded[BLOCK : span + BLOCK].reshape(block_count, BLOCK, -1),
            padded[2 * BLOCK : span + 2 * BLOCK].reshape(block_count, BLOCK, -1),
        ],
        axis=1,
    )


def undo_windows(window, block_count):
    span = block_count * BLOCK
    first_part = jnp.pad(window[:, :BLOCK].reshape(span, -1), ((0, 2 * BLOCK), (0, 0)))
    middle_part = jnp.pad(window[:, BLOCK : 2 * BLOCK].reshape(span, -1), ((BLOCK, BLOCK), (0, 0)))
    last_part = jnp.pad(window[:, 2 * BLOCK :].reshape(span, -1), ((2 * BLOCK, 0), (0, 0)))
    return first_part + middle_part + last_part


def head_pass(
    query_head, key_ext, value_ext, global_key, global_value, grad_head, mask_first, mask_last
):
    scale = HEAD_DIM ** (-0.5)
    tok_rows = query_head.shape[0]
    block_count = tok_rows // BLOCK
    key_windows = make_windows(key_ext, block_count)
    value_windows = make_windows(value_ext, block_count)
    query_blocks = query_head.reshape(block_count, BLOCK, -1)
    grad_blocks = grad_head.reshape(block_count, BLOCK, -1)
    local_scores = (
        jnp.einsum("nbd,nkd->nbk", query_blocks, key_windows, preferred_element_type=jnp.float32)
        * scale
    )
    global_scores = (
        jnp.einsum("td,gd->tg", query_head, global_key, preferred_element_type=jnp.float32) * scale
    )
    block_ids = jnp.arange(block_count)[:, None, None]
    key_ids = jnp.arange(3 * BLOCK)[None, None, :]
    invalid = jnp.logical_or(
        jnp.logical_and(mask_first, jnp.logical_and(block_ids == 0, key_ids < BLOCK)),
        jnp.logical_and(
            mask_last, jnp.logical_and(block_ids == block_count - 1, key_ids >= 2 * BLOCK)
        ),
    )
    local_scores = jnp.where(invalid, -jnp.inf, local_scores)
    row_max = jnp.maximum(local_scores.max(-1).reshape(tok_rows), global_scores.max(-1))
    local_exp = jnp.exp(local_scores - row_max.reshape(block_count, BLOCK, 1))
    global_exp = jnp.exp(global_scores - row_max[:, None])
    totals = local_exp.sum(-1).reshape(tok_rows) + global_exp.sum(-1)
    local_weights = local_exp / totals.reshape(block_count, BLOCK, 1)
    global_weights = global_exp / totals[:, None]
    local_probs = local_weights.astype(jnp.bfloat16)
    global_probs = global_weights.astype(jnp.bfloat16)
    mixed = jnp.einsum(
        "nbk,nkd->nbd", local_probs, value_windows, preferred_element_type=jnp.float32
    ).reshape(tok_rows, -1)
    mixed = mixed + jnp.dot(global_probs, global_value, preferred_element_type=jnp.float32)
    attended = lax.optimization_barrier(mixed.astype(jnp.bfloat16))
    delta = jnp.sum(grad_head.astype(jnp.float32) * attended.astype(jnp.float32), axis=-1)
    local_dprob = jnp.einsum(
        "nbd,nkd->nbk", grad_blocks, value_windows, preferred_element_type=jnp.float32
    )
    global_dprob = jnp.einsum(
        "td,gd->tg", grad_head, global_value, preferred_element_type=jnp.float32
    )
    local_dscore = (
        local_weights * (local_dprob - delta.reshape(block_count, BLOCK, 1)) * scale
    ).astype(jnp.bfloat16)
    global_dscore = (global_weights * (global_dprob - delta[:, None]) * scale).astype(jnp.bfloat16)
    query_grad = jnp.einsum(
        "nbk,nkd->nbd", local_dscore, key_windows, preferred_element_type=jnp.float32
    ).reshape(tok_rows, -1)
    query_grad = (
        query_grad + jnp.dot(global_dscore, global_key, preferred_element_type=jnp.float32)
    ).astype(jnp.bfloat16)
    key_window_grad = jnp.einsum(
        "nbk,nbd->nkd", local_dscore, query_blocks, preferred_element_type=jnp.float32
    )
    value_window_grad = jnp.einsum(
        "nbk,nbd->nkd", local_probs, grad_blocks, preferred_element_type=jnp.float32
    )
    global_key_grad = jnp.einsum(
        "tg,td->gd", global_dscore, query_head, preferred_element_type=jnp.float32
    )
    global_value_grad = jnp.einsum(
        "tg,td->gd", global_probs, grad_head, preferred_element_type=jnp.float32
    )
    return (
        attended,
        query_grad,
        undo_windows(key_window_grad, block_count),
        undo_windows(value_window_grad, block_count),
        global_key_grad,
        global_value_grad,
    )


def merge_heads(array):
    return jnp.transpose(array, (1, 0, 2)).reshape(array.shape[1], array.shape[0] * array.shape[2])


def local(queries, key_states, value_states, pool_weight, out_grad):
    tok_rows, local_width = queries.shape
    head_local = local_width // HEAD_DIM
    seg_rows = pool_weight.shape[0]
    group_index = lax.axis_index("seq")
    group_total = lax.axis_size("seq")
    key_segments = key_states.reshape(SUM_DEV, seg_rows, local_width).astype(jnp.float32)
    value_segments = value_states.reshape(SUM_DEV, seg_rows, local_width).astype(jnp.float32)
    pooled_key = jnp.einsum("spc,p->sc", key_segments, pool_weight, precision=lax.Precision.HIGHEST)
    pooled_value = jnp.einsum(
        "spc,p->sc", value_segments, pool_weight, precision=lax.Precision.HIGHEST
    )
    summary = jnp.concatenate([pooled_key, pooled_value], axis=1).astype(jnp.bfloat16)
    global_rows = lax.all_gather(summary, "seq", axis=0, tiled=True)
    joined = jnp.concatenate([key_states, value_states], axis=1)
    joined_ext = extended(joined, (("seq", 0),), BLOCK)
    mask_first = group_index == 0
    mask_last = group_index == group_total - 1

    def one_head(head_index):
        start = head_index * HEAD_DIM
        query_head = lax.dynamic_slice_in_dim(queries, start, HEAD_DIM, 1)
        key_ext = lax.dynamic_slice_in_dim(joined_ext, start, HEAD_DIM, 1)
        value_ext = lax.dynamic_slice_in_dim(joined_ext, local_width + start, HEAD_DIM, 1)
        global_key = lax.dynamic_slice_in_dim(global_rows, start, HEAD_DIM, 1)
        global_value = lax.dynamic_slice_in_dim(global_rows, local_width + start, HEAD_DIM, 1)
        grad_head = lax.dynamic_slice_in_dim(out_grad, start, HEAD_DIM, 1)
        return head_pass(
            query_head,
            key_ext,
            value_ext,
            global_key,
            global_value,
            grad_head,
            mask_first,
            mask_last,
        )

    results = lax.map(one_head, jnp.arange(head_local))
    attended = merge_heads(results[0])
    query_grad = merge_heads(results[1])
    joined_grad = jnp.concatenate([merge_heads(results[2]), merge_heads(results[3])], axis=1)
    global_part = jnp.concatenate([merge_heads(results[4]), merge_heads(results[5])], axis=1)
    edges = jnp.concatenate([joined_grad[:BLOCK], joined_grad[tok_rows + BLOCK :]], axis=0)
    returned = extended(edges.astype(jnp.bfloat16), (("seq", 0),), BLOCK).astype(edges.dtype)
    local_grad = joined_grad[BLOCK : tok_rows + BLOCK]
    local_grad = local_grad + jnp.pad(returned[:BLOCK], ((0, tok_rows - BLOCK), (0, 0)))
    local_grad = local_grad + jnp.pad(returned[3 * BLOCK :], ((tok_rows - BLOCK, 0), (0, 0)))
    summed = lax.psum(global_part, "seq")
    owned = lax.dynamic_slice_in_dim(summed, group_index * SUM_DEV, SUM_DEV, 0)
    owned_key = owned[:, :local_width]
    owned_value = owned[:, local_width:]
    key_pooled = (owned_key[:, None, :] * pool_weight[None, :, None]).reshape(tok_rows, local_width)
    value_pooled = (owned_value[:, None, :] * pool_weight[None, :, None]).reshape(
        tok_rows, local_width
    )
    key_grad = (local_grad[:, :local_width] + key_pooled).astype(jnp.bfloat16)
    value_grad = (local_grad[:, local_width:] + value_pooled).astype(jnp.bfloat16)
    pool_term = jnp.einsum(
        "sc,spc->p", owned_key, key_segments, precision=lax.Precision.HIGHEST
    ) + jnp.einsum("sc,spc->p", owned_value, value_segments, precision=lax.Precision.HIGHEST)
    pool_grad = lax.psum(pool_term, ("seq", "head"))
    return (attended, query_grad, key_grad, value_grad, pool_grad)


def solution(mesh):
    return jax.shard_map(
        local,
        mesh=mesh,
        in_specs=(P("seq", "head"), P("seq", "head"), P("seq", "head"), P(), P("seq", "head")),
        out_specs=(P("seq", "head"), P("seq", "head"), P("seq", "head"), P("seq", "head"), P()),
        check_vma=False,
    )
```

profile of v0, /device:TPU:0, one launch (start us, length us, event | category | flops | bytes accessed | tf_op | source)
XLA Modules:
  0.0 246.1 jit_solution(4200020440458818728)
XLA Ops:
  7.2 0.9 constant_dynamic-update-slice_fusion.1
  8.3 4.8 %collective-permute-start = (bf16[64,384]{0,1:T(8,128)(2,1)S(1)}, bf16[64,384]{0,1:T(8,128)(2,1)S(1)}, u32[]{:S(2)}, u32[]{:S(2)}) collective-permute-start(bf16[64,384]{0,1:T(8,128)(2,1)S(1)} %get-tuple-element.305), channel_id=1, source_target_pairs={{0,2},{2,4},{4,6},{6,8},{8,10},{10,12},{12,14},{14,16},{16,18},{18... | collective-permute-start | bytes 147464 | tf_op jit(solution)/shard_map/ppermute | solution.py:18
  13.1 1.3 collective-permute-start.1
  14.6 0.6 copy-done.2
  15.8 42.3 %all-gather = bf16[16,4,384]{2,1,0:T(4,128)(2,1)S(1)} all-gather(bf16[1,4,384]{2,1,0:T(4,128)(2,1)S(1)} %maximum_bitcast_fusion), channel_id=1, replica_groups=mesh['seq'=16,'head'=2] {'seq'}, dimensions={0}, use_global_device_ids=true | all-gather | bytes 52224 | tf_op jit(solution)/shard_map/all_gather | solution.py:139
  58.4 28.7 %while.22 = (s32[]{:T(128)}, bf16[3,256,64]{1,2,0:T(8,128)(2,1)S(1)}, bf16[3,256,64]{1,2,0:T(8,128)(2,1)S(1)}, f32[3,384,64]{1,2,0:T(8,128)S(1)}, f32[3,384,64]{...) while((s32[]{:T(128)}, ...), condition=%wide.region_6.7_spmd, body=%wide.region_0.6_spmd.sunk | while | flops 52694932 | bytes 8105640 | solution.py:164
  58.4 0.6 dynamic_slice.71
  59.8 0.8 constant_dynamic-slice_fusion.8
  61.8 0.3 fusion.130
  63.4 0.8 multiply_reduce_fusion.2
  64.8 0.3 fusion.137
  68.0 0.6 dynamic_slice.71
  69.4 0.8 constant_dynamic-slice_fusion.8
  71.4 0.3 fusion.130
  73.0 0.8 multiply_reduce_fusion.2
  74.3 0.3 fusion.137
  77.5 0.6 dynamic_slice.71
  78.9 0.8 constant_dynamic-slice_fusion.8
  81.0 0.3 fusion.130
  82.6 0.8 multiply_reduce_fusion.2
  83.9 0.3 fusion.137
  87.2 0.5 copy-done.4
  88.0 1.3 collective-permute-start.2
  89.3 1.3 collective-permute-start.3
  90.6 0.7 pad_maximum_fusion.8
  91.6 4.3 %collective-permute-done.3 = bf16[64,384]{0,1:T(8,128)(2,1)S(1)} collective-permute-done((bf16[64,384]{0,1:T(8,128)(2,1)S(1)}, bf16[64,384]{0,1:T(8,128)(2,1)S(1)}, u32[]{:S(2)}, u32[]{:S(2)}) %collective-permute-start.3) | collective-permute-done | bytes 49184 | tf_op jit(solution)/shard_map/ppermute | solution.py:19
  96.1 0.5 copy-done.3
  96.6 0.3 fusion.42
  97.0 100.1 %all-reduce.9.cloned.1.call-done = f32[64,384]{0,1:T(8,128)} async-done(((f32[64,384]{0,1:T(8,128)}), f32[64,384]{0,1:T(8,128)}) %all-reduce.9.cloned.1.call-update) | async-done | bytes 98320 | tf_op jit(solution)/shard_map/psum | solution.py:174
  197.1 1.0 fusion.54
  198.9 39.4 %psum.15 = f32[64]{0:T(128)} all-reduce(f32[64]{0:T(128)S(1)} %fusion.38), channel_id=1, replica_groups=mesh['seq'=16,'head'=2] {'seq','head'}, use_global_device_ids=true, to_apply=%region_8.9 | all-reduce | flops 64 | bytes 512 | tf_op jit(solution)/shard_map/psum | solution.py:187
  238.6 0.7 fusion.43
  (229 shorter events, 20.5 us)
Async XLA Ops:
  7.2 1.0 copy-start.1
  7.2 189.9 %all-reduce.9.cloned.1.call-start = ((), (), s32[]{:S(2)}) async-start(), calls=%async_computation | async-start | bytes 393216 | tf_op jit(solution)/shard_map/psum | solution.py:174
  8.1 6.3 %copy-start = (bf16[256,192]{0,1:T(8,128)(2,1)S(1)}, bf16[256,192]{0,1:T(8,128)(2,1)}, u32[]{:S(2)}) copy-start(bf16[256,192]{0,1:T(8,128)(2,1)} %param.8) | copy-start | bytes 294916
  8.3 49.9 %collective-permute-start = (bf16[64,384]{0,1:T(8,128)(2,1)S(1)}, bf16[64,384]{0,1:T(8,128)(2,1)S(1)}, u32[]{:S(2)}, u32[]{:S(2)}) collective-permute-start(bf16[64,384]{0,1:T(8,128)(2,1)S(1)} %get-tuple-element.305), channel_id=1, source_target_pairs={{0,2},{2,4},{4,6},{6,8},{8,10},{10,12},{12,14},{14,16},{16,18},{18... | collective-permute-start | bytes 147464 | tf_op jit(solution)/shard_map/ppermute | solution.py:18
  13.1 45.1 %collective-permute-start.1 = (bf16[64,384]{0,1:T(8,128)(2,1)S(1)}, bf16[64,384]{0,1:T(8,128)(2,1)S(1)}, u32[]{:S(2)}, u32[]{:S(2)}) collective-permute-start(bf16[64,384]{0,1:T(8,128)(2,1)S(1)} %get-tuple-element.306), channel_id=1, source_target_pairs={{2,0},{4,2},{6,4},{8,6},{10,8},{12,10},{14,12},{16,14},{18,16},{20... | collective-permute-start | bytes 147464 | tf_op jit(solution)/shard_map/ppermute | solution.py:19
  14.6 0.7 copy-start.2
  87.1 0.6 copy-start.4
  87.1 0.7 copy-start.5
  88.0 3.5 %collective-permute-start.2 = (bf16[64,384]{0,1:T(8,128)(2,1)S(1)}, bf16[64,384]{0,1:T(8,128)(2,1)S(1)}, u32[]{:S(2)}, u32[]{:S(2)}) collective-permute-start(bf16[64,384]{0,1:T(8,128)(2,1)S(1)} %get-tuple-element.301), channel_id=1, source_target_pairs={{0,2},{2,4},{4,6},{6,8},{8,10},{10,12},{12,14},{14,16},{16,18},{18... | collective-permute-start | bytes 147464 | tf_op jit(solution)/shard_map/ppermute | solution.py:18
  89.3 6.5 %collective-permute-start.3 = (bf16[64,384]{0,1:T(8,128)(2,1)S(1)}, bf16[64,384]{0,1:T(8,128)(2,1)S(1)}, u32[]{:S(2)}, u32[]{:S(2)}) collective-permute-start(bf16[64,384]{0,1:T(8,128)(2,1)S(1)} %get-tuple-element.302), channel_id=1, source_target_pairs={{2,0},{4,2},{6,4},{8,6},{10,8},{12,10},{14,12},{16,14},{18,16},{20... | collective-permute-start | bytes 147464 | tf_op jit(solution)/shard_map/ppermute | solution.py:19
  96.0 0.7 copy-start.3
Sparse Core Ops, SparseCore 0:
  91.5 105.5 all-reduce.8
where the time goes:
time: 247 us; the launch traced here: 246 us
  waiting for transfers between devices  105 us (43%)
  blocking collectives  81.7 us (33%)
  local copies, waits for them, and re-layouts  18.5 us (7%)
  between operations  14.3 us (6%)
  matrix products  8.91 us (4%)
  starting transfers between devices  8.76 us (4%)
  other arithmetic  6.43 us (3%)
  loops' own time  2.84 us (1%)
    psum x1, waiting for transfers between devices, local(): summed = lax.psum(global_part, 'seq')  100 us
    all_gather x1, blocking collectives, local(): global_rows = lax.all_gather(summary, 'seq', axis=0, tiled=True)  42.3 us
    psum x1, blocking collectives, local(): pool_grad = lax.psum(pool_term, ('seq', 'head'))  39.4 us
    ppermute x2, starting transfers between devices, extended(): before = lax.ppermute(last, axis, up)  6.14 us
  transfers between devices with their start and end apart: 5, of which 3 were waited for; matrix products, arithmetic and copies ran while one was open for 1% of the time, Pallas kernels for 0%

commit v1 on v0

--- a/solution.py
+++ b/solution.py
@@ -6,6 +6,14 @@
 HEAD_DIM = 64
 BLOCK = 64
 SUM_DEV = 4
+
+
+def exchanged(x, axes):
+    return lax.all_to_all(x, axes, split_axis=0, concat_axis=0)
+
+
+def to_all(x, axes):
+    return exchanged(jnp.broadcast_to(x[None], (lax.axis_size(axes),) + x.shape), axes)
 
 
 def extended(x, sides, width):
@@ -136,7 +144,7 @@
         "spc,p->sc", value_segments, pool_weight, precision=lax.Precision.HIGHEST
     )
     summary = jnp.concatenate([pooled_key, pooled_value], axis=1).astype(jnp.bfloat16)
-    global_rows = lax.all_gather(summary, "seq", axis=0, tiled=True)
+    global_rows = to_all(summary, "seq").reshape(group_total * SUM_DEV, 2 * local_width)
     joined = jnp.concatenate([key_states, value_states], axis=1)
     joined_ext = extended(joined, (("seq", 0),), BLOCK)
     mask_first = group_index == 0
@@ -171,8 +179,7 @@
     local_grad = joined_grad[BLOCK : tok_rows + BLOCK]
     local_grad = local_grad + jnp.pad(returned[:BLOCK], ((0, tok_rows - BLOCK), (0, 0)))
     local_grad = local_grad + jnp.pad(returned[3 * BLOCK :], ((tok_rows - BLOCK, 0), (0, 0)))
-    summed = lax.psum(global_part, "seq")
-    owned = lax.dynamic_slice_in_dim(summed, group_index * SUM_DEV, SUM_DEV, 0)
+    owned = exchanged(global_part.reshape(group_total, SUM_DEV, 2 * local_width), "seq").sum(0)
     owned_key = owned[:, :local_width]
     owned_value = owned[:, local_width:]
     key_pooled = (owned_key[:, None, :] * pool_weight[None, :, None]).reshape(tok_rows, local_width)
@@ -184,7 +191,7 @@
     pool_term = jnp.einsum(
         "sc,spc->p", owned_key, key_segments, precision=lax.Precision.HIGHEST
     ) + jnp.einsum("sc,spc->p", owned_value, value_segments, precision=lax.Precision.HIGHEST)
-    pool_grad = lax.psum(pool_term, ("seq", "head"))
+    pool_grad = to_all(pool_term, ("seq", "head")).sum(0)
     return (attended, query_grad, key_grad, value_grad, pool_grad)
 
 

time: 247 us -> 85.7 us (0.35)
  waiting for transfers between devices: 105 us -> 19.8 us
  blocking collectives: 81.7 us -> 0 us
  starting transfers between devices: 8.76 us -> 26.6 us
  between operations: 14.3 us -> 0.99 us
    psum x1 -> x0, waiting for transfers between devices: 100 us -> none  [local(): summed = lax.psum(global_part, 'seq')]
    all_gather x1 -> x0, blocking collectives: 42.3 us -> none  [local(): global_rows = lax.all_gather(summary, 'seq', axis=0, tiled=True)]
    psum x1 -> x0, blocking collectives: 39.4 us -> none  [local(): pool_grad = lax.psum(pool_term, ('seq', 'head'))]
    all_to_all x0 -> x3, waiting for transfers between devices: none -> 19.7 us  [exchanged(): return lax.all_to_all(x, axes, split_axis=0, concat_axis=0)]
    all_to_all x0 -> x3, starting transfers between devices: none -> 16.4 us  [exchanged(): return lax.all_to_all(x, axes, split_axis=0, concat_axis=0)]
    ppermute x2, waiting for transfers between devices: 4.28 us -> 0.01 us  [extended(): after = lax.ppermute(leading, axis, down)]
  transfers between devices with their start and end apart: 5 -> 7, of which waited for: 3 -> 3; matrix products, arithmetic and copies ran while one was open for 1% -> 5% of each run, Pallas kernels for 0% -> 0%
where the time goes in v1:
time: 85.7 us; the launch traced here: 84.8 us
  starting transfers between devices  26.6 us (31%)
  waiting for transfers between devices  19.8 us (23%)
  local copies, waits for them, and re-layouts  18.7 us (22%)
  matrix products  8.92 us (10%)
  other arithmetic  7.05 us (8%)
  loops' own time  2.86 us (3%)
  between operations  0.99 us (1%)
    all_to_all x3, waiting for transfers between devices, exchanged(): return lax.all_to_all(x, axes, split_axis=0, concat_axis=0)  19.7 us
    all_to_all x3, starting transfers between devices, exchanged(): return lax.all_to_all(x, axes, split_axis=0, concat_axis=0)  16.4 us
    ppermute x2, starting transfers between devices, extended(): before = lax.ppermute(last, axis, up)  7.52 us
    unnamed x15, local copies, waits for them, and re-layouts  2.91 us
    another operation x1, loops' own time, local(): results = lax.map(one_head, jnp.arange(head_local))  2.86 us
    dynamic_slice x6, local copies, waits for them, and re-layouts, one_head(): query_head = lax.dynamic_slice_in_dim(queries, start, HEAD_DIM, 1)  2.63 us
    ppermute x2, starting transfers between devices, extended(): after = lax.ppermute(leading, axis, down)  2.58 us
    reduce_sum x3, other arithmetic, head_pass(): jnp.sum(grad_head.astype(jnp.float32) * attended.astype(jnp.float32), axi...  2.37 us
  transfers between devices with their start and end apart: 7, of which 3 were waited for; matrix products, arithmetic and copies ran while one was open for 5% of the time, Pallas kernels for 0%

profile of v1, /device:TPU:0, one launch (start us, length us, event | category | flops | bytes accessed | tf_op | source)
XLA Modules:
  0.0 84.8 jit_solution(1465327727522179710)
XLA Ops:
  0.6 0.9 %constant_dynamic-update-slice_fusion.1 = bf16[256,384]{0,1:T(8,128)(2,1)S(1)} fusion(bf16[256,192]{0,1:T(8,128)(2,1)} %param.8), kind=kLoop, calls=%fused_computation.79 | loop fusion | bytes 196608
  1.7 4.8 %collective-permute-start = (bf16[64,384]{0,1:T(8,128)(2,1)S(1)}, bf16[64,384]{0,1:T(8,128)(2,1)S(1)}, u32[]{:S(2)}, u32[]{:S(2)}) collective-permute-start(bf16[64,384]{0,1:T(8,128)(2,1)S(1)} %get-tuple-element.317), channel_id=1, source_target_pairs={{0,2},{2,4},{4,6},{6,8},{8,10},{10,12},{12,14},{14,16},{16,18},{18... | collective-permute-start | bytes 147464 | tf_op jit(solution)/shard_map/ppermute | solution.py:26
  6.6 1.3 %collective-permute-start.1 = (bf16[64,384]{0,1:T(8,128)(2,1)S(1)}, bf16[64,384]{0,1:T(8,128)(2,1)S(1)}, u32[]{:S(2)}, u32[]{:S(2)}) collective-permute-start(bf16[64,384]{0,1:T(8,128)(2,1)S(1)} %get-tuple-element.318), channel_id=1, source_target_pairs={{2,0},{4,2},{6,4},{8,6},{10,8},{12,10},{14,12},{16,14},{18,16},{20... | collective-permute-start | bytes 147464 | tf_op jit(solution)/shard_map/ppermute | solution.py:27
  8.1 0.6 copy-done.2
  9.2 0.6 broadcast_in_dim.79
  9.8 8.0 %all-to-all-start = ((bf16[16,4,384]{2,1,0:T(4,128)(2,1)}), bf16[16,4,384]{2,1,0:T(4,128)(2,1)S(1)}, u32[]{:S(2)}, u32[]{:S(2)}) async-start(bf16[16,4,384]{2,1,0:T(4,128)(2,1)} %broadcast_in_dim.79), calls=%async_computation | async-start | bytes 98304 | tf_op jit(solution)/shard_map/all_to_all | solution.py:12
  18.2 7.1 %all-to-all-done = bf16[16,4,384]{2,1,0:T(4,128)(2,1)S(1)} async-done(((bf16[16,4,384]{2,1,0:T(4,128)(2,1)}), bf16[16,4,384]{2,1,0:T(4,128)(2,1)S(1)}, u32[]{:S(2)}, u32[]{:S(2)}) %all-to-all-start) | async-done | bytes 49184 | tf_op jit(solution)/shard_map/all_to_all | solution.py:12
  25.3 28.7 %while.22 = (s32[]{:T(128)}, bf16[3,256,64]{1,2,0:T(8,128)(2,1)S(1)}, bf16[3,256,64]{1,2,0:T(8,128)(2,1)S(1)}, f32[3,384,64]{1,2,0:T(8,128)S(1)}, f32[3,384,64]{...) while((s32[]{:T(128)}, ...), condition=%wide.region_6.7_spmd, body=%wide.region_0.6_spmd.sunk | while | flops 52694932 | bytes 8105640 | solution.py:172
  25.3 0.6 dynamic_slice.67
  26.7 0.8 constant_dynamic-slice_fusion.7
  28.8 0.3 fusion.129
  30.4 0.8 multiply_reduce_fusion.2
  34.9 0.6 dynamic_slice.67
  36.3 0.8 constant_dynamic-slice_fusion.7
  38.3 0.3 fusion.129
  39.9 0.8 multiply_reduce_fusion.2
  44.5 0.6 dynamic_slice.67
  45.9 0.8 constant_dynamic-slice_fusion.7
  47.9 0.3 fusion.129
  49.5 0.8 multiply_reduce_fusion.2
  54.1 0.5 copy-done.4
  55.2 2.7 %collective-permute-start.2 = (bf16[64,384]{0,1:T(8,128)(2,1)S(1)}, bf16[64,384]{0,1:T(8,128)(2,1)S(1)}, u32[]{:S(2)}, u32[]{:S(2)}) collective-permute-start(bf16[64,384]{0,1:T(8,128)(2,1)S(1)} %get-tuple-element.315), channel_id=1, source_target_pairs={{0,2},{2,4},{4,6},{6,8},{8,10},{10,12},{12,14},{14,16},{16,18},{18... | collective-permute-start | bytes 147464 | tf_op jit(solution)/shard_map/ppermute | solution.py:26
  57.8 1.3 %collective-permute-start.3 = (bf16[64,384]{0,1:T(8,128)(2,1)S(1)}, bf16[64,384]{0,1:T(8,128)(2,1)S(1)}, u32[]{:S(2)}, u32[]{:S(2)}) collective-permute-start(bf16[64,384]{0,1:T(8,128)(2,1)S(1)} %get-tuple-element.316), channel_id=1, source_target_pairs={{2,0},{4,2},{6,4},{8,6},{10,8},{12,10},{14,12},{16,14},{18,16},{20... | collective-permute-start | bytes 147464 | tf_op jit(solution)/shard_map/ppermute | solution.py:27
  59.1 0.7 pad_maximum_fusion.8
  59.9 5.9 %all-to-all-start.1 = ((f32[16,4,384]{2,1,0:T(4,128)}), f32[16,4,384]{2,1,0:T(4,128)S(1)}, u32[]{:S(2)}, u32[]{:S(2)}) async-start(f32[16,4,384]{2,1,0:T(4,128)} %pad_maximum_fusion.8), calls=%async_computation.1 | async-start | bytes 196608 | tf_op jit(solution)/shard_map/all_to_all | solution.py:12
  66.1 0.5 copy-done.3
  66.9 6.5 %all-to-all-done.1 = f32[16,4,384]{2,1,0:T(4,128)S(1)} async-done(((f32[16,4,384]{2,1,0:T(4,128)}), f32[16,4,384]{2,1,0:T(4,128)S(1)}, u32[]{:S(2)}, u32[]{:S(2)}) %all-to-all-start.1) | async-done | bytes 98336 | tf_op jit(solution)/shard_map/all_to_all | solution.py:12
  73.9 0.7 broadcast_in_dim.80
  74.6 2.6 %all-to-all-start.2 = ((f32[32,1,64]{2,1,0:T(1,128)}), f32[32,1,64]{2,1,0:T(1,128)S(1)}, u32[]{:S(2)}, u32[]{:S(2)}) async-start(f32[32,1,64]{2,1,0:T(1,128)} %broadcast_in_dim.80), calls=%async_computation.2 | async-start | bytes 32768 | tf_op jit(solution)/shard_map/all_to_all | solution.py:12
  77.5 0.7 fusion.43
  78.2 6.1 %all-to-all-done.2 = f32[32,1,64]{2,1,0:T(1,128)S(1)} async-done(((f32[32,1,64]{2,1,0:T(1,128)}), f32[32,1,64]{2,1,0:T(1,128)S(1)}, u32[]{:S(2)}, u32[]{:S(2)}) %all-to-all-start.2) | async-done | bytes 8224 | tf_op jit(solution)/shard_map/all_to_all | solution.py:12
  84.3 0.5 reduce_sum.57
  (232 shorter events, 21.3 us)
Async XLA Ops:
  0.6 0.9 %copy-start.1 = (bf16[256,192]{0,1:T(8,128)(2,1)S(1)}, bf16[256,192]{0,1:T(8,128)(2,1)}, u32[]{:S(2)}) copy-start(bf16[256,192]{0,1:T(8,128)(2,1)} %param.9) | copy-start | bytes 294916
  1.6 6.3 %copy-start = (bf16[256,192]{0,1:T(8,128)(2,1)S(1)}, bf16[256,192]{0,1:T(8,128)(2,1)}, u32[]{:S(2)}) copy-start(bf16[256,192]{0,1:T(8,128)(2,1)} %param.8) | copy-start | bytes 294916
  1.7 16.3 %collective-permute-start = (bf16[64,384]{0,1:T(8,128)(2,1)S(1)}, bf16[64,384]{0,1:T(8,128)(2,1)S(1)}, u32[]{:S(2)}, u32[]{:S(2)}) collective-permute-start(bf16[64,384]{0,1:T(8,128)(2,1)S(1)} %get-tuple-element.317), channel_id=1, source_target_pairs={{0,2},{2,4},{4,6},{6,8},{8,10},{10,12},{12,14},{14,16},{16,18},{18... | collective-permute-start | bytes 147464 | tf_op jit(solution)/shard_map/ppermute | solution.py:26
  6.6 11.4 %collective-permute-start.1 = (bf16[64,384]{0,1:T(8,128)(2,1)S(1)}, bf16[64,384]{0,1:T(8,128)(2,1)S(1)}, u32[]{:S(2)}, u32[]{:S(2)}) collective-permute-start(bf16[64,384]{0,1:T(8,128)(2,1)S(1)} %get-tuple-element.318), channel_id=1, source_target_pairs={{2,0},{4,2},{6,4},{8,6},{10,8},{12,10},{14,12},{16,14},{18,16},{20... | collective-permute-start | bytes 147464 | tf_op jit(solution)/shard_map/ppermute | solution.py:27
  8.1 0.7 copy-start.2
  9.8 15.5 %all-to-all-start = ((bf16[16,4,384]{2,1,0:T(4,128)(2,1)}), bf16[16,4,384]{2,1,0:T(4,128)(2,1)S(1)}, u32[]{:S(2)}, u32[]{:S(2)}) async-start(bf16[16,4,384]{2,1,0:T(4,128)(2,1)} %broadcast_in_dim.79), calls=%async_computation | async-start | bytes 98304 | tf_op jit(solution)/shard_map/all_to_all | solution.py:12
  54.0 0.6 copy-start.4
  54.0 0.7 copy-start.5
  55.2 10.6 %collective-permute-start.2 = (bf16[64,384]{0,1:T(8,128)(2,1)S(1)}, bf16[64,384]{0,1:T(8,128)(2,1)S(1)}, u32[]{:S(2)}, u32[]{:S(2)}) collective-permute-start(bf16[64,384]{0,1:T(8,128)(2,1)S(1)} %get-tuple-element.315), channel_id=1, source_target_pairs={{0,2},{2,4},{4,6},{6,8},{8,10},{10,12},{12,14},{14,16},{16,18},{18... | collective-permute-start | bytes 147464 | tf_op jit(solution)/shard_map/ppermute | solution.py:26
  57.8 7.9 %collective-permute-start.3 = (bf16[64,384]{0,1:T(8,128)(2,1)S(1)}, bf16[64,384]{0,1:T(8,128)(2,1)S(1)}, u32[]{:S(2)}, u32[]{:S(2)}) collective-permute-start(bf16[64,384]{0,1:T(8,128)(2,1)S(1)} %get-tuple-element.316), channel_id=1, source_target_pairs={{2,0},{4,2},{6,4},{8,6},{10,8},{12,10},{14,12},{16,14},{18,16},{20... | collective-permute-start | bytes 147464 | tf_op jit(solution)/shard_map/ppermute | solution.py:27
  59.9 13.6 %all-to-all-start.1 = ((f32[16,4,384]{2,1,0:T(4,128)}), f32[16,4,384]{2,1,0:T(4,128)S(1)}, u32[]{:S(2)}, u32[]{:S(2)}) async-start(f32[16,4,384]{2,1,0:T(4,128)} %pad_maximum_fusion.8), calls=%async_computation.1 | async-start | bytes 196608 | tf_op jit(solution)/shard_map/all_to_all | solution.py:12
  65.9 0.7 copy-start.3
  74.6 9.7 %all-to-all-start.2 = ((f32[32,1,64]{2,1,0:T(1,128)}), f32[32,1,64]{2,1,0:T(1,128)S(1)}, u32[]{:S(2)}, u32[]{:S(2)}) async-start(f32[32,1,64]{2,1,0:T(1,128)} %broadcast_in_dim.80), calls=%async_computation.2 | async-start | bytes 32768 | tf_op jit(solution)/shard_map/all_to_all | solution.py:12

commit v2 on v0

v2 whole, which is shorter than its diff:
```python
import functools

import jax
import jax.numpy as jnp
from jax import lax
from jax.experimental import pallas as pl
from jax.experimental.pallas import tpu as pltpu
from jax.sharding import PartitionSpec as P

HEAD_DIM = 64
BLOCK = 64
SUM_DEV = 4
PAIR = 2 * BLOCK
SCALE = HEAD_DIM ** (-0.5)
LOW = -1e30
VMEM = pl.BlockSpec(memory_space=pltpu.VMEM)
SMEM = pl.BlockSpec(memory_space=pltpu.SMEM)
PARAMS = pltpu.CompilerParams(vmem_limit_bytes=40 * 1024 * 1024)
F32 = jnp.float32
BF16 = jnp.bfloat16


def mm(a, b):
    return lax.dot_general(a, b, (((1,), (0,)), ((), ())), preferred_element_type=F32)


def mm_nt(a, b):
    return lax.dot_general(a, b, (((1,), (1,)), ((), ())), preferred_element_type=F32)


def mm_tn(a, b):
    return lax.dot_general(a, b, (((0,), (0,)), ((), ())), preferred_element_type=F32)


def pieces(x):
    high = x.astype(BF16)
    rest = x - high.astype(F32)
    middle = rest.astype(BF16)
    low = (rest - middle.astype(F32)).astype(BF16)
    return jnp.concatenate([high, middle, low], axis=0)


def segment_mask(first, rows, lanes, seg):
    row = lax.broadcasted_iota(jnp.int32, (rows, lanes), 0)
    lane = lax.broadcasted_iota(jnp.int32, (rows, lanes), 1)
    return row - first == lane // seg


def pool_kernel(q_ref, k_ref, v_ref, g_ref, w_ref, rows_ref, up_ref, down_ref):
    seg = w_ref.shape[1]
    w = jnp.concatenate([w_ref[...]] * SUM_DEV, axis=1)
    w = jnp.broadcast_to(w, (2 * SUM_DEV, w.shape[1]))
    pooled = jnp.zeros((2 * SUM_DEV, k_ref.shape[1]), F32)
    for first, ref in ((0, k_ref), (SUM_DEV, v_ref)):
        weights = jnp.where(segment_mask(first, w.shape[0], w.shape[1], seg), w, 0.0)
        parts = mm(pieces(weights), ref[...])
        n = 2 * SUM_DEV
        pooled += parts[:n] + parts[n : 2 * n] + parts[2 * n :]
    rows_ref[...] = jnp.broadcast_to(pooled.astype(BF16)[None], rows_ref.shape)
    tok = k_ref.shape[0]
    at = 0
    for ref, width in ((k_ref, PAIR), (v_ref, PAIR), (q_ref, BLOCK), (g_ref, BLOCK)):
        up_ref[at : at + width] = ref[tok - width :]
        down_ref[at : at + width] = ref[:width]
        at += width


def head_rows(x):
    feature = lax.broadcasted_iota(jnp.int32, (1, x.shape[1]), 1) // HEAD_DIM
    return jnp.concatenate(
        [x * jnp.where(feature == h, SCALE, 0.0).astype(BF16) for h in range(x.shape[1] // HEAD_DIM)],
        axis=0,
    )


def own_head(x):
    return jnp.concatenate(
        [
            x[h * HEAD_DIM : (h + 1) * HEAD_DIM, h * PAIR : (h + 1) * PAIR]
            for h in range(x.shape[0] // HEAD_DIM)
        ],
        axis=0,
    )


def head_sums(x):
    return jnp.concatenate(
        [
            jnp.sum(x[h * HEAD_DIM : (h + 1) * HEAD_DIM], axis=0, keepdims=True)
            for h in range(x.shape[0] // HEAD_DIM)
        ],
        axis=1,
    )


def softmax(local, glob):
    top = jnp.maximum(
        jnp.max(local, axis=0, keepdims=True), jnp.max(glob, axis=0, keepdims=True)
    )
    local = jnp.exp(local - top)
    glob = jnp.exp(glob - top)
    total = jnp.sum(local, axis=0, keepdims=True) + jnp.sum(glob, axis=0, keepdims=True)
    inverse = 1.0 / total
    return local * inverse, glob * inverse


def attention_kernel(
    edge_ref, q_ref, k_ref, v_ref, g_ref, before_ref, after_ref, rows_ref,
    att_ref, qg_ref, kg_ref, vg_ref, part_ref, kx, vx,
):
    tok, width = q_ref.shape
    heads = width // HEAD_DIM
    lanes = heads * PAIR
    is_first, is_last = edge_ref[0] == 1, edge_ref[1] == 1
    kx[:PAIR] = before_ref[:PAIR]
    vx[:PAIR] = before_ref[PAIR : 2 * PAIR]
    kx[PAIR : PAIR + tok] = k_ref[...]
    vx[PAIR : PAIR + tok] = v_ref[...]
    kx[PAIR + tok :] = after_ref[:PAIR]
    vx[PAIR + tok :] = after_ref[PAIR : 2 * PAIR]
    global_rows = rows_ref[...]
    count = global_rows.shape[0]
    second = lax.broadcasted_iota(jnp.int32, (1, lanes), 1) % PAIR >= BLOCK
    is_key = lax.broadcasted_iota(jnp.int32, (count, lanes), 0) % (2 * SUM_DEV) < SUM_DEV
    global_values = pltpu.roll(global_rows.astype(F32), count - SUM_DEV, 0).astype(BF16)

    kg = jnp.zeros((tok + PAIR, width), F32)
    vg = jnp.zeros((tok + PAIR, width), F32)
    part = jnp.zeros((count, width), F32)
    kg_rows = [jnp.zeros((BLOCK, width), F32) for _ in range(tok // BLOCK + 2)]
    vg_rows = [jnp.zeros((BLOCK, width), F32) for _ in range(tok // BLOCK + 2)]
    pairs = tok // PAIR
    for p in range(pairs):
        q = q_ref[p * PAIR : (p + 1) * PAIR]
        g = g_ref[p * PAIR : (p + 1) * PAIR]
        qm, gm = head_rows(q), head_rows(g)
        start = BLOCK + p * PAIR
        keys, values = kx[start : start + 2 * PAIR], vx[start : start + 2 * PAIR]
        s = mm_nt(keys, qm)
        hide_low = second
        hide_high = jnp.logical_not(second)
        if p == 0:
            hide_low = jnp.logical_or(hide_low, is_first)
        if p == pairs - 1:
            hide_high = jnp.logical_or(hide_high, is_last)
        s = jnp.concatenate(
            [
                s[:BLOCK] + jnp.where(hide_low, LOW, 0.0),
                s[BLOCK : 3 * BLOCK],
                s[3 * BLOCK :] + jnp.where(hide_high, LOW, 0.0),
            ],
            axis=0,
        )
        sg = jnp.where(is_key, mm_nt(global_rows, qm), LOW)
        w, wg = softmax(s, sg)
        pr, prg = w.astype(BF16), wg.astype(BF16)
        att = own_head(mm_tn(values, pr) + mm_tn(global_values, prg)).astype(BF16).astype(F32)
        att_ref[p * PAIR : (p + 1) * PAIR] = att.T.astype(BF16)
        delta = head_sums(g.astype(F32).T * att) * SCALE
        ds = (w * (mm_nt(values, gm) - delta)).astype(BF16)
        dsg = (wg * (mm_nt(global_values, gm) - delta)).astype(BF16)
        qg = own_head(mm_tn(keys, ds) + mm_tn(global_rows, dsg))
        qg_ref[p * PAIR : (p + 1) * PAIR] = qg.T.astype(BF16)
        kgp = mm(ds, qm)
        vgp = mm(pr, gm)
        for b in range(4):
            kg_rows[2 * p + b] += kgp[b * BLOCK : (b + 1) * BLOCK]
            vg_rows[2 * p + b] += vgp[b * BLOCK : (b + 1) * BLOCK]
        shifted = pltpu.roll(wg, SUM_DEV, 0).astype(BF16)
        part += mm(dsg, qm) + mm(shifted, gm)
    part_ref[...] = part * (1.0 / SCALE)

    q = jnp.concatenate([before_ref[2 * PAIR : 2 * PAIR + BLOCK], after_ref[2 * PAIR : 2 * PAIR + BLOCK]], axis=0)
    g = jnp.concatenate([before_ref[2 * PAIR + BLOCK :], after_ref[2 * PAIR + BLOCK :]], axis=0)
    qm, gm = head_rows(q), head_rows(g)
    low, high = slice(0, 3 * BLOCK), slice(tok + BLOCK, tok + 4 * BLOCK)
    s = jnp.where(second, mm_nt(kx[high], qm), mm_nt(kx[low], qm))
    sg = jnp.where(is_key, mm_nt(global_rows, qm), LOW)
    w, wg = softmax(s, sg)
    pr, prg = w.astype(BF16), wg.astype(BF16)
    att = jnp.where(second, mm_tn(vx[high], pr), mm_tn(vx[low], pr)) + mm_tn(global_values, prg)
    att = own_head(att).astype(BF16).astype(F32)
    delta = head_sums(g.astype(F32).T * att) * SCALE
    near_low, near_high = slice(PAIR, PAIR + BLOCK), slice(tok + BLOCK, tok + PAIR)
    dp = jnp.where(second, mm_nt(vx[near_high], gm), mm_nt(vx[near_low], gm))
    w = jnp.where(second, w[:BLOCK], w[2 * BLOCK :])
    ds = w * (dp - delta)
    ds = jnp.concatenate([jnp.where(second, 0.0, ds), jnp.where(second, ds, 0.0)], axis=0).astype(BF16)
    pr = jnp.concatenate([jnp.where(second, 0.0, w), jnp.where(second, w, 0.0)], axis=0).astype(BF16)
    kgp, vgp = mm(ds, qm), mm(pr, gm)
    kg_rows[1] += kgp[:BLOCK]
    vg_rows[1] += vgp[:BLOCK]
    kg_rows[-2] += kgp[BLOCK:]
    vg_rows[-2] += vgp[BLOCK:]
    kg_ref[...] = jnp.concatenate(kg_rows[1:-1], axis=0) * (1.0 / SCALE)
    vg_ref[...] = jnp.concatenate(vg_rows[1:-1], axis=0) * (1.0 / SCALE)


def owned_kernel(parts_ref, k_ref, v_ref, owned_ref, term_ref):
    owned = jnp.sum(parts_ref[...], axis=0)
    owned_ref[...] = owned
    split = pieces(owned)
    n = 2 * SUM_DEV
    seg = k_ref.shape[0] // SUM_DEV
    total = jnp.zeros((1, k_ref.shape[0]), F32)
    for first, ref in ((0, k_ref), (SUM_DEV, v_ref)):
        met = mm_nt(split, ref[...])
        met = met[:n] + met[n : 2 * n] + met[2 * n :]
        met = jnp.where(segment_mask(first, met.shape[0], met.shape[1], seg), met, 0.0)
        total += jnp.sum(met, axis=0, keepdims=True)
    term = total[:, :seg]
    for j in range(1, SUM_DEV):
        term += total[:, j * seg : (j + 1) * seg]
    term_ref[...] = jnp.broadcast_to(term, term_ref.shape)


def finish_kernel(owned_ref, kg_ref, vg_ref, w_ref, key_ref, value_ref):
    seg = w_ref.shape[1]
    same = lax.broadcasted_iota(jnp.int32, (seg, seg), 0) == lax.broadcasted_iota(
        jnp.int32, (seg, seg), 1
    )
    column = jnp.sum(jnp.where(same, w_ref[...], 0.0), axis=1, keepdims=True)
    for j in range(SUM_DEV):
        rows = slice(j * seg, (j + 1) * seg)
        key_ref[rows] = (kg_ref[rows] + column * owned_ref[j : j + 1]).astype(BF16)
        value_ref[rows] = (
            vg_ref[rows] + column * owned_ref[SUM_DEV + j : SUM_DEV + j + 1]
        ).astype(BF16)


def shaped(shape, dtype):
    return jax.ShapeDtypeStruct(shape, dtype)


def call(kernel, outs, count, scratch=(), first=VMEM):
    return pl.pallas_call(
        kernel,
        out_shape=outs,
        in_specs=[first] + [VMEM] * (count - 1),
        out_specs=[VMEM] * len(outs),
        scratch_shapes=list(scratch),
        compiler_params=PARAMS,
    )


def local(queries, key_states, value_states, pool_weight, out_grad):
    tok, width = queries.shape
    group_index = lax.axis_index("seq")
    groups = lax.axis_size("seq")
    everyone = groups * lax.axis_size("head")
    n = 2 * SUM_DEV
    seg = pool_weight.shape[0]
    weight_row = pool_weight.reshape(1, seg)
    halo = shaped((3 * PAIR, width), BF16)
    own = shaped((tok, width), BF16)
    grad = shaped((tok, width), F32)

    summary, up, down = call(pool_kernel, [shaped((groups, n, width), BF16), halo, halo], 5)(
        queries, key_states, value_states, out_grad, weight_row
    )
    forward = [(i, i + 1) for i in range(groups - 1)]
    backward = [(i + 1, i) for i in range(groups - 1)]
    before = lax.ppermute(up, "seq", forward)
    after = lax.ppermute(down, "seq", backward)
    rows = lax.all_to_all(summary, "seq", split_axis=0, concat_axis=0)

    edge = jnp.stack([group_index == 0, group_index == groups - 1]).astype(jnp.int32)
    ext = pltpu.VMEM((tok + 2 * PAIR, width), BF16)
    attended, query_grad, key_part, value_part, part = call(
        attention_kernel,
        [own, own, grad, grad, shaped((groups * n, width), F32)],
        8,
        [ext, ext],
        SMEM,
    )(edge, queries, key_states, value_states, out_grad, before, after, rows.reshape(groups * n, width))

    parts = lax.all_to_all(part.reshape(groups, n, width), "seq", split_axis=0, concat_axis=0)
    owned, term = call(owned_kernel, [shaped((n, width), F32), shaped((everyone, seg), F32)], 3)(
        parts, key_states, value_states
    )
    terms = lax.all_to_all(term, ("seq", "head"), split_axis=0, concat_axis=0)
    key_grad, value_grad = call(finish_kernel, [own, own], 4)(
        owned, key_part, value_part, weight_row
    )
    return (attended, query_grad, key_grad, value_grad, terms.sum(0))


def solution(mesh):
    return jax.shard_map(
        local,
        mesh=mesh,
        in_specs=(P("seq", "head"), P("seq", "head"), P("seq", "head"), P(), P("seq", "head")),
        out_specs=(P("seq", "head"), P("seq", "head"), P("seq", "head"), P("seq", "head"), P()),
        check_vma=False,
    )
```

time: 247 us -> 52.2 us (0.21)
  waiting for transfers between devices: 105 us -> 11.5 us
  blocking collectives: 81.7 us -> 10.4 us
  between operations: 14.3 us -> 0.75 us
  local copies, waits for them, and re-layouts: 18.5 us -> 6.52 us
  matrix products: 8.91 us -> 0 us
  starting transfers between devices: 8.76 us -> 16.7 us
  other arithmetic: 6.43 us -> 0.63 us
  Pallas kernels: 0 us -> 5.31 us
  loops' own time: 2.84 us -> 0 us
    psum x1 -> x0, waiting for transfers between devices: 100 us -> none  [local(): summed = lax.psum(global_part, 'seq')]
    all_gather x1 -> x0, blocking collectives: 42.3 us -> none  [local(): global_rows = lax.all_gather(summary, 'seq', axis=0, tiled=True)]
    psum x1 -> x0, blocking collectives: 39.4 us -> none  [local(): pool_grad = lax.psum(pool_term, ('seq', 'head'))]
    all_to_all x0 -> x2, waiting for transfers between devices: none -> 11.5 us  [the longest x1 7.45 us: local(): rows = lax.all_to_all(summary, 'seq', split_axis=0, concat_axis=0)]
    all_to_all x0 -> x2, starting transfers between devices: none -> 10.6 us  [the longest x1 8.03 us: local(): rows = lax.all_to_all(summary, 'seq', split_axis=0, concat_axis=0)]
    all_to_all x0 -> x1, blocking collectives: none -> 10.4 us  [local(): lax.all_to_all(part.reshape(groups, n, width), 'seq', split_axis=0, conca...]
    dot_general x40 -> x0, matrix products: 8.91 us -> none  [the longest x3 1 us: head_pass(): jnp.einsum('nbd,nkd->nbk', query_blocks, key_windows, preferred_element_t...]
    reshape x69 -> x0, local copies, waits for them, and re-layouts: 5.72 us -> none  [the longest x6 0.83 us: undo_windows(): window[:, 2 * BLOCK:].reshape(span, -1)]
  transfers between devices with their start and end apart: 5 -> 4, of which waited for: 3 -> 2; matrix products, arithmetic and copies ran while one was open for 1% -> 6% of each run, Pallas kernels for 0% -> 0%
where the time goes in v2:
time: 52.2 us; the launch traced here: 51.8 us
  starting transfers between devices  16.7 us (32%)
  waiting for transfers between devices  11.5 us (22%)
  blocking collectives  10.4 us (20%)
  local copies, waits for them, and re-layouts  6.52 us (12%)
  Pallas kernels  5.31 us (10%)
  between operations  0.75 us (1%)
  other arithmetic  0.63 us (1%)
    all_to_all x1, blocking collectives, local(): lax.all_to_all(part.reshape(groups, n, width), 'seq', split_axis=0, conca...  10.4 us
    all_to_all x1, starting transfers between devices, local(): rows = lax.all_to_all(summary, 'seq', split_axis=0, concat_axis=0)  8.03 us
    all_to_all x1, waiting for transfers between devices, local(): rows = lax.all_to_all(summary, 'seq', split_axis=0, concat_axis=0)  7.45 us
    unnamed x16, local copies, waits for them, and re-layouts  6.52 us
    ppermute x1, starting transfers between devices, local(): before = lax.ppermute(up, 'seq', forward)  4.84 us
    all_to_all x1, waiting for transfers between devices, local(): terms = lax.all_to_all(term, ('seq', 'head'), split_axis=0, concat_axis=0)  4.04 us
    pallas_call x1, Pallas kernels, local(): call(attention_kernel, [own, own, grad, grad, shaped((groups * n, width),...  3.48 us
    all_to_all x1, starting transfers between devices, local(): terms = lax.all_to_all(term, ('seq', 'head'), split_axis=0, concat_axis=0)  2.55 us
  transfers between devices with their start and end apart: 4, of which 2 were waited for; matrix products, arithmetic and copies ran while one was open for 6% of the time, Pallas kernels for 0%

profile of v2, /device:TPU:0, one launch (start us, length us, event | category | flops | bytes accessed | tf_op | source)
XLA Modules:
  0.0 51.8 jit_solution(13169573403470312457)
XLA Ops:
  0.6 0.0 copy-start.1
  0.6 1.0 %copy.29.k_ref = bf16[256,192]{1,0:T(8,128)(2,1)S(1)} copy(bf16[256,192]{0,1:T(8,128)(2,1)} %param.6) | data formatting | bytes 196608 | tf_op args[1]
  1.7 0.0 copy-done.1
  1.7 0.0 copy-start.2
  1.7 0.1 copy.30.v_ref
  1.8 0.8 %copy-done.2 = bf16[256,192]{0,1:T(8,128)(2,1)S(1)} copy-done((bf16[256,192]{0,1:T(8,128)(2,1)S(1)}, bf16[256,192]{0,1:T(8,128)(2,1)}, u32[]{:S(2)}) %copy-start.2) | copy-done | bytes 98328
  2.6 0.0 copy-start.3
  2.6 0.1 copy.28.q_ref
  2.7 0.8 %copy-done.3 = bf16[256,192]{0,1:T(8,128)(2,1)S(1)} copy-done((bf16[256,192]{0,1:T(8,128)(2,1)S(1)}, bf16[256,192]{0,1:T(8,128)(2,1)}, u32[]{:S(2)}) %copy-start.3) | copy-done | bytes 98328
  3.5 0.1 copy.31.g_ref
  3.6 0.0 copy-start
  3.6 0.6 %copy-done = f32[64]{0:T(128)S(1)} copy-done((f32[64]{0:T(128)S(1)}, f32[64]{0:T(128)}, u32[]{:S(2)}) %copy-start) | copy-done | bytes 280
  4.2 0.8 %shard_map.92 = (bf16[16,8,192]{2,1,0:T(8,128)(2,1)}, bf16[384,192]{1,0:T(8,128)(2,1)S(1)}, bf16[384,192]{1,0:T(8,128)(2,1)S(1)}) custom-call(bf16[256,192]{1,0:T(8,128)(2,1)S(1)} %copy.28.q_ref, bf16[256,192]{1,0:T(8,128)(2,1)S(1)} %copy.29.k_ref, bf16[256,192]{1,0:T(8,128)(2,1)S(1)} %copy.30.v_ref, bf16[256,192]{1,0:T(8,128)(2,1)S(1)} %copy.31.g_ref, ...), custom_call_target="tpu_custom_call" | custom-call | tf_op jit(solution)/shard_map/pallas_call | solution.py:258
  5.1 4.8 %collective-permute-start = (bf16[384,192]{1,0:T(8,128)(2,1)S(1)}, bf16[384,192]{1,0:T(8,128)(2,1)S(1)}, u32[]{:S(2)}, u32[]{:S(2)}) collective-permute-start(bf16[384,192]{1,0:T(8,128)(2,1)S(1)} %get-tuple-element.17), channel_id=1, source_target_pairs={{0,2},{2,4},{4,6},{6,8},{8,10},{10,12},{12,14},{14,16},{16,18},{18... | collective-permute-start | bytes 442376 | tf_op jit(solution)/shard_map/ppermute | solution.py:263
  9.9 1.3 %collective-permute-start.1 = (bf16[384,192]{1,0:T(8,128)(2,1)S(1)}, bf16[384,192]{1,0:T(8,128)(2,1)S(1)}, u32[]{:S(2)}, u32[]{:S(2)}) collective-permute-start(bf16[384,192]{1,0:T(8,128)(2,1)S(1)} %get-tuple-element.18), channel_id=1, source_target_pairs={{2,0},{4,2},{6,4},{8,6},{10,8},{12,10},{14,12},{16,14},{18,16},{20... | collective-permute-start | bytes 442376 | tf_op jit(solution)/shard_map/ppermute | solution.py:264
  11.2 8.0 %all-to-all-start = ((bf16[16,8,192]{2,1,0:T(8,128)(2,1)}), bf16[16,8,192]{2,1,0:T(8,128)(2,1)S(1)}, u32[]{:S(2)}, u32[]{:S(2)}) async-start(bf16[16,8,192]{2,1,0:T(8,128)(2,1)} %get-tuple-element.19), calls=%async_computation | async-start | bytes 131072 | tf_op jit(solution)/shard_map/all_to_all | solution.py:265
  19.3 0.1 add_convert_fusion.edge_ref
  19.3 7.4 %all-to-all-done = bf16[16,8,192]{2,1,0:T(8,128)(2,1)S(1)} async-done(((bf16[16,8,192]{2,1,0:T(8,128)(2,1)}), bf16[16,8,192]{2,1,0:T(8,128)(2,1)S(1)}, u32[]{:S(2)}, u32[]{:S(2)}) %all-to-all-start) | async-done | bytes 49184 | tf_op jit(solution)/shard_map/all_to_all | solution.py:265
  26.8 0.0 collective-permute-done.before_ref
  26.8 0.0 collective-permute-done.1.after_ref
  26.8 3.5 %shard_map.93 = (bf16[256,192]{1,0:T(8,128)(2,1)S(1)}, bf16[256,192]{1,0:T(8,128)(2,1)S(1)}, f32[256,192]{1,0:T(8,128)S(1)}, f32[256,192]{1,0:T(8,128)S(1)}, f32[128,192]{1,0:T(8,128)S(1)}) custom-call(s32[2]{0:T(128)S(1)} %add_convert_fusion.edge_ref, bf16[256,192]{1,0:T(8,128)(2,1)S(1)} %copy.28.q_ref, bf16[256,192]{1,0:T(8,128)(2,1)S(1)} %copy.29.k_ref, ...), custom_call_target="tpu_custom_call" | custom-call | tf_op jit(solution)/shard_map/pallas_call | solution.py:269
  30.3 10.4 %all_to_all.19.parts_ref = f32[16,8,192]{2,1,0:T(8,128)S(1)} all-to-all(f32[16,8,192]{2,1,0:T(8,128)S(1)} %bitcast.9), channel_id=1, replica_groups=mesh['seq'=16,'head'=2] {'seq'}, dimensions={0} | all-to-all | bytes 196608 | tf_op jit(solution)/shard_map/all_to_all | solution.py:277
  40.7 0.9 %shard_map.94 = (f32[8,192]{1,0:T(8,128)S(1)}, f32[32,64]{1,0:T(8,128)}) custom-call(f32[16,8,192]{2,1,0:T(8,128)S(1)} %all_to_all.19.parts_ref, bf16[256,192]{1,0:T(8,128)(2,1)S(1)} %copy.29.k_ref, bf16[256,192]{1,0:T(8,128)(2,1)S(1)} %copy.30.v_ref), custom_call_target="tpu_custom_call" | custom-call | tf_op jit(solution)/shard_map/pallas_call | solution.py:278
  41.5 2.6 %all-to-all-start.2 = ((f32[32,1,64]{2,1,0:T(1,128)}), f32[32,1,64]{2,1,0:T(1,128)S(1)}, u32[]{:S(2)}, u32[]{:S(2)}) async-start(f32[32,1,64]{2,1,0:T(1,128)} %bitcast.6), calls=%async_computation.2 | async-start | bytes 32768 | tf_op jit(solution)/shard_map/all_to_all | solution.py:281
  44.1 0.7 %copy.35 = bf16[256,192]{0,1:T(8,128)(2,1)} copy(bf16[256,192]{1,0:T(8,128)(2,1)S(1)} %get-tuple-element.34) | data formatting | bytes 196608
  44.8 0.7 %copy.36 = bf16[256,192]{0,1:T(8,128)(2,1)} copy(bf16[256,192]{1,0:T(8,128)(2,1)S(1)} %get-tuple-element.35) | data formatting | bytes 196608
  45.6 0.1 shard_map.95
  45.7 0.7 %copy.37 = bf16[256,192]{0,1:T(8,128)(2,1)} copy(bf16[256,192]{1,0:T(8,128)(2,1)S(1)} %get-tuple-element.36) | data formatting | bytes 196608
  46.5 0.7 %copy.38 = bf16[256,192]{0,1:T(8,128)(2,1)} copy(bf16[256,192]{1,0:T(8,128)(2,1)S(1)} %get-tuple-element.37) | data formatting | bytes 196608
  47.2 4.0 %all-to-all-done.2 = f32[32,1,64]{2,1,0:T(1,128)S(1)} async-done(((f32[32,1,64]{2,1,0:T(1,128)}), f32[32,1,64]{2,1,0:T(1,128)S(1)}, u32[]{:S(2)}, u32[]{:S(2)}) %all-to-all-start.2) | async-done | bytes 8224 | tf_op jit(solution)/shard_map/all_to_all | solution.py:281
  51.2 0.6 %reduce_sum.9 = f32[64]{0:T(128)} reduce(f32[32,1,64]{2,1,0:T(1,128)S(1)} %all-to-all-done.2, f32[]{:T(128)} %constant.11.clone.1), dimensions={0,1}, to_apply=%region_0.0 | reduce | flops 1984 | bytes 8452 | tf_op jit(solution)/shard_map/reduce_sum | solution.py:285
Async XLA Ops:
  0.6 1.0 %copy-start.1 = (bf16[256,192]{0,1:T(8,128)(2,1)S(1)}, bf16[256,192]{0,1:T(8,128)(2,1)}, u32[]{:S(2)}) copy-start(bf16[256,192]{0,1:T(8,128)(2,1)} %param.7) | copy-start | bytes 294916
  1.7 0.9 %copy-start.2 = (bf16[256,192]{0,1:T(8,128)(2,1)S(1)}, bf16[256,192]{0,1:T(8,128)(2,1)}, u32[]{:S(2)}) copy-start(bf16[256,192]{0,1:T(8,128)(2,1)} %param.5) | copy-start | bytes 294916
  2.6 0.9 %copy-start.3 = (bf16[256,192]{0,1:T(8,128)(2,1)S(1)}, bf16[256,192]{0,1:T(8,128)(2,1)}, u32[]{:S(2)}) copy-start(bf16[256,192]{0,1:T(8,128)(2,1)} %param.9) | copy-start | bytes 294916
  3.6 0.7 %copy-start = (f32[64]{0:T(128)S(1)}, f32[64]{0:T(128)}, u32[]{:S(2)}) copy-start(f32[64]{0:T(128)} %param.8) | copy-start | bytes 772
  5.1 21.7 %collective-permute-start = (bf16[384,192]{1,0:T(8,128)(2,1)S(1)}, bf16[384,192]{1,0:T(8,128)(2,1)S(1)}, u32[]{:S(2)}, u32[]{:S(2)}) collective-permute-start(bf16[384,192]{1,0:T(8,128)(2,1)S(1)} %get-tuple-element.17), channel_id=1, source_target_pairs={{0,2},{2,4},{4,6},{6,8},{8,10},{10,12},{12,14},{14,16},{16,18},{18... | collective-permute-start | bytes 442376 | tf_op jit(solution)/shard_map/ppermute | solution.py:263
  9.9 16.9 %collective-permute-start.1 = (bf16[384,192]{1,0:T(8,128)(2,1)S(1)}, bf16[384,192]{1,0:T(8,128)(2,1)S(1)}, u32[]{:S(2)}, u32[]{:S(2)}) collective-permute-start(bf16[384,192]{1,0:T(8,128)(2,1)S(1)} %get-tuple-element.18), channel_id=1, source_target_pairs={{2,0},{4,2},{6,4},{8,6},{10,8},{12,10},{14,12},{16,14},{18,16},{20... | collective-permute-start | bytes 442376 | tf_op jit(solution)/shard_map/ppermute | solution.py:264
  11.2 15.6 %all-to-all-start = ((bf16[16,8,192]{2,1,0:T(8,128)(2,1)}), bf16[16,8,192]{2,1,0:T(8,128)(2,1)S(1)}, u32[]{:S(2)}, u32[]{:S(2)}) async-start(bf16[16,8,192]{2,1,0:T(8,128)(2,1)} %get-tuple-element.19), calls=%async_computation | async-start | bytes 131072 | tf_op jit(solution)/shard_map/all_to_all | solution.py:265
  41.5 9.7 %all-to-all-start.2 = ((f32[32,1,64]{2,1,0:T(1,128)}), f32[32,1,64]{2,1,0:T(1,128)S(1)}, u32[]{:S(2)}, u32[]{:S(2)}) async-start(f32[32,1,64]{2,1,0:T(1,128)} %bitcast.6), calls=%async_computation.2 | async-start | bytes 32768 | tf_op jit(solution)/shard_map/all_to_all | solution.py:281

commit v3 on v2

v3 whole, which is shorter than its diff:
```python
import functools

import jax
import jax.numpy as jnp
from jax import lax
from jax.experimental import pallas as pl
from jax.experimental.pallas import tpu as pltpu
from jax.sharding import PartitionSpec as P

HEAD_DIM = 64
BLOCK = 64
SUM_DEV = 4
PAIR = 2 * BLOCK
SCALE = HEAD_DIM ** (-0.5)
LOW = -1e30
VMEM = pl.BlockSpec(memory_space=pltpu.VMEM)
SMEM = pl.BlockSpec(memory_space=pltpu.SMEM)
PARAMS = pltpu.CompilerParams(vmem_limit_bytes=40 * 1024 * 1024)
F32 = jnp.float32
BF16 = jnp.bfloat16


def mm(a, b):
    return lax.dot_general(a, b, (((1,), (0,)), ((), ())), preferred_element_type=F32)


def mm_nt(a, b):
    return lax.dot_general(a, b, (((1,), (1,)), ((), ())), preferred_element_type=F32)


def mm_tn(a, b):
    return lax.dot_general(a, b, (((0,), (0,)), ((), ())), preferred_element_type=F32)


def pieces(x):
    high = x.astype(BF16)
    rest = x - high.astype(F32)
    middle = rest.astype(BF16)
    low = (rest - middle.astype(F32)).astype(BF16)
    return jnp.concatenate([high, middle, low], axis=0)


def segment_mask(first, rows, lanes, seg):
    row = lax.broadcasted_iota(jnp.int32, (rows, lanes), 0)
    lane = lax.broadcasted_iota(jnp.int32, (rows, lanes), 1)
    return row - first == lane // seg


def pool_kernel(q_ref, k_ref, v_ref, g_ref, w_ref, rows_ref, up_ref, down_ref):
    seg = w_ref.shape[1]
    n = 2 * SUM_DEV
    w = jnp.concatenate([w_ref[...]] * SUM_DEV, axis=1)
    w = jnp.broadcast_to(w, (n, w.shape[1]))
    pooled = jnp.zeros((n, k_ref.shape[0]), F32)
    for first, ref in ((0, k_ref), (SUM_DEV, v_ref)):
        weights = jnp.where(segment_mask(first, w.shape[0], w.shape[1], seg), w, 0.0)
        parts = mm_nt(pieces(weights), ref[...])
        pooled += parts[:n] + parts[n : 2 * n] + parts[2 * n :]
    rows_ref[...] = jnp.broadcast_to(pooled.astype(BF16)[None], rows_ref.shape)
    tok = k_ref.shape[1]
    up_ref[:, :PAIR] = k_ref[:, tok - PAIR :]
    up_ref[:, PAIR : 2 * PAIR] = v_ref[:, tok - PAIR :]
    up_ref[:, 2 * PAIR :] = jnp.concatenate(
        [q_ref[:, tok - BLOCK :], g_ref[:, tok - BLOCK :]], axis=1
    )
    down_ref[:, :PAIR] = k_ref[:, :PAIR]
    down_ref[:, PAIR : 2 * PAIR] = v_ref[:, :PAIR]
    down_ref[:, 2 * PAIR :] = jnp.concatenate([q_ref[:, :BLOCK], g_ref[:, :BLOCK]], axis=1)


def by_head(x):
    width = x.shape[0]
    x = x * jnp.asarray(SCALE, BF16)
    columns = []
    for h in range(width // HEAD_DIM):
        rows = [x[h * HEAD_DIM : (h + 1) * HEAD_DIM]]
        if h:
            rows.insert(0, jnp.zeros((h * HEAD_DIM, x.shape[1]), BF16))
        if (h + 1) * HEAD_DIM < width:
            rows.append(jnp.zeros((width - (h + 1) * HEAD_DIM, x.shape[1]), BF16))
        columns.append(jnp.concatenate(rows, axis=0))
    return jnp.concatenate(columns, axis=1)


def own_head(x):
    return jnp.concatenate(
        [
            x[h * HEAD_DIM : (h + 1) * HEAD_DIM, h * PAIR : (h + 1) * PAIR]
            for h in range(x.shape[0] // HEAD_DIM)
        ],
        axis=0,
    )


def head_sums(x):
    return jnp.concatenate(
        [
            jnp.sum(x[h * HEAD_DIM : (h + 1) * HEAD_DIM], axis=0, keepdims=True)
            for h in range(x.shape[0] // HEAD_DIM)
        ],
        axis=1,
    )


def top_of(x):
    return jnp.max(x, axis=0, keepdims=True)


def total_of(x):
    return jnp.sum(x, axis=0, keepdims=True)


def second_half(lanes):
    return lax.broadcasted_iota(jnp.int32, (1, lanes), 1) % PAIR >= BLOCK


def global_scores(rows, qm):
    shape = (rows.shape[0], qm.shape[1])
    is_key = lax.broadcasted_iota(jnp.int32, shape, 0) % (2 * SUM_DEV) < SUM_DEV
    return jnp.where(is_key, mm(rows, qm), LOW)


def value_rows(rows):
    return pltpu.roll(rows.astype(F32), rows.shape[0] - SUM_DEV, 0).astype(BF16)


def local_kernel(edge_ref, q_ref, k_ref, v_ref, before_ref, after_ref, exp_ref, top_ref, total_ref, kx_ref, vx_ref):
    width, tok = q_ref.shape
    lanes = width // HEAD_DIM * PAIR
    pairs = tok // PAIR
    for at, x_ref, own_ref in ((0, kx_ref, k_ref), (PAIR, vx_ref, v_ref)):
        x_ref[:PAIR] = before_ref[:, at : at + PAIR].T
        x_ref[PAIR : PAIR + tok] = own_ref[...].T
        x_ref[PAIR + tok :] = after_ref[:, at : at + PAIR].T
    second = second_half(lanes)
    for p in range(pairs):
        qm = by_head(q_ref[:, p * PAIR : (p + 1) * PAIR])
        start = BLOCK + p * PAIR
        s = mm(kx_ref[start : start + 2 * PAIR], qm)
        hide_low = second
        hide_high = jnp.logical_not(second)
        if p == 0:
            hide_low = jnp.logical_or(hide_low, edge_ref[0] == 1)
        if p == pairs - 1:
            hide_high = jnp.logical_or(hide_high, edge_ref[1] == 1)
        s = jnp.concatenate(
            [
                s[:BLOCK] + jnp.where(hide_low, LOW, 0.0),
                s[BLOCK : 3 * BLOCK],
                s[3 * BLOCK :] + jnp.where(hide_high, LOW, 0.0),
            ],
            axis=0,
        )
        top = top_of(s)
        s = jnp.exp(s - top)
        exp_ref[p] = s
        top_ref[p] = top
        total_ref[p] = total_of(s)


def global_kernel(q_ref, g_ref, vx_ref, rows_ref, exp_ref, top_ref, total_ref, att_ref, part_ref, ds_ref, factor_ref, delta_ref):
    width, tok = q_ref.shape
    rows = rows_ref[...]
    values_g = value_rows(rows)
    part = jnp.zeros(part_ref.shape, F32)
    for p in range(tok // PAIR):
        own = slice(p * PAIR, (p + 1) * PAIR)
        start = BLOCK + p * PAIR
        g = g_ref[:, own]
        qm, gm = by_head(q_ref[:, own]), by_head(g)
        s = global_scores(rows, qm)
        local_top = top_ref[p]
        top = jnp.maximum(local_top, top_of(s))
        s = jnp.exp(s - top)
        factor = jnp.exp(local_top - top)
        inverse = 1.0 / (total_ref[p] * factor + total_of(s))
        factor = factor * inverse
        w = s * inverse
        probs = (exp_ref[p] * factor).astype(BF16)
        att = mm_tn(vx_ref[start : start + 2 * PAIR], probs) + mm_tn(values_g, w.astype(BF16))
        att = own_head(att).astype(BF16)
        att_ref[:, own] = att
        delta = head_sums(g.astype(F32) * att.astype(F32)) * SCALE
        ds = (w * (mm(values_g, gm) - delta)).astype(BF16)
        part += mm_nt(ds, qm) + mm_nt(pltpu.roll(w, SUM_DEV, 0).astype(BF16), gm)
        ds_ref[p] = ds
        factor_ref[p] = factor
        delta_ref[p] = delta
    part_ref[...] = part * (1.0 / SCALE)


def gradient_kernel(q_ref, g_ref, kx_ref, vx_ref, rows_ref, exp_ref, before_ref, after_ref, ds_ref, factor_ref, delta_ref, qg_ref, kg_ref, vg_ref):
    width, tok = q_ref.shape
    lanes = width // HEAD_DIM * PAIR
    rows = rows_ref[...]
    kg = [jnp.zeros((width, PAIR), F32) for _ in range(tok // PAIR + 1)]
    vg = [jnp.zeros((width, PAIR), F32) for _ in range(tok // PAIR + 1)]
    for p in range(tok // PAIR):
        own = slice(p * PAIR, (p + 1) * PAIR)
        start = BLOCK + p * PAIR
        near = slice(start, start + 2 * PAIR)
        qm, gm = by_head(q_ref[:, own]), by_head(g_ref[:, own])
        w = exp_ref[p] * factor_ref[p]
        probs = w.astype(BF16)
        ds = (w * (mm(vx_ref[near], gm) - delta_ref[p])).astype(BF16)
        qg = own_head(mm_tn(kx_ref[near], ds) + mm_tn(rows, ds_ref[p]))
        qg_ref[:, own] = qg.astype(BF16)
        kgp, vgp = mm_nt(qm, ds), mm_nt(gm, probs)
        for b in range(2):
            kg[p + b] += kgp[:, b * PAIR : (b + 1) * PAIR]
            vg[p + b] += vgp[:, b * PAIR : (b + 1) * PAIR]

    second = second_half(lanes)
    edges = jnp.concatenate([before_ref[:, 2 * PAIR :], after_ref[:, 2 * PAIR :]], axis=1)
    q = jnp.concatenate([edges[:, :BLOCK], edges[:, PAIR : PAIR + BLOCK]], axis=1)
    g = jnp.concatenate([edges[:, BLOCK:PAIR], edges[:, PAIR + BLOCK :]], axis=1)
    qm, gm = by_head(q), by_head(g)
    low, high = slice(0, 3 * BLOCK), slice(tok + BLOCK, tok + 4 * BLOCK)
    values_g = value_rows(rows)
    s = jnp.where(second, mm(kx_ref[high], qm), mm(kx_ref[low], qm))
    sg = global_scores(rows, qm)
    top = jnp.maximum(top_of(s), top_of(sg))
    s, sg = jnp.exp(s - top), jnp.exp(sg - top)
    inverse = 1.0 / (total_of(s) + total_of(sg))
    s, sg = s * inverse, sg * inverse
    probs = s.astype(BF16)
    att = jnp.where(second, mm_tn(vx_ref[high], probs), mm_tn(vx_ref[low], probs))
    att = own_head(att + mm_tn(values_g, sg.astype(BF16))).astype(BF16)
    delta = head_sums(g.astype(F32) * att.astype(F32)) * SCALE
    near_low, near_high = slice(PAIR, PAIR + BLOCK), slice(tok + BLOCK, tok + PAIR)
    dp = jnp.where(second, mm(vx_ref[near_high], gm), mm(vx_ref[near_low], gm))
    w = jnp.where(second, s[:BLOCK], s[2 * BLOCK :])
    ds = w * (dp - delta)
    ds = jnp.concatenate([jnp.where(second, 0.0, ds), jnp.where(second, ds, 0.0)], axis=0)
    w = jnp.concatenate([jnp.where(second, 0.0, w), jnp.where(second, w, 0.0)], axis=0)
    kge, vge = mm_nt(qm, ds.astype(BF16)), mm_nt(gm, w.astype(BF16))
    for grads, edge, ref in ((kg, kge, kg_ref), (vg, vge, vg_ref)):
        whole = jnp.concatenate(grads, axis=1)[:, BLOCK : BLOCK + tok]
        ref[:, :BLOCK] = (whole[:, :BLOCK] + edge[:, :BLOCK]) * (1.0 / SCALE)
        ref[:, BLOCK : tok - BLOCK] = whole[:, BLOCK : tok - BLOCK] * (1.0 / SCALE)
        ref[:, tok - BLOCK :] = (whole[:, tok - BLOCK :] + edge[:, BLOCK:]) * (1.0 / SCALE)


def owned_kernel(parts_ref, k_ref, v_ref, owned_ref, term_ref):
    owned = jnp.sum(parts_ref[...], axis=0)
    owned_ref[...] = owned
    split = pieces(owned)
    n = 2 * SUM_DEV
    seg = k_ref.shape[1] // SUM_DEV
    total = jnp.zeros((1, k_ref.shape[1]), F32)
    for first, ref in ((0, k_ref), (SUM_DEV, v_ref)):
        met = mm(split, ref[...])
        met = met[:n] + met[n : 2 * n] + met[2 * n :]
        met = jnp.where(segment_mask(first, met.shape[0], met.shape[1], seg), met, 0.0)
        total += jnp.sum(met, axis=0, keepdims=True)
    term = total[:, :seg]
    for j in range(1, SUM_DEV):
        term += total[:, j * seg : (j + 1) * seg]
    term_ref[...] = jnp.broadcast_to(term, term_ref.shape)


def finish_kernel(owned_ref, kg_ref, vg_ref, w_ref, key_ref, value_ref):
    seg = w_ref.shape[1]
    columns = owned_ref[...].T
    w = w_ref[...]
    for first, grad_ref, out_ref in ((0, kg_ref, key_ref), (SUM_DEV, vg_ref, value_ref)):
        pooled = jnp.concatenate(
            [columns[:, first + j : first + j + 1] * w for j in range(SUM_DEV)], axis=1
        )
        out_ref[...] = (grad_ref[...] + pooled).astype(BF16)


def shaped(shape, dtype):
    return jax.ShapeDtypeStruct(shape, dtype)


def call(kernel, outs, count, first=VMEM):
    return pl.pallas_call(
        kernel,
        out_shape=outs,
        in_specs=[first] + [VMEM] * (count - 1),
        out_specs=[VMEM] * len(outs),
        compiler_params=PARAMS,
    )


def local(queries, key_states, value_states, pool_weight, out_grad):
    tok, width = queries.shape
    group_index = lax.axis_index("seq")
    groups = lax.axis_size("seq")
    everyone = groups * lax.axis_size("head")
    n = 2 * SUM_DEV
    seg = pool_weight.shape[0]
    pairs, lanes = tok // PAIR, width // HEAD_DIM * PAIR
    weight_row = pool_weight.reshape(1, seg)
    q, k, v, g = queries.T, key_states.T, value_states.T, out_grad.T
    halo = shaped((width, 3 * PAIR), BF16)
    own = shaped((width, tok), BF16)
    grad = shaped((width, tok), F32)
    ext = shaped((tok + 2 * PAIR, width), BF16)
    stat = shaped((pairs, 1, lanes), F32)

    summary, up, down = call(pool_kernel, [shaped((groups, n, width), BF16), halo, halo], 5)(
        q, k, v, g, weight_row
    )
    before = lax.ppermute(up, "seq", [(i, i + 1) for i in range(groups - 1)])
    after = lax.ppermute(down, "seq", [(i + 1, i) for i in range(groups - 1)])
    rows = lax.all_to_all(summary, "seq", split_axis=0, concat_axis=0)
    rows = rows.reshape(groups * n, width)
    edge = jnp.stack([group_index == 0, group_index == groups - 1]).astype(jnp.int32)
    exps, top, total, kx, vx = call(
        local_kernel, [shaped((pairs, 2 * PAIR, lanes), F32), stat, stat, ext, ext], 6, SMEM
    )(edge, q, k, v, before, after)

    attended, part, ds, factor, delta = call(
        global_kernel,
        [own, shaped((groups * n, width), F32), shaped((pairs, groups * n, lanes), BF16), stat, stat],
        7,
    )(q, g, vx, rows, exps, top, total)
    parts = lax.all_to_all(part.reshape(groups, n, width), "seq", split_axis=0, concat_axis=0)
    query_grad, key_part, value_part = call(gradient_kernel, [own, grad, grad], 11)(
        q, g, kx, vx, rows, exps, before, after, ds, factor, delta
    )
    owned, term = call(owned_kernel, [shaped((n, width), F32), shaped((everyone, seg), F32)], 3)(
        parts, k, v
    )
    terms = lax.all_to_all(term, ("seq", "head"), split_axis=0, concat_axis=0)
    key_grad, value_grad = call(finish_kernel, [own, own], 4)(
        owned, key_part, value_part, weight_row
    )
    return (attended.T, query_grad.T, key_grad.T, value_grad.T, terms.sum(0))


def solution(mesh):
    return jax.shard_map(
        local,
        mesh=mesh,
        in_specs=(P("seq", "head"), P("seq", "head"), P("seq", "head"), P(), P("seq", "head")),
        out_specs=(P("seq", "head"), P("seq", "head"), P("seq", "head"), P("seq", "head"), P()),
        check_vma=False,
    )
```

time: 52.2 us -> 51.2 us (0.981)
  Pallas kernels: 5.31 us -> 7.64 us
  local copies, waits for them, and re-layouts: 6.52 us -> 4.23 us
  waiting for transfers between devices: 11.5 us -> 10.3 us
    unnamed x16 -> x18, local copies, waits for them, and re-layouts: 6.52 us -> 4.23 us
    pallas_call x1 -> x3, Pallas kernels: 3.48 us -> 4.75 us  [the longest x1 1.99 us: local(): call(gradient_kernel, [own, grad, grad], 11)]
    pallas_call x1, Pallas kernels: 0.12 us -> 1.21 us  [local(): call(finish_kernel, [own, own], 4)(owned, key_part, value_part, weight_row)]
    all_to_all x1, waiting for transfers between devices: 7.45 us -> 6.38 us  [local(): rows = lax.all_to_all(summary, 'seq', split_axis=0, concat_axis=0)]
  transfers between devices with their start and end apart: 4 -> 4, of which waited for: 2 -> 2; matrix products, arithmetic and copies ran while one was open for 6% -> 0% of each run, Pallas kernels for 0% -> 8%
where the time goes in v3:
time: 51.2 us; the launch traced here: 50.8 us
  starting transfers between devices  16.9 us (33%)
  blocking collectives  10.4 us (20%)
  waiting for transfers between devices  10.3 us (20%)
  Pallas kernels  7.64 us (15%)
  local copies, waits for them, and re-layouts  4.23 us (8%)
  between operations  0.72 us (1%)
  other arithmetic  0.63 us (1%)
    all_to_all x1, blocking collectives, local(): lax.all_to_all(part.reshape(groups, n, width), 'seq', split_axis=0, conca...  10.4 us
    all_to_all x1, starting transfers between devices, local(): rows = lax.all_to_all(summary, 'seq', split_axis=0, concat_axis=0)  8.03 us
    all_to_all x1, waiting for transfers between devices, local(): rows = lax.all_to_all(summary, 'seq', split_axis=0, concat_axis=0)  6.38 us
    ppermute x1, starting transfers between devices, local(): before = lax.ppermute(up, 'seq', [(i, i + 1) for i in range(groups - 1)])  4.97 us
    unnamed x18, local copies, waits for them, and re-layouts  4.23 us
    all_to_all x1, waiting for transfers between devices, local(): terms = lax.all_to_all(term, ('seq', 'head'), split_axis=0, concat_axis=0)  3.94 us
    all_to_all x1, starting transfers between devices, local(): terms = lax.all_to_all(term, ('seq', 'head'), split_axis=0, concat_axis=0)  2.56 us
    pallas_call x1, Pallas kernels, local(): call(gradient_kernel, [own, grad, grad], 11)  1.99 us
  transfers between devices with their start and end apart: 4, of which 2 were waited for; matrix products, arithmetic and copies ran while one was open for 0% of the time, Pallas kernels for 8%

profile of v3, /device:TPU:0, one launch (start us, length us, event | category | flops | bytes accessed | tf_op | source)
XLA Modules:
  0.0 50.8 jit_solution(5361242153687268078)
XLA Ops:
  0.6 0.0 copy-start.8
  0.6 0.6 %copy-done.8 = f32[64]{0:T(128)S(1)} copy-done((f32[64]{0:T(128)S(1)}, f32[64]{0:T(128)}, u32[]{:S(2)}) %copy-start.8) | copy-done | bytes 280
  1.3 0.0 copy-start
  1.3 0.9 %copy-done = bf16[256,192]{0,1:T(8,128)(2,1)S(1)} copy-done((bf16[256,192]{0,1:T(8,128)(2,1)S(1)}, bf16[256,192]{0,1:T(8,128)(2,1)}, u32[]{:S(2)}) %copy-start) | copy-done | bytes 98328
  2.2 0.0 copy-start.2
  2.2 0.9 %copy-done.2 = bf16[256,192]{0,1:T(8,128)(2,1)S(1)} copy-done((bf16[256,192]{0,1:T(8,128)(2,1)S(1)}, bf16[256,192]{0,1:T(8,128)(2,1)}, u32[]{:S(2)}) %copy-start.2) | copy-done | bytes 98328
  3.1 0.0 copy-start.4
  3.1 0.9 %copy-done.4 = bf16[256,192]{0,1:T(8,128)(2,1)S(1)} copy-done((bf16[256,192]{0,1:T(8,128)(2,1)S(1)}, bf16[256,192]{0,1:T(8,128)(2,1)}, u32[]{:S(2)}) %copy-start.4) | copy-done | bytes 98328
  4.0 0.0 copy-start.6
  4.0 0.9 %copy-done.6 = bf16[256,192]{0,1:T(8,128)(2,1)S(1)} copy-done((bf16[256,192]{0,1:T(8,128)(2,1)S(1)}, bf16[256,192]{0,1:T(8,128)(2,1)}, u32[]{:S(2)}) %copy-start.6) | copy-done | bytes 98328
  4.9 0.0 copy-start.5
  4.9 0.8 %shard_map.92 = (bf16[16,8,192]{2,1,0:T(8,128)(2,1)}, bf16[192,384]{1,0:T(8,128)(2,1)S(1)}, bf16[192,384]{1,0:T(8,128)(2,1)S(1)}) custom-call(bf16[192,256]{1,0:T(8,128)(2,1)S(1)} %bitcast.16, bf16[192,256]{1,0:T(8,128)(2,1)S(1)} %bitcast.23, bf16[192,256]{1,0:T(8,128)(2,1)S(1)} %bitcast.26, bf16[192,256]{1,0:T(8,128)(2,1)S(1)} %bitcast.20, f32[1,64]{1,0:T(1,128)S(1)} %bitcast.32), custom_call_target="tpu_custom_call" | custom-call | tf_op jit(solution)/shard_map/pallas_call | solution.py:303
  5.7 5.0 %collective-permute-start = (bf16[192,384]{1,0:T(8,128)(2,1)S(1)}, bf16[192,384]{1,0:T(8,128)(2,1)S(1)}, u32[]{:S(2)}, u32[]{:S(2)}) collective-permute-start(bf16[192,384]{1,0:T(8,128)(2,1)S(1)} %get-tuple-element.25), channel_id=1, source_target_pairs={{0,2},{2,4},{4,6},{6,8},{8,10},{10,12},{12,14},{14,16},{16,18},{18... | collective-permute-start | bytes 442376 | tf_op jit(solution)/shard_map/ppermute | solution.py:306
  10.7 1.3 %collective-permute-start.1 = (bf16[192,384]{1,0:T(8,128)(2,1)S(1)}, bf16[192,384]{1,0:T(8,128)(2,1)S(1)}, u32[]{:S(2)}, u32[]{:S(2)}) collective-permute-start(bf16[192,384]{1,0:T(8,128)(2,1)S(1)} %get-tuple-element.26), channel_id=1, source_target_pairs={{2,0},{4,2},{6,4},{8,6},{10,8},{12,10},{14,12},{16,14},{18,16},{20... | collective-permute-start | bytes 442376 | tf_op jit(solution)/shard_map/ppermute | solution.py:307
  12.0 8.0 %all-to-all-start = ((bf16[16,8,192]{2,1,0:T(8,128)(2,1)}), bf16[16,8,192]{2,1,0:T(8,128)(2,1)S(1)}, u32[]{:S(2)}, u32[]{:S(2)}) async-start(bf16[16,8,192]{2,1,0:T(8,128)(2,1)} %get-tuple-element.28), calls=%async_computation | async-start | bytes 131072 | tf_op jit(solution)/shard_map/all_to_all | solution.py:308
  20.0 0.1 add_convert_fusion.edge_ref
  20.1 0.0 collective-permute-done.before_ref
  20.1 0.0 collective-permute-done.1.after_ref
  20.1 0.0 copy-done.5
  20.1 0.0 copy-done.7
  20.1 0.0 copy-done.1
  20.1 1.0 %shard_map.93 = (f32[2,256,384]{2,1,0:T(8,128)S(1)}, f32[2,1,384]{2,1,0:T(1,128)S(1)}, f32[2,1,384]{2,1,0:T(1,128)S(1)}, bf16[512,192]{1,0:T(8,128)(2,1)S(1)}, bf16[512,192]{1,0:T(8,128)(2,1)S(1)}) custom-call(s32[2]{0:T(128)S(1)} %add_convert_fusion.edge_ref, bf16[192,256]{1,0:T(8,128)(2,1)S(1)} %bitcast.17, bf16[192,256]{1,0:T(8,128)(2,1)S(1)} %bitcast.24, ...), custom_call_target="tpu_custom_call" | custom-call | tf_op jit(solution)/shard_map/pallas_call | solution.py:311
  21.2 6.4 %all-to-all-done = bf16[16,8,192]{2,1,0:T(8,128)(2,1)S(1)} async-done(((bf16[16,8,192]{2,1,0:T(8,128)(2,1)}), bf16[16,8,192]{2,1,0:T(8,128)(2,1)S(1)}, u32[]{:S(2)}, u32[]{:S(2)}) %all-to-all-start) | async-done | bytes 49184 | tf_op jit(solution)/shard_map/all_to_all | solution.py:308
  27.5 0.0 copy-done.3
  27.5 1.7 %shard_map.94 = (bf16[192,256]{1,0:T(8,128)(2,1)}, f32[128,192]{1,0:T(8,128)S(1)}, bf16[2,128,384]{2,1,0:T(8,128)(2,1)S(1)}, f32[2,1,384]{2,1,0:T(1,128)S(1)}, f32[2,1,384]{2,1,0:T(1,128)S(1)}) custom-call(bf16[192,256]{1,0:T(8,128)(2,1)S(1)} %bitcast.18, bf16[192,256]{1,0:T(8,128)(2,1)S(1)} %bitcast.21, bf16[512,192]{1,0:T(8,128)(2,1)S(1)} %get-tuple-element.27.vx_ref, ...), custom_call_target="tpu_custom_call" | custom-call | tf_op jit(solution)/shard_map/pallas_call | solution.py:315
  29.3 10.4 %all_to_all.19.parts_ref = f32[16,8,192]{2,1,0:T(8,128)S(1)} all-to-all(f32[16,8,192]{2,1,0:T(8,128)S(1)} %bitcast.31), channel_id=1, replica_groups=mesh['seq'=16,'head'=2] {'seq'}, dimensions={0} | all-to-all | bytes 196608 | tf_op jit(solution)/shard_map/all_to_all | solution.py:320
  39.7 0.8 %shard_map.96 = (f32[8,192]{1,0:T(8,128)S(1)}, f32[32,64]{1,0:T(8,128)}) custom-call(f32[16,8,192]{2,1,0:T(8,128)S(1)} %all_to_all.19.parts_ref, bf16[192,256]{1,0:T(8,128)(2,1)S(1)} %bitcast.25, bf16[192,256]{1,0:T(8,128)(2,1)S(1)} %bitcast.28), custom_call_target="tpu_custom_call" | custom-call | tf_op jit(solution)/shard_map/pallas_call | solution.py:324
  40.5 2.6 %all-to-all-start.2 = ((f32[32,1,64]{2,1,0:T(1,128)}), f32[32,1,64]{2,1,0:T(1,128)S(1)}, u32[]{:S(2)}, u32[]{:S(2)}) async-start(f32[32,1,64]{2,1,0:T(1,128)} %bitcast.14), calls=%async_computation.2 | async-start | bytes 32768 | tf_op jit(solution)/shard_map/all_to_all | solution.py:327
  43.1 2.0 %shard_map.95 = (bf16[192,256]{1,0:T(8,128)(2,1)}, f32[192,256]{1,0:T(8,128)S(1)}, f32[192,256]{1,0:T(8,128)S(1)}) custom-call(bf16[192,256]{1,0:T(8,128)(2,1)S(1)} %bitcast.19, bf16[192,256]{1,0:T(8,128)(2,1)S(1)} %bitcast.22, bf16[512,192]{1,0:T(8,128)(2,1)S(1)} %get-tuple-element.33.kx_ref, bf16[512,192]{1,0:T(8,128)(2,1)S(1)} %get-tuple-element.27.vx_ref, ...), custom_call_target="tpu_custom_call" | custom-call | tf_op jit(solution)/shard_map/pallas_call | solution.py:321
  45.1 1.2 %shard_map.97 = (bf16[192,256]{1,0:T(8,128)(2,1)}, bf16[192,256]{1,0:T(8,128)(2,1)}) custom-call(f32[8,192]{1,0:T(8,128)S(1)} %get-tuple-element.39.owned_ref, f32[192,256]{1,0:T(8,128)S(1)} %get-tuple-element.40.kg_ref, f32[192,256]{1,0:T(8,128)S(1)} %get-tuple-element.41.vg_ref, f32[1,64]{1,0:T(1,128)S(1)} %bitcast.33), custom_call_target="tpu_custom_call" | custom-call | tf_op jit(solution)/shard_map/pallas_call | solution.py:328
  46.3 3.9 %all-to-all-done.2 = f32[32,1,64]{2,1,0:T(1,128)S(1)} async-done(((f32[32,1,64]{2,1,0:T(1,128)}), f32[32,1,64]{2,1,0:T(1,128)S(1)}, u32[]{:S(2)}, u32[]{:S(2)}) %all-to-all-start.2) | async-done | bytes 8224 | tf_op jit(solution)/shard_map/all_to_all | solution.py:327
  50.2 0.6 %reduce_sum.9 = f32[64]{0:T(128)} reduce(f32[32,1,64]{2,1,0:T(1,128)S(1)} %all-to-all-done.2, f32[]{:T(128)} %constant.11.clone.1), dimensions={0,1}, to_apply=%region_0.0 | reduce | flops 1984 | bytes 8452 | tf_op jit(solution)/shard_map/reduce_sum | solution.py:331
  (3 shorter events, 0.0 us)
Async XLA Ops:
  0.6 0.7 %copy-start.8 = (f32[64]{0:T(128)S(1)}, f32[64]{0:T(128)}, u32[]{:S(2)}) copy-start(f32[64]{0:T(128)} %param.8) | copy-start | bytes 772
  1.3 0.9 %copy-start = (bf16[256,192]{0,1:T(8,128)(2,1)S(1)}, bf16[256,192]{0,1:T(8,128)(2,1)}, u32[]{:S(2)}) copy-start(bf16[256,192]{0,1:T(8,128)(2,1)} %param.5) | copy-start | bytes 294916
  2.2 0.9 %copy-start.2 = (bf16[256,192]{0,1:T(8,128)(2,1)S(1)}, bf16[256,192]{0,1:T(8,128)(2,1)}, u32[]{:S(2)}) copy-start(bf16[256,192]{0,1:T(8,128)(2,1)} %param.9) | copy-start | bytes 294916
  3.1 0.9 %copy-start.4 = (bf16[256,192]{0,1:T(8,128)(2,1)S(1)}, bf16[256,192]{0,1:T(8,128)(2,1)}, u32[]{:S(2)}) copy-start(bf16[256,192]{0,1:T(8,128)(2,1)} %param.6) | copy-start | bytes 294916
  4.0 0.9 %copy-start.6 = (bf16[256,192]{0,1:T(8,128)(2,1)S(1)}, bf16[256,192]{0,1:T(8,128)(2,1)}, u32[]{:S(2)}) copy-start(bf16[256,192]{0,1:T(8,128)(2,1)} %param.7) | copy-start | bytes 294916
  4.9 15.2 %copy-start.5 = (bf16[256,192]{0,1:T(8,128)(2,1)S(1)}, bf16[256,192]{0,1:T(8,128)(2,1)}, u32[]{:S(2)}) copy-start(bf16[256,192]{0,1:T(8,128)(2,1)} %param.6) | copy-start | bytes 294916
  4.9 15.3 %copy-start.7 = (bf16[256,192]{0,1:T(8,128)(2,1)S(1)}, bf16[256,192]{0,1:T(8,128)(2,1)}, u32[]{:S(2)}) copy-start(bf16[256,192]{0,1:T(8,128)(2,1)} %param.7) | copy-start | bytes 294916
  5.7 14.4 %copy-start.1 = (bf16[256,192]{0,1:T(8,128)(2,1)S(1)}, bf16[256,192]{0,1:T(8,128)(2,1)}, u32[]{:S(2)}) copy-start(bf16[256,192]{0,1:T(8,128)(2,1)} %param.5) | copy-start | bytes 294916
  5.7 14.4 %collective-permute-start = (bf16[192,384]{1,0:T(8,128)(2,1)S(1)}, bf16[192,384]{1,0:T(8,128)(2,1)S(1)}, u32[]{:S(2)}, u32[]{:S(2)}) collective-permute-start(bf16[192,384]{1,0:T(8,128)(2,1)S(1)} %get-tuple-element.25), channel_id=1, source_target_pairs={{0,2},{2,4},{4,6},{6,8},{8,10},{10,12},{12,14},{14,16},{16,18},{18... | collective-permute-start | bytes 442376 | tf_op jit(solution)/shard_map/ppermute | solution.py:306
  10.7 9.4 %collective-permute-start.1 = (bf16[192,384]{1,0:T(8,128)(2,1)S(1)}, bf16[192,384]{1,0:T(8,128)(2,1)S(1)}, u32[]{:S(2)}, u32[]{:S(2)}) collective-permute-start(bf16[192,384]{1,0:T(8,128)(2,1)S(1)} %get-tuple-element.26), channel_id=1, source_target_pairs={{2,0},{4,2},{6,4},{8,6},{10,8},{12,10},{14,12},{16,14},{18,16},{20... | collective-permute-start | bytes 442376 | tf_op jit(solution)/shard_map/ppermute | solution.py:307
  12.0 15.6 %all-to-all-start = ((bf16[16,8,192]{2,1,0:T(8,128)(2,1)}), bf16[16,8,192]{2,1,0:T(8,128)(2,1)S(1)}, u32[]{:S(2)}, u32[]{:S(2)}) async-start(bf16[16,8,192]{2,1,0:T(8,128)(2,1)} %get-tuple-element.28), calls=%async_computation | async-start | bytes 131072 | tf_op jit(solution)/shard_map/all_to_all | solution.py:308
  20.1 7.5 %copy-start.3 = (bf16[256,192]{0,1:T(8,128)(2,1)S(1)}, bf16[256,192]{0,1:T(8,128)(2,1)}, u32[]{:S(2)}) copy-start(bf16[256,192]{0,1:T(8,128)(2,1)} %param.9) | copy-start | bytes 294916
  40.5 9.7 %all-to-all-start.2 = ((f32[32,1,64]{2,1,0:T(1,128)}), f32[32,1,64]{2,1,0:T(1,128)S(1)}, u32[]{:S(2)}, u32[]{:S(2)}) async-start(f32[32,1,64]{2,1,0:T(1,128)} %bitcast.14), calls=%async_computation.2 | async-start | bytes 32768 | tf_op jit(solution)/shard_map/all_to_all | solution.py:327

commit v4 on v3

--- a/solution.py
+++ b/solution.py
@@ -46,7 +46,17 @@
     return row - first == lane // seg
 
 
-def pool_kernel(q_ref, k_ref, v_ref, g_ref, w_ref, rows_ref, up_ref, down_ref):
+def pool_kernel(*refs):
+    sources, (rows_ref, up_ref, down_ref, *kept), sem = refs[:5], refs[5:13], refs[13]
+    q_ref, k_ref, v_ref, g_ref, w_ref = kept
+    copies = [
+        pltpu.make_async_copy(source, target, sem.at[i])
+        for i, (source, target) in enumerate(zip(sources, kept))
+    ]
+    for i in (4, 1, 2, 0, 3):
+        copies[i].start()
+    for i in (4, 1, 2):
+        copies[i].wait()
     seg = w_ref.shape[1]
     n = 2 * SUM_DEV
     w = jnp.concatenate([w_ref[...]] * SUM_DEV, axis=1)
@@ -57,6 +67,8 @@
         parts = mm_nt(pieces(weights), ref[...])
         pooled += parts[:n] + parts[n : 2 * n] + parts[2 * n :]
     rows_ref[...] = jnp.broadcast_to(pooled.astype(BF16)[None], rows_ref.shape)
+    copies[0].wait()
+    copies[3].wait()
     tok = k_ref.shape[1]
     up_ref[:, :PAIR] = k_ref[:, tok - PAIR :]
     up_ref[:, PAIR : 2 * PAIR] = v_ref[:, tok - PAIR :]
@@ -292,17 +304,21 @@
     n = 2 * SUM_DEV
     seg = pool_weight.shape[0]
     pairs, lanes = tok // PAIR, width // HEAD_DIM * PAIR
-    weight_row = pool_weight.reshape(1, seg)
-    q, k, v, g = queries.T, key_states.T, value_states.T, out_grad.T
     halo = shaped((width, 3 * PAIR), BF16)
     own = shaped((width, tok), BF16)
     grad = shaped((width, tok), F32)
     ext = shaped((tok + 2 * PAIR, width), BF16)
     stat = shaped((pairs, 1, lanes), F32)
 
-    summary, up, down = call(pool_kernel, [shaped((groups, n, width), BF16), halo, halo], 5)(
-        q, k, v, g, weight_row
-    )
+    arguments = (queries.T, key_states.T, value_states.T, out_grad.T, pool_weight.reshape(1, seg))
+    summary, up, down, q, k, v, g, weight_row = pl.pallas_call(
+        pool_kernel,
+        out_shape=[shaped((groups, n, width), BF16), halo, halo] + [own] * 4 + [shaped((1, seg), F32)],
+        in_specs=[pl.BlockSpec(memory_space=pltpu.HBM)] * 5,
+        out_specs=[VMEM] * 8,
+        scratch_shapes=[pltpu.SemaphoreType.DMA((5,))],
+        compiler_params=PARAMS,
+    )(*[pltpu.with_memory_space_constraint(x, pltpu.HBM) for x in arguments])
     before = lax.ppermute(up, "seq", [(i, i + 1) for i in range(groups - 1)])
     after = lax.ppermute(down, "seq", [(i + 1, i) for i in range(groups - 1)])
     rows = lax.all_to_all(summary, "seq", split_axis=0, concat_axis=0)

time: 51.2 us -> 47.8 us (0.934)
  local copies, waits for them, and re-layouts: 4.23 us -> 0 us
  Pallas kernels: 7.64 us -> 8.67 us
    unnamed x18 -> x0, local copies, waits for them, and re-layouts: 4.23 us -> none
    pallas_call x1, Pallas kernels: 0.83 us -> 1.87 us  [local(): pl.pallas_call(pool_kernel, out_shape=[shaped((groups, n, width), BF16),...]
  transfers between devices with their start and end apart: 4 -> 4, of which waited for: 2 -> 2; matrix products, arithmetic and copies ran while one was open for 0% -> 0% of each run, Pallas kernels for 8% -> 9%
where the time goes in v4:
time: 47.8 us; the launch traced here: 47.4 us
  starting transfers between devices  16.7 us (35%)
  waiting for transfers between devices  10.4 us (22%)
  blocking collectives  10.4 us (22%)
  Pallas kernels  8.67 us (18%)
  between operations  0.69 us (1%)
  other arithmetic  0.63 us (1%)
    all_to_all x1, blocking collectives, local(): lax.all_to_all(part.reshape(groups, n, width), 'seq', split_axis=0, conca...  10.4 us
    all_to_all x1, starting transfers between devices, local(): rows = lax.all_to_all(summary, 'seq', split_axis=0, concat_axis=0)  8.03 us
    all_to_all x1, waiting for transfers between devices, local(): rows = lax.all_to_all(summary, 'seq', split_axis=0, concat_axis=0)  6.41 us
    ppermute x1, starting transfers between devices, local(): before = lax.ppermute(up, 'seq', [(i, i + 1) for i in range(groups - 1)])  4.85 us
    all_to_all x1, waiting for transfers between devices, local(): terms = lax.all_to_all(term, ('seq', 'head'), split_axis=0, concat_axis=0)  3.94 us
    all_to_all x1, starting transfers between devices, local(): terms = lax.all_to_all(term, ('seq', 'head'), split_axis=0, concat_axis=0)  2.54 us
    pallas_call x1, Pallas kernels, local(): call(gradient_kernel, [own, grad, grad], 11)  1.99 us
    pallas_call x1, Pallas kernels, local(): pl.pallas_call(pool_kernel, out_shape=[shaped((groups, n, width), BF16),...  1.87 us
  transfers between devices with their start and end apart: 4, of which 2 were waited for; matrix products, arithmetic and copies ran while one was open for 0% of the time, Pallas kernels for 9%

profile of v4, /device:TPU:0, one launch (start us, length us, event | category | flops | bytes accessed | tf_op | source)
XLA Modules:
  0.0 47.4 jit_solution(3139854782637390672)
XLA Ops:
  0.6 1.9 %shard_map.92 = (bf16[16,8,192]{2,1,0:T(8,128)(2,1)}, bf16[192,384]{1,0:T(8,128)(2,1)S(1)}, bf16[192,384]{1,0:T(8,128)(2,1)S(1)}, bf16[192,256]{1,0:T(8,128)(2,1...) custom-call(bf16[192,256]{1,0:T(8,128)(2,1)} %bitcast.19, ...), custom_call_target="tpu_custom_call" | custom-call | tf_op jit(solution)/shard_map/pallas_call | solution.py:314
  2.5 4.9 %collective-permute-start = (bf16[192,384]{1,0:T(8,128)(2,1)S(1)}, bf16[192,384]{1,0:T(8,128)(2,1)S(1)}, u32[]{:S(2)}, u32[]{:S(2)}) collective-permute-start(bf16[192,384]{1,0:T(8,128)(2,1)S(1)} %get-tuple-element.34), channel_id=1, source_target_pairs={{0,2},{2,4},{4,6},{6,8},{8,10},{10,12},{12,14},{14,16},{16,18},{18... | collective-permute-start | bytes 442376 | tf_op jit(solution)/shard_map/ppermute | solution.py:322
  7.4 1.3 %collective-permute-start.1 = (bf16[192,384]{1,0:T(8,128)(2,1)S(1)}, bf16[192,384]{1,0:T(8,128)(2,1)S(1)}, u32[]{:S(2)}, u32[]{:S(2)}) collective-permute-start(bf16[192,384]{1,0:T(8,128)(2,1)S(1)} %get-tuple-element.35), channel_id=1, source_target_pairs={{2,0},{4,2},{6,4},{8,6},{10,8},{12,10},{14,12},{16,14},{18,16},{20... | collective-permute-start | bytes 442376 | tf_op jit(solution)/shard_map/ppermute | solution.py:323
  8.7 8.0 %all-to-all-start = ((bf16[16,8,192]{2,1,0:T(8,128)(2,1)}), bf16[16,8,192]{2,1,0:T(8,128)(2,1)S(1)}, u32[]{:S(2)}, u32[]{:S(2)}) async-start(bf16[16,8,192]{2,1,0:T(8,128)(2,1)} %get-tuple-element.37), calls=%async_computation | async-start | bytes 131072 | tf_op jit(solution)/shard_map/all_to_all | solution.py:324
  16.7 0.1 add_convert_fusion.edge_ref
  16.8 0.0 collective-permute-done.before_ref
  16.8 0.0 collective-permute-done.1.after_ref
  16.8 1.0 %shard_map.93 = (f32[2,256,384]{2,1,0:T(8,128)S(1)}, f32[2,1,384]{2,1,0:T(1,128)S(1)}, f32[2,1,384]{2,1,0:T(1,128)S(1)}, bf16[512,192]{1,0:T(8,128)(2,1)S(1)}, bf16[512,192]{1,0:T(8,128)(2,1)S(1)}) custom-call(s32[2]{0:T(128)S(1)} %add_convert_fusion.edge_ref, bf16[192,256]{1,0:T(8,128)(2,1)S(1)} %get-tuple-element.30.q_ref, ...), custom_call_target="tpu_custom_call" | custom-call | tf_op jit(solution)/shard_map/pallas_call | solution.py:327
  17.8 6.4 %all-to-all-done = bf16[16,8,192]{2,1,0:T(8,128)(2,1)S(1)} async-done(((bf16[16,8,192]{2,1,0:T(8,128)(2,1)}), bf16[16,8,192]{2,1,0:T(8,128)(2,1)S(1)}, u32[]{:S(2)}, u32[]{:S(2)}) %all-to-all-start) | async-done | bytes 49184 | tf_op jit(solution)/shard_map/all_to_all | solution.py:324
  24.2 1.7 %shard_map.94 = (bf16[192,256]{1,0:T(8,128)(2,1)}, f32[128,192]{1,0:T(8,128)S(1)}, bf16[2,128,384]{2,1,0:T(8,128)(2,1)S(1)}, f32[2,1,384]{2,1,0:T(1,128)S(1)}, f32[2,1,384]{2,1,0:T(1,128)S(1)}) custom-call(bf16[192,256]{1,0:T(8,128)(2,1)S(1)} %get-tuple-element.30.q_ref, bf16[192,256]{1,0:T(8,128)(2,1)S(1)} %get-tuple-element.31.g_ref, ...), custom_call_target="tpu_custom_call" | custom-call | tf_op jit(solution)/shard_map/pallas_call | solution.py:331
  26.0 10.4 %all_to_all.19.parts_ref = f32[16,8,192]{2,1,0:T(8,128)S(1)} all-to-all(f32[16,8,192]{2,1,0:T(8,128)S(1)} %bitcast.18), channel_id=1, replica_groups=mesh['seq'=16,'head'=2] {'seq'}, dimensions={0} | all-to-all | bytes 196608 | tf_op jit(solution)/shard_map/all_to_all | solution.py:336
  36.3 0.8 %shard_map.96 = (f32[8,192]{1,0:T(8,128)S(1)}, f32[32,64]{1,0:T(8,128)}) custom-call(f32[16,8,192]{2,1,0:T(8,128)S(1)} %all_to_all.19.parts_ref, bf16[192,256]{1,0:T(8,128)(2,1)S(1)} %get-tuple-element.32.k_ref, bf16[192,256]{1,0:T(8,128)(2,1)S(1)} %get-tuple-element.33.v_ref), custom_call_target="tpu_custom_call" | custom-call | tf_op jit(solution)/shard_map/pallas_call | solution.py:340
  37.2 2.5 %all-to-all-start.2 = ((f32[32,1,64]{2,1,0:T(1,128)}), f32[32,1,64]{2,1,0:T(1,128)S(1)}, u32[]{:S(2)}, u32[]{:S(2)}) async-start(f32[32,1,64]{2,1,0:T(1,128)} %bitcast.14), calls=%async_computation.2 | async-start | bytes 32768 | tf_op jit(solution)/shard_map/all_to_all | solution.py:343
  39.7 2.0 %shard_map.95 = (bf16[192,256]{1,0:T(8,128)(2,1)}, f32[192,256]{1,0:T(8,128)S(1)}, f32[192,256]{1,0:T(8,128)S(1)}) custom-call(bf16[192,256]{1,0:T(8,128)(2,1)S(1)} %get-tuple-element.30.q_ref, bf16[192,256]{1,0:T(8,128)(2,1)S(1)} %get-tuple-element.31.g_ref, bf16[512,192]{1,0:T(8,128)(2,1)S(1)} %get-tuple-element.42.kx_ref, ...), custom_call_target="tpu_custom_call" | custom-call | tf_op jit(solution)/shard_map/pallas_call | solution.py:337
  41.7 1.2 %shard_map.97 = (bf16[192,256]{1,0:T(8,128)(2,1)}, bf16[192,256]{1,0:T(8,128)(2,1)}) custom-call(f32[8,192]{1,0:T(8,128)S(1)} %get-tuple-element.48.owned_ref, f32[192,256]{1,0:T(8,128)S(1)} %get-tuple-element.49.kg_ref, f32[192,256]{1,0:T(8,128)S(1)} %get-tuple-element.50.vg_ref, f32[1,64]{1,0:T(1,128)S(1)} %get-tuple-element.51.w_ref), custom_call_target="tpu_custom_call" | custom-call | tf_op jit(solution)/shard_map/pallas_call | solution.py:344
  42.9 3.9 %all-to-all-done.2 = f32[32,1,64]{2,1,0:T(1,128)S(1)} async-done(((f32[32,1,64]{2,1,0:T(1,128)}), f32[32,1,64]{2,1,0:T(1,128)S(1)}, u32[]{:S(2)}, u32[]{:S(2)}) %all-to-all-start.2) | async-done | bytes 8224 | tf_op jit(solution)/shard_map/all_to_all | solution.py:343
  46.9 0.6 %reduce_sum.9 = f32[64]{0:T(128)} reduce(f32[32,1,64]{2,1,0:T(1,128)S(1)} %all-to-all-done.2, f32[]{:T(128)} %constant.11.clone.1), dimensions={0,1}, to_apply=%region_0.0 | reduce | flops 1984 | bytes 8452 | tf_op jit(solution)/shard_map/reduce_sum | solution.py:347
Async XLA Ops:
  2.5 14.3 %collective-permute-start = (bf16[192,384]{1,0:T(8,128)(2,1)S(1)}, bf16[192,384]{1,0:T(8,128)(2,1)S(1)}, u32[]{:S(2)}, u32[]{:S(2)}) collective-permute-start(bf16[192,384]{1,0:T(8,128)(2,1)S(1)} %get-tuple-element.34), channel_id=1, source_target_pairs={{0,2},{2,4},{4,6},{6,8},{8,10},{10,12},{12,14},{14,16},{16,18},{18... | collective-permute-start | bytes 442376 | tf_op jit(solution)/shard_map/ppermute | solution.py:322
  7.4 9.4 %collective-permute-start.1 = (bf16[192,384]{1,0:T(8,128)(2,1)S(1)}, bf16[192,384]{1,0:T(8,128)(2,1)S(1)}, u32[]{:S(2)}, u32[]{:S(2)}) collective-permute-start(bf16[192,384]{1,0:T(8,128)(2,1)S(1)} %get-tuple-element.35), channel_id=1, source_target_pairs={{2,0},{4,2},{6,4},{8,6},{10,8},{12,10},{14,12},{16,14},{18,16},{20... | collective-permute-start | bytes 442376 | tf_op jit(solution)/shard_map/ppermute | solution.py:323
  8.7 15.6 %all-to-all-start = ((bf16[16,8,192]{2,1,0:T(8,128)(2,1)}), bf16[16,8,192]{2,1,0:T(8,128)(2,1)S(1)}, u32[]{:S(2)}, u32[]{:S(2)}) async-start(bf16[16,8,192]{2,1,0:T(8,128)(2,1)} %get-tuple-element.37), calls=%async_computation | async-start | bytes 131072 | tf_op jit(solution)/shard_map/all_to_all | solution.py:324
  37.2 9.7 %all-to-all-start.2 = ((f32[32,1,64]{2,1,0:T(1,128)}), f32[32,1,64]{2,1,0:T(1,128)S(1)}, u32[]{:S(2)}, u32[]{:S(2)}) async-start(f32[32,1,64]{2,1,0:T(1,128)} %bitcast.14), calls=%async_computation.2 | async-start | bytes 32768 | tf_op jit(solution)/shard_map/all_to_all | solution.py:343

commit v5 on v4

--- a/solution.py
+++ b/solution.py
@@ -321,7 +321,10 @@
     )(*[pltpu.with_memory_space_constraint(x, pltpu.HBM) for x in arguments])
     before = lax.ppermute(up, "seq", [(i, i + 1) for i in range(groups - 1)])
     after = lax.ppermute(down, "seq", [(i + 1, i) for i in range(groups - 1)])
-    rows = lax.all_to_all(summary, "seq", split_axis=0, concat_axis=0)
+    reverse = [list(range(groups))[::-1]]
+    rows = lax.all_to_all(
+        summary, "seq", split_axis=0, concat_axis=0, axis_index_groups=reverse
+    )
     rows = rows.reshape(groups * n, width)
     edge = jnp.stack([group_index == 0, group_index == groups - 1]).astype(jnp.int32)
     exps, top, total, kx, vx = call(
@@ -333,7 +336,9 @@
         [own, shaped((groups * n, width), F32), shaped((pairs, groups * n, lanes), BF16), stat, stat],
         7,
     )(q, g, vx, rows, exps, top, total)
-    parts = lax.all_to_all(part.reshape(groups, n, width), "seq", split_axis=0, concat_axis=0)
+    parts = lax.all_to_all(
+        part.reshape(groups, n, width), "seq", split_axis=0, concat_axis=0, axis_index_groups=reverse
+    )
     query_grad, key_part, value_part = call(gradient_kernel, [own, grad, grad], 11)(
         q, g, kx, vx, rows, exps, before, after, ds, factor, delta
     )

time: 47.8 us -> 47.8 us (level)
  waiting for transfers between devices: 10.4 us -> 5.8 us
  starting transfers between devices: 16.7 us -> 21.1 us
    all_to_all x1, waiting for transfers between devices: 6.41 us -> 1.85 us  [local(): lax.all_to_all(summary, 'seq', split_axis=0, concat_axis=0, axis_index_gr...]
    all_to_all x1, starting transfers between devices: 8.03 us -> 10.2 us  [local(): lax.all_to_all(summary, 'seq', split_axis=0, concat_axis=0, axis_index_gr...]
    all_to_all x1, starting transfers between devices: 2.54 us -> 4.69 us  [local(): terms = lax.all_to_all(term, ('seq', 'head'), split_axis=0, concat_axis=0)]
where the time goes in v5:
time: 47.8 us; the launch traced here: 47.5 us
  starting transfers between devices  21.1 us (44%)
  blocking collectives  10.7 us (22%)
  Pallas kernels  8.66 us (18%)
  waiting for transfers between devices  5.8 us (12%)
  between operations  0.67 us (1%)
  other arithmetic  0.63 us (1%)
    all_to_all x1, blocking collectives, local(): lax.all_to_all(part.reshape(groups, n, width), 'seq', split_axis=0, conca...  10.7 us
    all_to_all x1, starting transfers between devices, local(): lax.all_to_all(summary, 'seq', split_axis=0, concat_axis=0, axis_index_gr...  10.2 us
    ppermute x1, starting transfers between devices, local(): before = lax.ppermute(up, 'seq', [(i, i + 1) for i in range(groups - 1)])  4.85 us
    all_to_all x1, starting transfers between devices, local(): terms = lax.all_to_all(term, ('seq', 'head'), split_axis=0, concat_axis=0)  4.69 us
    all_to_all x1, waiting for transfers between devices, local(): terms = lax.all_to_all(term, ('seq', 'head'), split_axis=0, concat_axis=0)  3.94 us
    pallas_call x1, Pallas kernels, local(): call(gradient_kernel, [own, grad, grad], 11)  1.99 us
    pallas_call x1, Pallas kernels, local(): pl.pallas_call(pool_kernel, out_shape=[shaped((groups, n, width), BF16),...  1.87 us
    all_to_all x1, waiting for transfers between devices, local(): lax.all_to_all(summary, 'seq', split_axis=0, concat_axis=0, axis_index_gr...  1.85 us
  transfers between devices with their start and end apart: 4, of which 2 were waited for; matrix products, arithmetic and copies ran while one was open for 0% of the time, Pallas kernels for 9%

profile of v5, /device:TPU:0, one launch (start us, length us, event | category | flops | bytes accessed | tf_op | source)
XLA Modules:
  0.0 47.5 jit_solution(1284432087825581714)
XLA Ops:
  0.6 1.9 %shard_map.92 = (bf16[16,8,192]{2,1,0:T(8,128)(2,1)}, bf16[192,384]{1,0:T(8,128)(2,1)S(1)}, bf16[192,384]{1,0:T(8,128)(2,1)S(1)}, bf16[192,256]{1,0:T(8,128)(2,1...) custom-call(bf16[192,256]{1,0:T(8,128)(2,1)} %bitcast.19, ...), custom_call_target="tpu_custom_call" | custom-call | tf_op jit(solution)/shard_map/pallas_call | solution.py:314
  2.5 4.9 %collective-permute-start = (bf16[192,384]{1,0:T(8,128)(2,1)S(1)}, bf16[192,384]{1,0:T(8,128)(2,1)S(1)}, u32[]{:S(2)}, u32[]{:S(2)}) collective-permute-start(bf16[192,384]{1,0:T(8,128)(2,1)S(1)} %get-tuple-element.34), channel_id=1, source_target_pairs={{0,2},{2,4},{4,6},{6,8},{8,10},{10,12},{12,14},{14,16},{16,18},{18... | collective-permute-start | bytes 442376 | tf_op jit(solution)/shard_map/ppermute | solution.py:322
  7.4 1.3 %collective-permute-start.1 = (bf16[192,384]{1,0:T(8,128)(2,1)S(1)}, bf16[192,384]{1,0:T(8,128)(2,1)S(1)}, u32[]{:S(2)}, u32[]{:S(2)}) collective-permute-start(bf16[192,384]{1,0:T(8,128)(2,1)S(1)} %get-tuple-element.35), channel_id=1, source_target_pairs={{2,0},{4,2},{6,4},{8,6},{10,8},{12,10},{14,12},{16,14},{18,16},{20... | collective-permute-start | bytes 442376 | tf_op jit(solution)/shard_map/ppermute | solution.py:323
  8.7 10.2 %all-to-all-start = ((bf16[16,8,192]{2,1,0:T(8,128)(2,1)}), bf16[16,8,192]{2,1,0:T(8,128)(2,1)S(1)}, u32[]{:S(2)}, u32[]{:S(2)}) async-start(bf16[16,8,192]{2,1,0:T(8,128)(2,1)} %get-tuple-element.37), calls=%async_computation | async-start | bytes 131072 | tf_op jit(solution)/shard_map/all_to_all | solution.py:325
  18.9 0.1 add_convert_fusion.edge_ref
  19.0 0.0 collective-permute-done.before_ref
  19.0 0.0 collective-permute-done.1.after_ref
  19.0 1.0 %shard_map.93 = (f32[2,256,384]{2,1,0:T(8,128)S(1)}, f32[2,1,384]{2,1,0:T(1,128)S(1)}, f32[2,1,384]{2,1,0:T(1,128)S(1)}, bf16[512,192]{1,0:T(8,128)(2,1)S(1)}, bf16[512,192]{1,0:T(8,128)(2,1)S(1)}) custom-call(s32[2]{0:T(128)S(1)} %add_convert_fusion.edge_ref, bf16[192,256]{1,0:T(8,128)(2,1)S(1)} %get-tuple-element.30.q_ref, ...), custom_call_target="tpu_custom_call" | custom-call | tf_op jit(solution)/shard_map/pallas_call | solution.py:330
  20.0 1.8 %all-to-all-done = bf16[16,8,192]{2,1,0:T(8,128)(2,1)S(1)} async-done(((bf16[16,8,192]{2,1,0:T(8,128)(2,1)}), bf16[16,8,192]{2,1,0:T(8,128)(2,1)S(1)}, u32[]{:S(2)}, u32[]{:S(2)}) %all-to-all-start) | async-done | bytes 49184 | tf_op jit(solution)/shard_map/all_to_all | solution.py:325
  21.8 1.7 %shard_map.94 = (bf16[192,256]{1,0:T(8,128)(2,1)}, f32[128,192]{1,0:T(8,128)S(1)}, bf16[2,128,384]{2,1,0:T(8,128)(2,1)S(1)}, f32[2,1,384]{2,1,0:T(1,128)S(1)}, f32[2,1,384]{2,1,0:T(1,128)S(1)}) custom-call(bf16[192,256]{1,0:T(8,128)(2,1)S(1)} %get-tuple-element.30.q_ref, bf16[192,256]{1,0:T(8,128)(2,1)S(1)} %get-tuple-element.31.g_ref, ...), custom_call_target="tpu_custom_call" | custom-call | tf_op jit(solution)/shard_map/pallas_call | solution.py:334
  23.6 10.7 %all_to_all.19.parts_ref = f32[16,8,192]{2,1,0:T(8,128)S(1)} all-to-all(f32[16,8,192]{2,1,0:T(8,128)S(1)} %bitcast.18), channel_id=1, replica_groups={{30,28,26,24,22,20,18,16,14,12,10,8,6,4,2,0},{31,29,27,25,23,21,19,17,1..., dimensions={0} | all-to-all | bytes 196608 | tf_op jit(solution)/shard_map/all_to_all | solution.py:339
  34.3 0.8 %shard_map.96 = (f32[8,192]{1,0:T(8,128)S(1)}, f32[32,64]{1,0:T(8,128)}) custom-call(f32[16,8,192]{2,1,0:T(8,128)S(1)} %all_to_all.19.parts_ref, bf16[192,256]{1,0:T(8,128)(2,1)S(1)} %get-tuple-element.32.k_ref, bf16[192,256]{1,0:T(8,128)(2,1)S(1)} %get-tuple-element.33.v_ref), custom_call_target="tpu_custom_call" | custom-call | tf_op jit(solution)/shard_map/pallas_call | solution.py:345
  35.1 4.7 %all-to-all-start.2 = ((f32[32,1,64]{2,1,0:T(1,128)}), f32[32,1,64]{2,1,0:T(1,128)S(1)}, u32[]{:S(2)}, u32[]{:S(2)}) async-start(f32[32,1,64]{2,1,0:T(1,128)} %bitcast.14), calls=%async_computation.2 | async-start | bytes 32768 | tf_op jit(solution)/shard_map/all_to_all | solution.py:348
  39.8 2.0 %shard_map.95 = (bf16[192,256]{1,0:T(8,128)(2,1)}, f32[192,256]{1,0:T(8,128)S(1)}, f32[192,256]{1,0:T(8,128)S(1)}) custom-call(bf16[192,256]{1,0:T(8,128)(2,1)S(1)} %get-tuple-element.30.q_ref, bf16[192,256]{1,0:T(8,128)(2,1)S(1)} %get-tuple-element.31.g_ref, bf16[512,192]{1,0:T(8,128)(2,1)S(1)} %get-tuple-element.42.kx_ref, ...), custom_call_target="tpu_custom_call" | custom-call | tf_op jit(solution)/shard_map/pallas_call | solution.py:342
  41.8 1.2 %shard_map.97 = (bf16[192,256]{1,0:T(8,128)(2,1)}, bf16[192,256]{1,0:T(8,128)(2,1)}) custom-call(f32[8,192]{1,0:T(8,128)S(1)} %get-tuple-element.48.owned_ref, f32[192,256]{1,0:T(8,128)S(1)} %get-tuple-element.49.kg_ref, f32[192,256]{1,0:T(8,128)S(1)} %get-tuple-element.50.vg_ref, f32[1,64]{1,0:T(1,128)S(1)} %get-tuple-element.51.w_ref), custom_call_target="tpu_custom_call" | custom-call | tf_op jit(solution)/shard_map/pallas_call | solution.py:349
  43.0 3.9 %all-to-all-done.2 = f32[32,1,64]{2,1,0:T(1,128)S(1)} async-done(((f32[32,1,64]{2,1,0:T(1,128)}), f32[32,1,64]{2,1,0:T(1,128)S(1)}, u32[]{:S(2)}, u32[]{:S(2)}) %all-to-all-start.2) | async-done | bytes 8224 | tf_op jit(solution)/shard_map/all_to_all | solution.py:348
  47.0 0.6 %reduce_sum.9 = f32[64]{0:T(128)} reduce(f32[32,1,64]{2,1,0:T(1,128)S(1)} %all-to-all-done.2, f32[]{:T(128)} %constant.11.clone.1), dimensions={0,1}, to_apply=%region_0.0 | reduce | flops 1984 | bytes 8452 | tf_op jit(solution)/shard_map/reduce_sum | solution.py:352
Async XLA Ops:
  2.5 16.5 %collective-permute-start = (bf16[192,384]{1,0:T(8,128)(2,1)S(1)}, bf16[192,384]{1,0:T(8,128)(2,1)S(1)}, u32[]{:S(2)}, u32[]{:S(2)}) collective-permute-start(bf16[192,384]{1,0:T(8,128)(2,1)S(1)} %get-tuple-element.34), channel_id=1, source_target_pairs={{0,2},{2,4},{4,6},{6,8},{8,10},{10,12},{12,14},{14,16},{16,18},{18... | collective-permute-start | bytes 442376 | tf_op jit(solution)/shard_map/ppermute | solution.py:322
  7.4 11.6 %collective-permute-start.1 = (bf16[192,384]{1,0:T(8,128)(2,1)S(1)}, bf16[192,384]{1,0:T(8,128)(2,1)S(1)}, u32[]{:S(2)}, u32[]{:S(2)}) collective-permute-start(bf16[192,384]{1,0:T(8,128)(2,1)S(1)} %get-tuple-element.35), channel_id=1, source_target_pairs={{2,0},{4,2},{6,4},{8,6},{10,8},{12,10},{14,12},{16,14},{18,16},{20... | collective-permute-start | bytes 442376 | tf_op jit(solution)/shard_map/ppermute | solution.py:323
  8.7 13.2 %all-to-all-start = ((bf16[16,8,192]{2,1,0:T(8,128)(2,1)}), bf16[16,8,192]{2,1,0:T(8,128)(2,1)S(1)}, u32[]{:S(2)}, u32[]{:S(2)}) async-start(bf16[16,8,192]{2,1,0:T(8,128)(2,1)} %get-tuple-element.37), calls=%async_computation | async-start | bytes 131072 | tf_op jit(solution)/shard_map/all_to_all | solution.py:325
  35.1 11.8 %all-to-all-start.2 = ((f32[32,1,64]{2,1,0:T(1,128)}), f32[32,1,64]{2,1,0:T(1,128)S(1)}, u32[]{:S(2)}, u32[]{:S(2)}) async-start(f32[32,1,64]{2,1,0:T(1,128)} %bitcast.14), calls=%async_computation.2 | async-start | bytes 32768 | tf_op jit(solution)/shard_map/all_to_all | solution.py:348

commit v6 on v5

--- a/solution.py
+++ b/solution.py
@@ -321,9 +321,9 @@
     )(*[pltpu.with_memory_space_constraint(x, pltpu.HBM) for x in arguments])
     before = lax.ppermute(up, "seq", [(i, i + 1) for i in range(groups - 1)])
     after = lax.ppermute(down, "seq", [(i + 1, i) for i in range(groups - 1)])
-    reverse = [list(range(groups))[::-1]]
+    order = [[(i + groups // 2) % groups for i in range(groups)]]
     rows = lax.all_to_all(
-        summary, "seq", split_axis=0, concat_axis=0, axis_index_groups=reverse
+        summary, "seq", split_axis=0, concat_axis=0, axis_index_groups=order
     )
     rows = rows.reshape(groups * n, width)
     edge = jnp.stack([group_index == 0, group_index == groups - 1]).astype(jnp.int32)
@@ -337,7 +337,7 @@
         7,
     )(q, g, vx, rows, exps, top, total)
     parts = lax.all_to_all(
-        part.reshape(groups, n, width), "seq", split_axis=0, concat_axis=0, axis_index_groups=reverse
+        part.reshape(groups, n, width), "seq", split_axis=0, concat_axis=0, axis_index_groups=order
     )
     query_grad, key_part, value_part = call(gradient_kernel, [own, grad, grad], 11)(
         q, g, kx, vx, rows, exps, before, after, ds, factor, delta

time: 47.8 us -> 46.5 us (0.973)
  starting transfers between devices: 21.1 us -> 18.3 us
  waiting for transfers between devices: 5.8 us -> 8.08 us
  blocking collectives: 10.7 us -> 9.8 us
    all_to_all x1, waiting for transfers between devices: 1.85 us -> 4.15 us  [local(): lax.all_to_all(summary, 'seq', split_axis=0, concat_axis=0, axis_index_gr...]
    all_to_all x1, starting transfers between devices: 4.69 us -> 3.25 us  [local(): terms = lax.all_to_all(term, ('seq', 'head'), split_axis=0, concat_axis=0)]
    all_to_all x1, starting transfers between devices: 10.2 us -> 8.88 us  [local(): lax.all_to_all(summary, 'seq', split_axis=0, concat_axis=0, axis_index_gr...]
    all_to_all x1, blocking collectives: 10.7 us -> 9.8 us  [local(): lax.all_to_all(part.reshape(groups, n, width), 'seq', split_axis=0, conca...]
where the time goes in v6:
time: 46.5 us; the launch traced here: 46.1 us
  starting transfers between devices  18.3 us (39%)
  blocking collectives  9.8 us (21%)
  Pallas kernels  8.67 us (19%)
  waiting for transfers between devices  8.08 us (17%)
  between operations  0.67 us (1%)
  other arithmetic  0.63 us (1%)
    all_to_all x1, blocking collectives, local(): lax.all_to_all(part.reshape(groups, n, width), 'seq', split_axis=0, conca...  9.8 us
    all_to_all x1, starting transfers between devices, local(): lax.all_to_all(summary, 'seq', split_axis=0, concat_axis=0, axis_index_gr...  8.88 us
    ppermute x1, starting transfers between devices, local(): before = lax.ppermute(up, 'seq', [(i, i + 1) for i in range(groups - 1)])  4.85 us
    all_to_all x1, waiting for transfers between devices, local(): lax.all_to_all(summary, 'seq', split_axis=0, concat_axis=0, axis_index_gr...  4.15 us
    all_to_all x1, waiting for transfers between devices, local(): terms = lax.all_to_all(term, ('seq', 'head'), split_axis=0, concat_axis=0)  3.93 us
    all_to_all x1, starting transfers between devices, local(): terms = lax.all_to_all(term, ('seq', 'head'), split_axis=0, concat_axis=0)  3.25 us
    pallas_call x1, Pallas kernels, local(): call(gradient_kernel, [own, grad, grad], 11)  2 us
    pallas_call x1, Pallas kernels, local(): pl.pallas_call(pool_kernel, out_shape=[shaped((groups, n, width), BF16),...  1.87 us
  transfers between devices with their start and end apart: 4, of which 2 were waited for; matrix products, arithmetic and copies ran while one was open for 0% of the time, Pallas kernels for 9%

profile of v6, /device:TPU:0, one launch (start us, length us, event | category | flops | bytes accessed | tf_op | source)
XLA Modules:
  0.0 46.1 jit_solution(5631111167721112359)
XLA Ops:
  0.6 1.9 %shard_map.92 = (bf16[16,8,192]{2,1,0:T(8,128)(2,1)}, bf16[192,384]{1,0:T(8,128)(2,1)S(1)}, bf16[192,384]{1,0:T(8,128)(2,1)S(1)}, bf16[192,256]{1,0:T(8,128)(2,1...) custom-call(bf16[192,256]{1,0:T(8,128)(2,1)} %bitcast.19, ...), custom_call_target="tpu_custom_call" | custom-call | tf_op jit(solution)/shard_map/pallas_call | solution.py:314
  2.5 4.9 %collective-permute-start = (bf16[192,384]{1,0:T(8,128)(2,1)S(1)}, bf16[192,384]{1,0:T(8,128)(2,1)S(1)}, u32[]{:S(2)}, u32[]{:S(2)}) collective-permute-start(bf16[192,384]{1,0:T(8,128)(2,1)S(1)} %get-tuple-element.34), channel_id=1, source_target_pairs={{0,2},{2,4},{4,6},{6,8},{8,10},{10,12},{12,14},{14,16},{16,18},{18... | collective-permute-start | bytes 442376 | tf_op jit(solution)/shard_map/ppermute | solution.py:322
  7.4 1.3 %collective-permute-start.1 = (bf16[192,384]{1,0:T(8,128)(2,1)S(1)}, bf16[192,384]{1,0:T(8,128)(2,1)S(1)}, u32[]{:S(2)}, u32[]{:S(2)}) collective-permute-start(bf16[192,384]{1,0:T(8,128)(2,1)S(1)} %get-tuple-element.35), channel_id=1, source_target_pairs={{2,0},{4,2},{6,4},{8,6},{10,8},{12,10},{14,12},{16,14},{18,16},{20... | collective-permute-start | bytes 442376 | tf_op jit(solution)/shard_map/ppermute | solution.py:323
  8.7 8.9 %all-to-all-start = ((bf16[16,8,192]{2,1,0:T(8,128)(2,1)}), bf16[16,8,192]{2,1,0:T(8,128)(2,1)S(1)}, u32[]{:S(2)}, u32[]{:S(2)}) async-start(bf16[16,8,192]{2,1,0:T(8,128)(2,1)} %get-tuple-element.37), calls=%async_computation | async-start | bytes 131072 | tf_op jit(solution)/shard_map/all_to_all | solution.py:325
  17.6 0.1 add_convert_fusion.edge_ref
  17.6 0.0 collective-permute-done.before_ref
  17.6 0.0 collective-permute-done.1.after_ref
  17.6 1.0 %shard_map.93 = (f32[2,256,384]{2,1,0:T(8,128)S(1)}, f32[2,1,384]{2,1,0:T(1,128)S(1)}, f32[2,1,384]{2,1,0:T(1,128)S(1)}, bf16[512,192]{1,0:T(8,128)(2,1)S(1)}, bf16[512,192]{1,0:T(8,128)(2,1)S(1)}) custom-call(s32[2]{0:T(128)S(1)} %add_convert_fusion.edge_ref, bf16[192,256]{1,0:T(8,128)(2,1)S(1)} %get-tuple-element.30.q_ref, ...), custom_call_target="tpu_custom_call" | custom-call | tf_op jit(solution)/shard_map/pallas_call | solution.py:330
  18.7 4.1 %all-to-all-done = bf16[16,8,192]{2,1,0:T(8,128)(2,1)S(1)} async-done(((bf16[16,8,192]{2,1,0:T(8,128)(2,1)}), bf16[16,8,192]{2,1,0:T(8,128)(2,1)S(1)}, u32[]{:S(2)}, u32[]{:S(2)}) %all-to-all-start) | async-done | bytes 49184 | tf_op jit(solution)/shard_map/all_to_all | solution.py:325
  22.8 1.7 %shard_map.94 = (bf16[192,256]{1,0:T(8,128)(2,1)}, f32[128,192]{1,0:T(8,128)S(1)}, bf16[2,128,384]{2,1,0:T(8,128)(2,1)S(1)}, f32[2,1,384]{2,1,0:T(1,128)S(1)}, f32[2,1,384]{2,1,0:T(1,128)S(1)}) custom-call(bf16[192,256]{1,0:T(8,128)(2,1)S(1)} %get-tuple-element.30.q_ref, bf16[192,256]{1,0:T(8,128)(2,1)S(1)} %get-tuple-element.31.g_ref, ...), custom_call_target="tpu_custom_call" | custom-call | tf_op jit(solution)/shard_map/pallas_call | solution.py:334
  24.5 9.8 %all_to_all.19.parts_ref = f32[16,8,192]{2,1,0:T(8,128)S(1)} all-to-all(f32[16,8,192]{2,1,0:T(8,128)S(1)} %bitcast.18), channel_id=1, replica_groups={{16,18,20,22,24,26,28,30,0,2,4,6,8,10,12,14},{17,19,21,23,25,27,29,31,1..., dimensions={0} | all-to-all | bytes 196608 | tf_op jit(solution)/shard_map/all_to_all | solution.py:339
  34.3 0.8 %shard_map.96 = (f32[8,192]{1,0:T(8,128)S(1)}, f32[32,64]{1,0:T(8,128)}) custom-call(f32[16,8,192]{2,1,0:T(8,128)S(1)} %all_to_all.19.parts_ref, bf16[192,256]{1,0:T(8,128)(2,1)S(1)} %get-tuple-element.32.k_ref, bf16[192,256]{1,0:T(8,128)(2,1)S(1)} %get-tuple-element.33.v_ref), custom_call_target="tpu_custom_call" | custom-call | tf_op jit(solution)/shard_map/pallas_call | solution.py:345
  35.2 3.3 %all-to-all-start.2 = ((f32[32,1,64]{2,1,0:T(1,128)}), f32[32,1,64]{2,1,0:T(1,128)S(1)}, u32[]{:S(2)}, u32[]{:S(2)}) async-start(f32[32,1,64]{2,1,0:T(1,128)} %bitcast.14), calls=%async_computation.2 | async-start | bytes 32768 | tf_op jit(solution)/shard_map/all_to_all | solution.py:348
  38.4 2.0 %shard_map.95 = (bf16[192,256]{1,0:T(8,128)(2,1)}, f32[192,256]{1,0:T(8,128)S(1)}, f32[192,256]{1,0:T(8,128)S(1)}) custom-call(bf16[192,256]{1,0:T(8,128)(2,1)S(1)} %get-tuple-element.30.q_ref, bf16[192,256]{1,0:T(8,128)(2,1)S(1)} %get-tuple-element.31.g_ref, bf16[512,192]{1,0:T(8,128)(2,1)S(1)} %get-tuple-element.42.kx_ref, ...), custom_call_target="tpu_custom_call" | custom-call | tf_op jit(solution)/shard_map/pallas_call | solution.py:342
  40.4 1.2 %shard_map.97 = (bf16[192,256]{1,0:T(8,128)(2,1)}, bf16[192,256]{1,0:T(8,128)(2,1)}) custom-call(f32[8,192]{1,0:T(8,128)S(1)} %get-tuple-element.48.owned_ref, f32[192,256]{1,0:T(8,128)S(1)} %get-tuple-element.49.kg_ref, f32[192,256]{1,0:T(8,128)S(1)} %get-tuple-element.50.vg_ref, f32[1,64]{1,0:T(1,128)S(1)} %get-tuple-element.51.w_ref), custom_call_target="tpu_custom_call" | custom-call | tf_op jit(solution)/shard_map/pallas_call | solution.py:349
  41.7 3.9 %all-to-all-done.2 = f32[32,1,64]{2,1,0:T(1,128)S(1)} async-done(((f32[32,1,64]{2,1,0:T(1,128)}), f32[32,1,64]{2,1,0:T(1,128)S(1)}, u32[]{:S(2)}, u32[]{:S(2)}) %all-to-all-start.2) | async-done | bytes 8224 | tf_op jit(solution)/shard_map/all_to_all | solution.py:348
  45.6 0.6 %reduce_sum.9 = f32[64]{0:T(128)} reduce(f32[32,1,64]{2,1,0:T(1,128)S(1)} %all-to-all-done.2, f32[]{:T(128)} %constant.11.clone.1), dimensions={0,1}, to_apply=%region_0.0 | reduce | flops 1984 | bytes 8452 | tf_op jit(solution)/shard_map/reduce_sum | solution.py:352
Async XLA Ops:
  2.5 15.1 %collective-permute-start = (bf16[192,384]{1,0:T(8,128)(2,1)S(1)}, bf16[192,384]{1,0:T(8,128)(2,1)S(1)}, u32[]{:S(2)}, u32[]{:S(2)}) collective-permute-start(bf16[192,384]{1,0:T(8,128)(2,1)S(1)} %get-tuple-element.34), channel_id=1, source_target_pairs={{0,2},{2,4},{4,6},{6,8},{8,10},{10,12},{12,14},{14,16},{16,18},{18... | collective-permute-start | bytes 442376 | tf_op jit(solution)/shard_map/ppermute | solution.py:322
  7.4 10.3 %collective-permute-start.1 = (bf16[192,384]{1,0:T(8,128)(2,1)S(1)}, bf16[192,384]{1,0:T(8,128)(2,1)S(1)}, u32[]{:S(2)}, u32[]{:S(2)}) collective-permute-start(bf16[192,384]{1,0:T(8,128)(2,1)S(1)} %get-tuple-element.35), channel_id=1, source_target_pairs={{2,0},{4,2},{6,4},{8,6},{10,8},{12,10},{14,12},{16,14},{18,16},{20... | collective-permute-start | bytes 442376 | tf_op jit(solution)/shard_map/ppermute | solution.py:323
  8.7 14.1 %all-to-all-start = ((bf16[16,8,192]{2,1,0:T(8,128)(2,1)}), bf16[16,8,192]{2,1,0:T(8,128)(2,1)S(1)}, u32[]{:S(2)}, u32[]{:S(2)}) async-start(bf16[16,8,192]{2,1,0:T(8,128)(2,1)} %get-tuple-element.37), calls=%async_computation | async-start | bytes 131072 | tf_op jit(solution)/shard_map/all_to_all | solution.py:325
  35.2 10.4 %all-to-all-start.2 = ((f32[32,1,64]{2,1,0:T(1,128)}), f32[32,1,64]{2,1,0:T(1,128)S(1)}, u32[]{:S(2)}, u32[]{:S(2)}) async-start(f32[32,1,64]{2,1,0:T(1,128)} %bitcast.14), calls=%async_computation.2 | async-start | bytes 32768 | tf_op jit(solution)/shard_map/all_to_all | solution.py:348

commit v7 on v6

v7 whole, which is shorter than its diff:
```python
import functools

import jax
import jax.numpy as jnp
from jax import lax
from jax.experimental import pallas as pl
from jax.experimental.pallas import tpu as pltpu
from jax.sharding import PartitionSpec as P

HEAD_DIM = 64
BLOCK = 64
SUM_DEV = 4
PAIR = 2 * BLOCK
SCALE = HEAD_DIM ** (-0.5)
LOW = -1e30
VMEM = pl.BlockSpec(memory_space=pltpu.VMEM)
SMEM = pl.BlockSpec(memory_space=pltpu.SMEM)
PARAMS = pltpu.CompilerParams(vmem_limit_bytes=40 * 1024 * 1024)
F32 = jnp.float32
BF16 = jnp.bfloat16


def mm(a, b):
    return lax.dot_general(a, b, (((1,), (0,)), ((), ())), preferred_element_type=F32)


def mm_nt(a, b):
    return lax.dot_general(a, b, (((1,), (1,)), ((), ())), preferred_element_type=F32)


def mm_tn(a, b):
    return lax.dot_general(a, b, (((0,), (0,)), ((), ())), preferred_element_type=F32)


def pieces(x):
    high = x.astype(BF16)
    rest = x - high.astype(F32)
    middle = rest.astype(BF16)
    low = (rest - middle.astype(F32)).astype(BF16)
    return jnp.concatenate([high, middle, low], axis=0)


def segment_mask(first, rows, lanes, seg):
    row = lax.broadcasted_iota(jnp.int32, (rows, lanes), 0)
    lane = lax.broadcasted_iota(jnp.int32, (rows, lanes), 1)
    return row - first == lane // seg


def pool_kernel(*refs):
    sources, (rows_ref, up_ref, *kept), sem = refs[:5], refs[5:12], refs[12]
    q_ref, k_ref, v_ref, g_ref, w_ref = kept
    copies = [
        pltpu.make_async_copy(source, target, sem.at[i])
        for i, (source, target) in enumerate(zip(sources, kept))
    ]
    for i in (4, 1, 2, 0, 3):
        copies[i].start()
    for i in (4, 1, 2):
        copies[i].wait()
    seg = w_ref.shape[1]
    n = 2 * SUM_DEV
    w = jnp.concatenate([w_ref[...]] * SUM_DEV, axis=1)
    w = jnp.broadcast_to(w, (n, w.shape[1]))
    pooled = jnp.zeros((n, k_ref.shape[0]), F32)
    for first, ref in ((0, k_ref), (SUM_DEV, v_ref)):
        weights = jnp.where(segment_mask(first, w.shape[0], w.shape[1], seg), w, 0.0)
        parts = mm_nt(pieces(weights), ref[...])
        pooled += parts[:n] + parts[n : 2 * n] + parts[2 * n :]
    rows_ref[...] = jnp.broadcast_to(pooled.astype(BF16)[None], rows_ref.shape)
    copies[0].wait()
    copies[3].wait()
    tok = k_ref.shape[1]
    up_ref[:, :PAIR] = k_ref[:, tok - PAIR :]
    up_ref[:, PAIR : 2 * PAIR] = v_ref[:, tok - PAIR :]
    up_ref[:, 2 * PAIR :] = jnp.concatenate(
        [q_ref[:, tok - BLOCK :], g_ref[:, tok - BLOCK :]], axis=1
    )


def by_head(x):
    width = x.shape[0]
    x = x * jnp.asarray(SCALE, BF16)
    columns = []
    for h in range(width // HEAD_DIM):
        rows = [x[h * HEAD_DIM : (h + 1) * HEAD_DIM]]
        if h:
            rows.insert(0, jnp.zeros((h * HEAD_DIM, x.shape[1]), BF16))
        if (h + 1) * HEAD_DIM < width:
            rows.append(jnp.zeros((width - (h + 1) * HEAD_DIM, x.shape[1]), BF16))
        columns.append(jnp.concatenate(rows, axis=0))
    return jnp.concatenate(columns, axis=1)


def own_head(x):
    return jnp.concatenate(
        [
            x[h * HEAD_DIM : (h + 1) * HEAD_DIM, h * PAIR : (h + 1) * PAIR]
            for h in range(x.shape[0] // HEAD_DIM)
        ],
        axis=0,
    )


def head_sums(x):
    return jnp.concatenate(
        [
            jnp.sum(x[h * HEAD_DIM : (h + 1) * HEAD_DIM], axis=0, keepdims=True)
            for h in range(x.shape[0] // HEAD_DIM)
        ],
        axis=1,
    )


def top_of(x):
    return jnp.max(x, axis=0, keepdims=True)


def total_of(x):
    return jnp.sum(x, axis=0, keepdims=True)


def second_half(lanes):
    return lax.broadcasted_iota(jnp.int32, (1, lanes), 1) % PAIR >= BLOCK


def global_scores(rows, qm):
    shape = (rows.shape[0], qm.shape[1])
    is_key = lax.broadcasted_iota(jnp.int32, shape, 0) % (2 * SUM_DEV) < SUM_DEV
    return jnp.where(is_key, mm(rows, qm), LOW)


def value_rows(rows):
    return pltpu.roll(rows.astype(F32), rows.shape[0] - SUM_DEV, 0).astype(BF16)


def local_kernel(
    edge_ref, q_ref, k_ref, v_ref, g_ref, before_ref,
    exp_ref, top_ref, total_ref, qx_ref, gx_ref, kx_ref, vx_ref, kt_ref, vt_ref,
):
    width, tok = q_ref.shape
    lanes = width // HEAD_DIM * PAIR
    pairs = tok // PAIR
    for at, t_ref, x_ref, own_ref in ((0, kt_ref, kx_ref, k_ref), (PAIR, vt_ref, vx_ref, v_ref)):
        t_ref[:, :PAIR] = before_ref[:, at : at + PAIR]
        t_ref[:, PAIR:] = own_ref[...]
        x_ref[:PAIR] = before_ref[:, at : at + PAIR].T
        x_ref[PAIR:] = own_ref[...].T
    for at, x_ref, own_ref in ((2 * PAIR, qx_ref, q_ref), (2 * PAIR + BLOCK, gx_ref, g_ref)):
        nothing = jnp.zeros((width, BLOCK), BF16)
        x_ref[...] = jnp.concatenate([before_ref[:, at : at + BLOCK], own_ref[...], nothing], axis=1)
    second = second_half(lanes)
    for p in range(pairs):
        s = mm(kx_ref[p * PAIR : (p + 2) * PAIR], by_head(qx_ref[:, p * PAIR : (p + 1) * PAIR]))
        parts = [s[b * BLOCK : (b + 1) * BLOCK] for b in range(4)]
        parts[0] += jnp.where(second, LOW, 0.0)
        if p == 0:
            parts[1] += jnp.where(edge_ref[0] == 1, LOW, 0.0)
        parts[3] += jnp.where(second, 0.0, LOW)
        s = jnp.concatenate(parts, axis=0)
        top = top_of(s)
        s = jnp.exp(s - top)
        exp_ref[p] = s
        top_ref[p] = top
        total_ref[p] = total_of(s)

    @pl.when(edge_ref[1] == 1)
    def _():
        s = mm(kx_ref[tok:], by_head(qx_ref[:, tok:]))
        top = top_of(s)
        s = jnp.exp(s - top)
        exp_ref[pairs, :PAIR] = s
        top_ref[pairs] = top
        total_ref[pairs] = total_of(s)


def global_kernel(
    edge_ref, qx_ref, gx_ref, vt_ref, rows_ref, exp_ref, top_ref, total_ref,
    att_ref, part_ref, ds_ref, factor_ref, delta_ref,
):
    pairs = qx_ref.shape[1] // PAIR - 1
    rows = rows_ref[...]
    values_g = value_rows(rows)

    def pair(p, keys):
        own = slice(p * PAIR, (p + 1) * PAIR)
        near = slice(p * PAIR, p * PAIR + keys)
        g = gx_ref[:, own]
        qm, gm = by_head(qx_ref[:, own]), by_head(g)
        s = global_scores(rows, qm)
        local_top = top_ref[p]
        top = jnp.maximum(local_top, top_of(s))
        s = jnp.exp(s - top)
        factor = jnp.exp(local_top - top)
        inverse = 1.0 / (total_ref[p] * factor + total_of(s))
        factor = factor * inverse
        w = s * inverse
        probs = (exp_ref[p, :keys] * factor).astype(BF16)
        att = mm(vt_ref[:, near], probs) + mm_tn(values_g, w.astype(BF16))
        att = own_head(att).astype(BF16)
        att_ref[:, own] = att
        delta = head_sums(g.astype(F32) * att.astype(F32)) * SCALE
        ds = (w * (mm(values_g, gm) - delta)).astype(BF16)
        ds_ref[p] = ds
        factor_ref[p] = factor
        delta_ref[p] = delta
        part = mm_nt(ds, qm) + mm_nt(pltpu.roll(w, SUM_DEV, 0).astype(BF16), gm)
        return part * (1.0 / SCALE)

    part_ref[...] = sum(pair(p, 2 * PAIR) for p in range(pairs))

    @pl.when(edge_ref[1] == 1)
    def _():
        part_ref[...] += pair(pairs, PAIR)


def gradient_kernel(
    edge_ref, qx_ref, gx_ref, kt_ref, vx_ref, rows_ref, exp_ref, att_ref, ds_ref, factor_ref, delta_ref,
    qg_ref, kg_ref, vg_ref, back_ref,
):
    width, tok = kg_ref.shape
    pairs = qx_ref.shape[1] // PAIR - 1
    rows = rows_ref[...]

    def pair(p, keys):
        own = slice(p * PAIR, (p + 1) * PAIR)
        near = slice(p * PAIR, p * PAIR + keys)
        qm, gm = by_head(qx_ref[:, own]), by_head(gx_ref[:, own])
        w = exp_ref[p, :keys] * factor_ref[p]
        ds = (w * (mm(vx_ref[near], gm) - delta_ref[p])).astype(BF16)
        qg = own_head(mm(kt_ref[:, near], ds) + mm_tn(rows, ds_ref[p])).astype(BF16)
        qg_ref[:, own] = qg
        kg = mm_nt(qm, ds) * (1.0 / SCALE)
        vg = mm_nt(gm, w.astype(BF16)) * (1.0 / SCALE)
        return qg, kg, vg

    grads = [pair(p, 2 * PAIR) for p in range(pairs)]
    edge = jnp.concatenate([att_ref[:, :BLOCK], grads[0][0][:, :BLOCK]], axis=1)
    back_ref[:, 2 * PAIR :] = edge
    for at, i, ref in ((0, 1, kg_ref), (PAIR, 2, vg_ref)):
        back_ref[:, at : at + PAIR] = grads[0][i][:, :PAIR].astype(BF16)
        for p in range(pairs - 1):
            ref[:, p * PAIR : (p + 1) * PAIR] = grads[p][i][:, PAIR:] + grads[p + 1][i][:, :PAIR]
        ref[:, tok - PAIR :] = grads[-1][i][:, PAIR:]

    @pl.when(edge_ref[1] == 1)
    def _():
        _, kg, vg = pair(pairs, PAIR)
        kg_ref[:, tok - PAIR :] += kg
        vg_ref[:, tok - PAIR :] += vg


def owned_kernel(parts_ref, k_ref, v_ref, owned_ref, term_ref):
    owned = jnp.sum(parts_ref[...], axis=0)
    owned_ref[...] = owned
    split = pieces(owned)
    n = 2 * SUM_DEV
    seg = k_ref.shape[1] // SUM_DEV
    total = jnp.zeros((1, k_ref.shape[1]), F32)
    for first, ref in ((0, k_ref), (SUM_DEV, v_ref)):
        met = mm(split, ref[...])
        met = met[:n] + met[n : 2 * n] + met[2 * n :]
        met = jnp.where(segment_mask(first, met.shape[0], met.shape[1], seg), met, 0.0)
        total += jnp.sum(met, axis=0, keepdims=True)
    term = total[:, :seg]
    for j in range(1, SUM_DEV):
        term += total[:, j * seg : (j + 1) * seg]
    term_ref[...] = jnp.broadcast_to(term, term_ref.shape)


def finish_kernel(
    edge_ref, owned_ref, kg_ref, vg_ref, w_ref, back_ref, attx_ref, qgx_ref,
    key_ref, value_ref, att_ref, qg_ref,
):
    tok = kg_ref.shape[1]
    columns = owned_ref[...].T
    w = w_ref[...]
    for first, at, grad_ref, out_ref in ((0, 0, kg_ref, key_ref), (SUM_DEV, PAIR, vg_ref, value_ref)):
        pooled = jnp.concatenate(
            [columns[:, first + j : first + j + 1] * w for j in range(SUM_DEV)], axis=1
        )
        total = grad_ref[...] + pooled
        out_ref[:, : tok - PAIR] = total[:, : tok - PAIR].astype(BF16)
        total = total[:, tok - PAIR :] + back_ref[:, at : at + PAIR].astype(F32)
        out_ref[:, tok - PAIR :] = total.astype(BF16)
    last = edge_ref[1] == 1
    for at, x_ref, out_ref in ((0, attx_ref, att_ref), (BLOCK, qgx_ref, qg_ref)):
        x = x_ref[:, BLOCK : tok + BLOCK]
        out_ref[...] = x
        edge = back_ref[:, 2 * PAIR + at : 2 * PAIR + at + BLOCK]

        @pl.when(jnp.logical_not(last))
        def _():
            out_ref[:, tok - BLOCK :] = edge


def shaped(shape, dtype):
    return jax.ShapeDtypeStruct(shape, dtype)


def call(kernel, outs, count, first=VMEM):
    return pl.pallas_call(
        kernel,
        out_shape=outs,
        in_specs=[first] + [VMEM] * (count - 1),
        out_specs=[VMEM] * len(outs),
        compiler_params=PARAMS,
    )


def local(queries, key_states, value_states, pool_weight, out_grad):
    tok, width = queries.shape
    group_index = lax.axis_index("seq")
    groups = lax.axis_size("seq")
    everyone = groups * lax.axis_size("head")
    n = 2 * SUM_DEV
    seg = pool_weight.shape[0]
    pairs, lanes = tok // PAIR, width // HEAD_DIM * PAIR
    halo = shaped((width, 3 * PAIR), BF16)
    own = shaped((width, tok), BF16)
    grad = shaped((width, tok), F32)
    queries_x = shaped((width, tok + PAIR), BF16)
    keys_x = shaped((tok + PAIR, width), BF16)
    stat = shaped((pairs + 1, 1, lanes), F32)

    arguments = (queries.T, key_states.T, value_states.T, out_grad.T, pool_weight.reshape(1, seg))
    summary, up, q, k, v, g, weight_row = pl.pallas_call(
        pool_kernel,
        out_shape=[shaped((groups, n, width), BF16), halo] + [own] * 4 + [shaped((1, seg), F32)],
        in_specs=[pl.BlockSpec(memory_space=pltpu.HBM)] * 5,
        out_specs=[VMEM] * 7,
        scratch_shapes=[pltpu.SemaphoreType.DMA((5,))],
        compiler_params=PARAMS,
    )(*[pltpu.with_memory_space_constraint(x, pltpu.HBM) for x in arguments])
    before = lax.ppermute(up, "seq", [(i, i + 1) for i in range(groups - 1)])
    order = [[(i + groups // 2) % groups for i in range(groups)]]
    rows = lax.all_to_all(
        summary, "seq", split_axis=0, concat_axis=0, axis_index_groups=order
    )
    rows = rows.reshape(groups * n, width)
    edge = jnp.stack([group_index == 0, group_index == groups - 1]).astype(jnp.int32)
    exps, top, total, qx, gx, kx, vx, kt, vt = call(
        local_kernel,
        [shaped((pairs + 1, 2 * PAIR, lanes), F32), stat, stat]
        + [queries_x, queries_x, keys_x, keys_x, queries_x, queries_x],
        6,
        SMEM,
    )(edge, q, k, v, g, before)

    att_x, part, ds, factor, delta = call(
        global_kernel,
        [queries_x, shaped((groups * n, width), F32)]
        + [shaped((pairs + 1, groups * n, lanes), BF16), stat, stat],
        8,
        SMEM,
    )(edge, qx, gx, vt, rows, exps, top, total)
    parts = lax.all_to_all(
        part.reshape(groups, n, width), "seq", split_axis=0, concat_axis=0, axis_index_groups=order
    )
    qg_x, key_part, value_part, down = call(gradient_kernel, [queries_x, grad, grad, halo], 11, SMEM)(
        edge, qx, gx, kt, vx, rows, exps, att_x, ds, factor, delta
    )
    back = lax.ppermute(down, "seq", [(i + 1, i) for i in range(groups - 1)])
    parts, qg_x = lax.optimization_barrier((parts, qg_x))
    owned, term = call(owned_kernel, [shaped((n, width), F32), shaped((everyone, seg), F32)], 3)(
        parts, k, v
    )
    terms = lax.all_to_all(term, ("seq", "head"), split_axis=0, concat_axis=0)
    key_grad, value_grad, attended, query_grad = call(finish_kernel, [own] * 4, 8, SMEM)(
        edge, owned, key_part, value_part, weight_row, back, att_x, qg_x
    )
    return (attended.T, query_grad.T, key_grad.T, value_grad.T, terms.sum(0))


def solution(mesh):
    return jax.shard_map(
        local,
        mesh=mesh,
        in_specs=(P("seq", "head"), P("seq", "head"), P("seq", "head"), P(), P("seq", "head")),
        out_specs=(P("seq", "head"), P("seq", "head"), P("seq", "head"), P("seq", "head"), P()),
        check_vma=False,
    )
```

time: 46.5 us -> 44.3 us (0.953)
  blocking collectives: 9.8 us -> 0 us
  waiting for transfers between devices: 8.08 us -> 11.4 us
  starting transfers between devices: 18.3 us -> 20.9 us
  Pallas kernels: 8.67 us -> 10.3 us
    all_to_all x1 -> x0, blocking collectives: 9.8 us -> none  [local(): lax.all_to_all(part.reshape(groups, n, width), 'seq', split_axis=0, conca...]
    all_to_all x0 -> x1, starting transfers between devices: none -> 5.21 us  [local(): lax.all_to_all(part.reshape(groups, n, width), 'seq', split_axis=0, conca...]
    all_to_all x0 -> x1, waiting for transfers between devices: none -> 2.84 us  [local(): lax.all_to_all(part.reshape(groups, n, width), 'seq', split_axis=0, conca...]
    all_to_all x1, starting transfers between devices: 8.88 us -> 6.42 us  [local(): lax.all_to_all(summary, 'seq', split_axis=0, concat_axis=0, axis_index_gr...]
    pallas_call x4, Pallas kernels: 5.96 us -> 7.59 us  [the longest x1 2.31 us: local(): call(global_kernel, [queries_x, shaped((groups * n, width), F32)] + [shap...]
    all_to_all x1, waiting for transfers between devices: 3.93 us -> 5.08 us  [local(): terms = lax.all_to_all(term, ('seq', 'head'), split_axis=0, concat_axis=0)]
    all_to_all x1, waiting for transfers between devices: 4.15 us -> 3.43 us  [local(): lax.all_to_all(summary, 'seq', split_axis=0, concat_axis=0, axis_index_gr...]
  transfers between devices with their start and end apart: 4 -> 5, of which waited for: 2 -> 3; matrix products, arithmetic and copies ran while one was open for 0% -> 0% of each run, Pallas kernels for 9% -> 14%
where the time goes in v7:
time: 44.3 us; the launch traced here: 43.9 us
  starting transfers between devices  20.9 us (47%)
  waiting for transfers between devices  11.4 us (26%)
  Pallas kernels  10.3 us (23%)
  between operations  0.69 us (2%)
  other arithmetic  0.63 us (1%)
    all_to_all x1, starting transfers between devices, local(): lax.all_to_all(summary, 'seq', split_axis=0, concat_axis=0, axis_index_gr...  6.42 us
    all_to_all x1, starting transfers between devices, local(): lax.all_to_all(part.reshape(groups, n, width), 'seq', split_axis=0, conca...  5.21 us
    all_to_all x1, waiting for transfers between devices, local(): terms = lax.all_to_all(term, ('seq', 'head'), split_axis=0, concat_axis=0)  5.08 us
    ppermute x1, starting transfers between devices, local(): before = lax.ppermute(up, 'seq', [(i, i + 1) for i in range(groups - 1)])  4.85 us
    all_to_all x1, waiting for transfers between devices, local(): lax.all_to_all(summary, 'seq', split_axis=0, concat_axis=0, axis_index_gr...  3.43 us
    all_to_all x1, starting transfers between devices, local(): terms = lax.all_to_all(term, ('seq', 'head'), split_axis=0, concat_axis=0)  3.17 us
    all_to_all x1, waiting for transfers between devices, local(): lax.all_to_all(part.reshape(groups, n, width), 'seq', split_axis=0, conca...  2.84 us
    pallas_call x1, Pallas kernels, local(): call(global_kernel, [queries_x, shaped((groups * n, width), F32)] + [shap...  2.31 us
  transfers between devices with their start and end apart: 5, of which 3 were waited for; matrix products, arithmetic and copies ran while one was open for 0% of the time, Pallas kernels for 14%

profile of v7, /device:TPU:0, one launch (start us, length us, event | category | flops | bytes accessed | tf_op | source)
XLA Modules:
  0.0 43.9 jit_solution(3873889703515242200)
XLA Ops:
  0.6 1.9 %shard_map.92 = (bf16[16,8,192]{2,1,0:T(8,128)(2,1)}, bf16[192,384]{1,0:T(8,128)(2,1)S(1)}, bf16[192,256]{1,0:T(8,128)(2,1)S(1)}, bf16[192,256]{1,0:T(8,128)(2,1...) custom-call(bf16[192,256]{1,0:T(8,128)(2,1)} %bitcast.18, ...), custom_call_target="tpu_custom_call" | custom-call | tf_op jit(solution)/shard_map/pallas_call | solution.py:326
  2.5 4.9 %collective-permute-start = (bf16[192,384]{1,0:T(8,128)(2,1)S(1)}, bf16[192,384]{1,0:T(8,128)(2,1)S(1)}, u32[]{:S(2)}, u32[]{:S(2)}) collective-permute-start(bf16[192,384]{1,0:T(8,128)(2,1)S(1)} %get-tuple-element.41), channel_id=1, source_target_pairs={{0,2},{2,4},{4,6},{6,8},{8,10},{10,12},{12,14},{14,16},{16,18},{18... | collective-permute-start | bytes 442376 | tf_op jit(solution)/shard_map/ppermute | solution.py:334
  7.4 6.4 %all-to-all-start = ((bf16[16,8,192]{2,1,0:T(8,128)(2,1)}), bf16[16,8,192]{2,1,0:T(8,128)(2,1)S(1)}, u32[]{:S(2)}, u32[]{:S(2)}) async-start(bf16[16,8,192]{2,1,0:T(8,128)(2,1)} %get-tuple-element.45), calls=%async_computation | async-start | bytes 131072 | tf_op jit(solution)/shard_map/all_to_all | solution.py:336
  13.8 0.1 add_convert_fusion.edge_ref
  13.8 0.0 collective-permute-done.before_ref
  13.9 1.8 %shard_map.93 = (f32[3,256,384]{2,1,0:T(8,128)S(1)}, f32[3,1,384]{2,1,0:T(1,128)S(1)}, f32[3,1,384]{2,1,0:T(1,128)S(1)}, bf16[192,384]{1,0:T(8,128)(2,1)S(1)}, b...) custom-call(s32[2]{0:T(128)S(1)} %add_convert_fusion.edge_ref, ...), custom_call_target="tpu_custom_call" | custom-call | tf_op jit(solution)/shard_map/pallas_call | solution.py:341
  15.6 3.4 %all-to-all-done = bf16[16,8,192]{2,1,0:T(8,128)(2,1)S(1)} async-done(((bf16[16,8,192]{2,1,0:T(8,128)(2,1)}), bf16[16,8,192]{2,1,0:T(8,128)(2,1)S(1)}, u32[]{:S(2)}, u32[]{:S(2)}) %all-to-all-start) | async-done | bytes 49184 | tf_op jit(solution)/shard_map/all_to_all | solution.py:336
  19.0 2.3 %shard_map.94 = (bf16[192,384]{1,0:T(8,128)(2,1)S(1)}, f32[128,192]{1,0:T(8,128)}, bf16[3,128,384]{2,1,0:T(8,128)(2,1)S(1)}, f32[3,1,384]{2,1,0:T(1,128)S(1)}, f32[3,1,384]{2,1,0:T(1,128)S(1)}) custom-call(s32[2]{0:T(128)S(1)} %add_convert_fusion.edge_ref, bf16[192,384]{1,0:T(8,128)(2,1)S(1)} %get-tuple-element.42.qx_ref, ...), custom_call_target="tpu_custom_call" | custom-call | tf_op jit(solution)/shard_map/pallas_call | solution.py:349
  21.4 5.2 %all-to-all-start.1 = ((f32[16,8,192]{2,1,0:T(8,128)}), f32[16,8,192]{2,1,0:T(8,128)S(1)}, u32[]{:S(2)}, u32[]{:S(2)}) async-start(f32[16,8,192]{2,1,0:T(8,128)} %bitcast.8), calls=%async_computation.1 | async-start | bytes 262144 | tf_op jit(solution)/shard_map/all_to_all | solution.py:356
  26.6 1.5 %shard_map.95 = (bf16[192,384]{1,0:T(8,128)(2,1)S(1)}, f32[192,256]{1,0:T(8,128)S(1)}, f32[192,256]{1,0:T(8,128)S(1)}, bf16[192,384]{1,0:T(8,128)(2,1)S(1)}) custom-call(s32[2]{0:T(128)S(1)} %add_convert_fusion.edge_ref, bf16[192,384]{1,0:T(8,128)(2,1)S(1)} %get-tuple-element.42.qx_ref, bf16[192,384]{1,0:T(8,128)(2,1)S(1)} %get-tuple-element.43.gx_ref, ...), custom_call_target="tpu_custom_call" | custom-call | tf_op jit(solution)/shard_map/pallas_call | solution.py:359
  28.1 1.3 %collective-permute-start.1 = (bf16[192,384]{1,0:T(8,128)(2,1)S(1)}, bf16[192,384]{1,0:T(8,128)(2,1)S(1)}, u32[]{:S(2)}, u32[]{:S(2)}) collective-permute-start(bf16[192,384]{1,0:T(8,128)(2,1)S(1)} %get-tuple-element.62), channel_id=1, source_target_pairs={{2,0},{4,2},{6,4},{8,6},{10,8},{12,10},{14,12},{16,14},{18,16},{20... | collective-permute-start | bytes 442376 | tf_op jit(solution)/shard_map/ppermute | solution.py:362
  29.4 2.8 %all-to-all-done.1.parts_ref = f32[16,8,192]{2,1,0:T(8,128)S(1)} async-done(((f32[16,8,192]{2,1,0:T(8,128)}), f32[16,8,192]{2,1,0:T(8,128)S(1)}, u32[]{:S(2)}, u32[]{:S(2)}) %all-to-all-start.1) | async-done | bytes 98336 | tf_op jit(solution)/shard_map/all_to_all | solution.py:356
  32.2 0.8 %shard_map.96 = (f32[8,192]{1,0:T(8,128)S(1)}, f32[32,64]{1,0:T(8,128)}) custom-call(f32[16,8,192]{2,1,0:T(8,128)S(1)} %all-to-all-done.1.parts_ref, bf16[192,256]{1,0:T(8,128)(2,1)S(1)} %get-tuple-element.38.k_ref, bf16[192,256]{1,0:T(8,128)(2,1)S(1)} %get-tuple-element.39.v_ref), custom_call_target="tpu_custom_call" | custom-call | tf_op jit(solution)/shard_map/pallas_call | solution.py:364
  33.0 3.2 %all-to-all-start.2 = ((f32[32,1,64]{2,1,0:T(1,128)}), f32[32,1,64]{2,1,0:T(1,128)S(1)}, u32[]{:S(2)}, u32[]{:S(2)}) async-start(f32[32,1,64]{2,1,0:T(1,128)} %bitcast.14), calls=%async_computation.2 | async-start | bytes 32768 | tf_op jit(solution)/shard_map/all_to_all | solution.py:367
  36.2 0.0 collective-permute-done.1.back_ref
  36.2 2.1 %shard_map.97 = (bf16[192,256]{1,0:T(8,128)(2,1)}, bf16[192,256]{1,0:T(8,128)(2,1)}, bf16[192,256]{1,0:T(8,128)(2,1)}, bf16[192,256]{1,0:T(8,128)(2,1)}) custom-call(s32[2]{0:T(128)S(1)} %add_convert_fusion.edge_ref, f32[8,192]{1,0:T(8,128)S(1)} %get-tuple-element.58.owned_ref, f32[192,256]{1,0:T(8,128)S(1)} %get-tuple-element.59.kg_ref, ...), custom_call_target="tpu_custom_call" | custom-call | tf_op jit(solution)/shard_map/pallas_call | solution.py:368
  38.3 5.1 %all-to-all-done.2 = f32[32,1,64]{2,1,0:T(1,128)S(1)} async-done(((f32[32,1,64]{2,1,0:T(1,128)}), f32[32,1,64]{2,1,0:T(1,128)S(1)}, u32[]{:S(2)}, u32[]{:S(2)}) %all-to-all-start.2) | async-done | bytes 8224 | tf_op jit(solution)/shard_map/all_to_all | solution.py:367
  43.4 0.6 %reduce_sum.9 = f32[64]{0:T(128)} reduce(f32[32,1,64]{2,1,0:T(1,128)S(1)} %all-to-all-done.2, f32[]{:T(128)} %constant.11.clone.1), dimensions={0,1}, to_apply=%region_0.0 | reduce | flops 1984 | bytes 8452 | tf_op jit(solution)/shard_map/reduce_sum | solution.py:371
Async XLA Ops:
  2.5 11.4 %collective-permute-start = (bf16[192,384]{1,0:T(8,128)(2,1)S(1)}, bf16[192,384]{1,0:T(8,128)(2,1)S(1)}, u32[]{:S(2)}, u32[]{:S(2)}) collective-permute-start(bf16[192,384]{1,0:T(8,128)(2,1)S(1)} %get-tuple-element.41), channel_id=1, source_target_pairs={{0,2},{2,4},{4,6},{6,8},{8,10},{10,12},{12,14},{14,16},{16,18},{18... | collective-permute-start | bytes 442376 | tf_op jit(solution)/shard_map/ppermute | solution.py:334
  7.4 11.7 %all-to-all-start = ((bf16[16,8,192]{2,1,0:T(8,128)(2,1)}), bf16[16,8,192]{2,1,0:T(8,128)(2,1)S(1)}, u32[]{:S(2)}, u32[]{:S(2)}) async-start(bf16[16,8,192]{2,1,0:T(8,128)(2,1)} %get-tuple-element.45), calls=%async_computation | async-start | bytes 131072 | tf_op jit(solution)/shard_map/all_to_all | solution.py:336
  21.4 10.8 %all-to-all-start.1 = ((f32[16,8,192]{2,1,0:T(8,128)}), f32[16,8,192]{2,1,0:T(8,128)S(1)}, u32[]{:S(2)}, u32[]{:S(2)}) async-start(f32[16,8,192]{2,1,0:T(8,128)} %bitcast.8), calls=%async_computation.1 | async-start | bytes 262144 | tf_op jit(solution)/shard_map/all_to_all | solution.py:356
  28.1 8.2 %collective-permute-start.1 = (bf16[192,384]{1,0:T(8,128)(2,1)S(1)}, bf16[192,384]{1,0:T(8,128)(2,1)S(1)}, u32[]{:S(2)}, u32[]{:S(2)}) collective-permute-start(bf16[192,384]{1,0:T(8,128)(2,1)S(1)} %get-tuple-element.62), channel_id=1, source_target_pairs={{2,0},{4,2},{6,4},{8,6},{10,8},{12,10},{14,12},{16,14},{18,16},{20... | collective-permute-start | bytes 442376 | tf_op jit(solution)/shard_map/ppermute | solution.py:362
  33.0 10.3 %all-to-all-start.2 = ((f32[32,1,64]{2,1,0:T(1,128)}), f32[32,1,64]{2,1,0:T(1,128)S(1)}, u32[]{:S(2)}, u32[]{:S(2)}) async-start(f32[32,1,64]{2,1,0:T(1,128)} %bitcast.14), calls=%async_computation.2 | async-start | bytes 32768 | tf_op jit(solution)/shard_map/all_to_all | solution.py:367

commit v8 on v7

--- a/solution.py
+++ b/solution.py
@@ -134,27 +134,28 @@
 
 
 def local_kernel(
-    edge_ref, q_ref, k_ref, v_ref, g_ref, before_ref,
+    first_ref, q_ref, k_ref, v_ref, g_ref, before_ref,
     exp_ref, top_ref, total_ref, qx_ref, gx_ref, kx_ref, vx_ref, kt_ref, vt_ref,
 ):
     width, tok = q_ref.shape
-    lanes = width // HEAD_DIM * PAIR
-    pairs = tok // PAIR
     for at, t_ref, x_ref, own_ref in ((0, kt_ref, kx_ref, k_ref), (PAIR, vt_ref, vx_ref, v_ref)):
         t_ref[:, :PAIR] = before_ref[:, at : at + PAIR]
         t_ref[:, PAIR:] = own_ref[...]
         x_ref[:PAIR] = before_ref[:, at : at + PAIR].T
         x_ref[PAIR:] = own_ref[...].T
     for at, x_ref, own_ref in ((2 * PAIR, qx_ref, q_ref), (2 * PAIR + BLOCK, gx_ref, g_ref)):
-        nothing = jnp.zeros((width, BLOCK), BF16)
-        x_ref[...] = jnp.concatenate([before_ref[:, at : at + BLOCK], own_ref[...], nothing], axis=1)
-    second = second_half(lanes)
-    for p in range(pairs):
+        x_ref[...] = jnp.concatenate(
+            [before_ref[:, at : at + BLOCK], own_ref[:, : tok - BLOCK]], axis=1
+        )
+    second = second_half(width // HEAD_DIM * PAIR)
+    is_first = first_ref[0] == 1
+    for p in range(tok // PAIR):
         s = mm(kx_ref[p * PAIR : (p + 2) * PAIR], by_head(qx_ref[:, p * PAIR : (p + 1) * PAIR]))
         parts = [s[b * BLOCK : (b + 1) * BLOCK] for b in range(4)]
         parts[0] += jnp.where(second, LOW, 0.0)
         if p == 0:
-            parts[1] += jnp.where(edge_ref[0] == 1, LOW, 0.0)
+            parts[1] += jnp.where(jnp.logical_and(is_first, second), LOW, 0.0)
+            parts[2] += jnp.where(jnp.logical_and(is_first, jnp.logical_not(second)), LOW, 0.0)
         parts[3] += jnp.where(second, 0.0, LOW)
         s = jnp.concatenate(parts, axis=0)
         top = top_of(s)
@@ -163,27 +164,17 @@
         top_ref[p] = top
         total_ref[p] = total_of(s)
 
-    @pl.when(edge_ref[1] == 1)
-    def _():
-        s = mm(kx_ref[tok:], by_head(qx_ref[:, tok:]))
-        top = top_of(s)
-        s = jnp.exp(s - top)
-        exp_ref[pairs, :PAIR] = s
-        top_ref[pairs] = top
-        total_ref[pairs] = total_of(s)
-
 
 def global_kernel(
-    edge_ref, qx_ref, gx_ref, vt_ref, rows_ref, exp_ref, top_ref, total_ref,
+    qx_ref, gx_ref, vt_ref, rows_ref, exp_ref, top_ref, total_ref,
     att_ref, part_ref, ds_ref, factor_ref, delta_ref,
 ):
-    pairs = qx_ref.shape[1] // PAIR - 1
     rows = rows_ref[...]
     values_g = value_rows(rows)
-
-    def pair(p, keys):
+    values_gt = values_g.T
+    part = jnp.zeros(part_ref.shape, F32)
+    for p in range(qx_ref.shape[1] // PAIR):
         own = slice(p * PAIR, (p + 1) * PAIR)
-        near = slice(p * PAIR, p * PAIR + keys)
         g = gx_ref[:, own]
         qm, gm = by_head(qx_ref[:, own]), by_head(g)
         s = global_scores(rows, qm)
@@ -194,59 +185,48 @@
         inverse = 1.0 / (total_ref[p] * factor + total_of(s))
         factor = factor * inverse
         w = s * inverse
-        probs = (exp_ref[p, :keys] * factor).astype(BF16)
-        att = mm(vt_ref[:, near], probs) + mm_tn(values_g, w.astype(BF16))
+        probs = (exp_ref[p] * factor).astype(BF16)
+        att = mm(vt_ref[:, p * PAIR : (p + 2) * PAIR], probs) + mm(values_gt, w.astype(BF16))
         att = own_head(att).astype(BF16)
         att_ref[:, own] = att
         delta = head_sums(g.astype(F32) * att.astype(F32)) * SCALE
         ds = (w * (mm(values_g, gm) - delta)).astype(BF16)
+        part += mm_nt(ds, qm) + mm_nt(pltpu.roll(w, SUM_DEV, 0).astype(BF16), gm)
         ds_ref[p] = ds
         factor_ref[p] = factor
         delta_ref[p] = delta
-        part = mm_nt(ds, qm) + mm_nt(pltpu.roll(w, SUM_DEV, 0).astype(BF16), gm)
-        return part * (1.0 / SCALE)
-
-    part_ref[...] = sum(pair(p, 2 * PAIR) for p in range(pairs))
-
-    @pl.when(edge_ref[1] == 1)
-    def _():
-        part_ref[...] += pair(pairs, PAIR)
+    part_ref[...] = part * (1.0 / SCALE)
 
 
 def gradient_kernel(
-    edge_ref, qx_ref, gx_ref, kt_ref, vx_ref, rows_ref, exp_ref, att_ref, ds_ref, factor_ref, delta_ref,
+    qx_ref, gx_ref, kt_ref, vx_ref, rows_ref, exp_ref, att_ref, ds_ref, factor_ref, delta_ref,
     qg_ref, kg_ref, vg_ref, back_ref,
 ):
     width, tok = kg_ref.shape
-    pairs = qx_ref.shape[1] // PAIR - 1
-    rows = rows_ref[...]
-
-    def pair(p, keys):
+    pairs = tok // PAIR
+    rows_t = rows_ref[...].T
+
+    def pair(p):
         own = slice(p * PAIR, (p + 1) * PAIR)
-        near = slice(p * PAIR, p * PAIR + keys)
+        near = slice(p * PAIR, (p + 2) * PAIR)
         qm, gm = by_head(qx_ref[:, own]), by_head(gx_ref[:, own])
-        w = exp_ref[p, :keys] * factor_ref[p]
+        w = exp_ref[p] * factor_ref[p]
         ds = (w * (mm(vx_ref[near], gm) - delta_ref[p])).astype(BF16)
-        qg = own_head(mm(kt_ref[:, near], ds) + mm_tn(rows, ds_ref[p])).astype(BF16)
+        qg = own_head(mm(kt_ref[:, near], ds) + mm(rows_t, ds_ref[p])).astype(BF16)
         qg_ref[:, own] = qg
         kg = mm_nt(qm, ds) * (1.0 / SCALE)
         vg = mm_nt(gm, w.astype(BF16)) * (1.0 / SCALE)
         return qg, kg, vg
 
-    grads = [pair(p, 2 * PAIR) for p in range(pairs)]
-    edge = jnp.concatenate([att_ref[:, :BLOCK], grads[0][0][:, :BLOCK]], axis=1)
-    back_ref[:, 2 * PAIR :] = edge
+    grads = [pair(p) for p in range(pairs)]
+    back_ref[:, 2 * PAIR :] = jnp.concatenate(
+        [att_ref[:, :BLOCK], grads[0][0][:, :BLOCK]], axis=1
+    )
     for at, i, ref in ((0, 1, kg_ref), (PAIR, 2, vg_ref)):
         back_ref[:, at : at + PAIR] = grads[0][i][:, :PAIR].astype(BF16)
         for p in range(pairs - 1):
             ref[:, p * PAIR : (p + 1) * PAIR] = grads[p][i][:, PAIR:] + grads[p + 1][i][:, :PAIR]
         ref[:, tok - PAIR :] = grads[-1][i][:, PAIR:]
-
-    @pl.when(edge_ref[1] == 1)
-    def _():
-        _, kg, vg = pair(pairs, PAIR)
-        kg_ref[:, tok - PAIR :] += kg
-        vg_ref[:, tok - PAIR :] += vg
 
 
 def owned_kernel(parts_ref, k_ref, v_ref, owned_ref, term_ref):
@@ -268,7 +248,7 @@
 
 
 def finish_kernel(
-    edge_ref, owned_ref, kg_ref, vg_ref, w_ref, back_ref, attx_ref, qgx_ref,
+    owned_ref, kg_ref, vg_ref, w_ref, back_ref, attx_ref, qgx_ref,
     key_ref, value_ref, att_ref, qg_ref,
 ):
     tok = kg_ref.shape[1]
@@ -282,15 +262,9 @@
         out_ref[:, : tok - PAIR] = total[:, : tok - PAIR].astype(BF16)
         total = total[:, tok - PAIR :] + back_ref[:, at : at + PAIR].astype(F32)
         out_ref[:, tok - PAIR :] = total.astype(BF16)
-    last = edge_ref[1] == 1
     for at, x_ref, out_ref in ((0, attx_ref, att_ref), (BLOCK, qgx_ref, qg_ref)):
-        x = x_ref[:, BLOCK : tok + BLOCK]
-        out_ref[...] = x
         edge = back_ref[:, 2 * PAIR + at : 2 * PAIR + at + BLOCK]
-
-        @pl.when(jnp.logical_not(last))
-        def _():
-            out_ref[:, tok - BLOCK :] = edge
+        out_ref[...] = jnp.concatenate([x_ref[:, BLOCK:], edge], axis=1)
 
 
 def shaped(shape, dtype):
@@ -318,12 +292,19 @@
     halo = shaped((width, 3 * PAIR), BF16)
     own = shaped((width, tok), BF16)
     grad = shaped((width, tok), F32)
-    queries_x = shaped((width, tok + PAIR), BF16)
-    keys_x = shaped((tok + PAIR, width), BF16)
-    stat = shaped((pairs + 1, 1, lanes), F32)
+    keys = shaped((tok + PAIR, width), BF16)
+    keys_t = shaped((width, tok + PAIR), BF16)
+    stat = shaped((pairs, 1, lanes), F32)
+    up = [(i, (i + 1) % groups) for i in range(groups)]
+    down = [(j, i) for i, j in up]
+    order = [[(i + groups // 2) % groups for i in range(groups)]]
+
+    def exchange(x):
+        x = x.reshape(groups, n, width)
+        return lax.all_to_all(x, "seq", split_axis=0, concat_axis=0, axis_index_groups=order)
 
     arguments = (queries.T, key_states.T, value_states.T, out_grad.T, pool_weight.reshape(1, seg))
-    summary, up, q, k, v, g, weight_row = pl.pallas_call(
+    summary, edge, q, k, v, g, weight_row = pl.pallas_call(
         pool_kernel,
         out_shape=[shaped((groups, n, width), BF16), halo] + [own] * 4 + [shaped((1, seg), F32)],
         in_specs=[pl.BlockSpec(memory_space=pltpu.HBM)] * 5,
@@ -331,42 +312,33 @@
         scratch_shapes=[pltpu.SemaphoreType.DMA((5,))],
         compiler_params=PARAMS,
     )(*[pltpu.with_memory_space_constraint(x, pltpu.HBM) for x in arguments])
-    before = lax.ppermute(up, "seq", [(i, i + 1) for i in range(groups - 1)])
-    order = [[(i + groups // 2) % groups for i in range(groups)]]
-    rows = lax.all_to_all(
-        summary, "seq", split_axis=0, concat_axis=0, axis_index_groups=order
-    )
-    rows = rows.reshape(groups * n, width)
-    edge = jnp.stack([group_index == 0, group_index == groups - 1]).astype(jnp.int32)
+    before = lax.ppermute(edge, "seq", up)
+    rows = exchange(summary).reshape(groups * n, width)
+    is_first = (group_index == 0).astype(jnp.int32).reshape(1)
     exps, top, total, qx, gx, kx, vx, kt, vt = call(
         local_kernel,
-        [shaped((pairs + 1, 2 * PAIR, lanes), F32), stat, stat]
-        + [queries_x, queries_x, keys_x, keys_x, queries_x, queries_x],
+        [shaped((pairs, 2 * PAIR, lanes), F32), stat, stat, own, own, keys, keys, keys_t, keys_t],
         6,
         SMEM,
-    )(edge, q, k, v, g, before)
+    )(is_first, q, k, v, g, before)
 
     att_x, part, ds, factor, delta = call(
         global_kernel,
-        [queries_x, shaped((groups * n, width), F32)]
-        + [shaped((pairs + 1, groups * n, lanes), BF16), stat, stat],
-        8,
-        SMEM,
-    )(edge, qx, gx, vt, rows, exps, top, total)
-    parts = lax.all_to_all(
-        part.reshape(groups, n, width), "seq", split_axis=0, concat_axis=0, axis_index_groups=order
-    )
-    qg_x, key_part, value_part, down = call(gradient_kernel, [queries_x, grad, grad, halo], 11, SMEM)(
-        edge, qx, gx, kt, vx, rows, exps, att_x, ds, factor, delta
-    )
-    back = lax.ppermute(down, "seq", [(i + 1, i) for i in range(groups - 1)])
+        [own, shaped((groups * n, width), F32), shaped((pairs, groups * n, lanes), BF16), stat, stat],
+        7,
+    )(qx, gx, vt, rows, exps, top, total)
+    parts = exchange(part)
+    qg_x, key_part, value_part, edge = call(gradient_kernel, [own, grad, grad, halo], 10)(
+        qx, gx, kt, vx, rows, exps, att_x, ds, factor, delta
+    )
+    back = lax.ppermute(edge, "seq", down)
     parts, qg_x = lax.optimization_barrier((parts, qg_x))
     owned, term = call(owned_kernel, [shaped((n, width), F32), shaped((everyone, seg), F32)], 3)(
         parts, k, v
     )
     terms = lax.all_to_all(term, ("seq", "head"), split_axis=0, concat_axis=0)
-    key_grad, value_grad, attended, query_grad = call(finish_kernel, [own] * 4, 8, SMEM)(
-        edge, owned, key_part, value_part, weight_row, back, att_x, qg_x
+    key_grad, value_grad, attended, query_grad = call(finish_kernel, [own] * 4, 7)(
+        owned, key_part, value_part, weight_row, back, att_x, qg_x
     )
     return (attended.T, query_grad.T, key_grad.T, value_grad.T, terms.sum(0))
 

time: 44.3 us -> 41.7 us (0.941)
  Pallas kernels: 10.3 us -> 7.92 us
    pallas_call x4, Pallas kernels: 7.59 us -> 5.23 us  [the longest x1 1.89 us: local(): call(global_kernel, [own, shaped((groups * n, width), F32), shaped((pairs...]
    all_to_all x2, waiting for transfers between devices: 6.27 us -> 4 us  [exchange(): lax.all_to_all(x, 'seq', split_axis=0, concat_axis=0, axis_index_groups=o...]
    ppermute x2, waiting for transfers between devices: 0.01 us -> 1.43 us  [the longest x1 1.43 us: local(): before = lax.ppermute(edge, 'seq', up)]
    all_to_all x1, waiting for transfers between devices: 5.08 us -> 5.84 us  [local(): terms = lax.all_to_all(term, ('seq', 'head'), split_axis=0, concat_axis=0)]
  transfers between devices with their start and end apart: 5 -> 5, of which waited for: 3 -> 4; matrix products, arithmetic and copies ran while one was open for 0% -> 0% of each run, Pallas kernels for 14% -> 10%
where the time goes in v8:
time: 41.7 us; the launch traced here: 41.4 us
  starting transfers between devices  21 us (50%)
  waiting for transfers between devices  11.3 us (27%)
  Pallas kernels  7.92 us (19%)
  between operations  0.67 us (2%)
  other arithmetic  0.56 us (1%)
    all_to_all x2, starting transfers between devices, exchange(): lax.all_to_all(x, 'seq', split_axis=0, concat_axis=0, axis_index_groups=o...  11.3 us
    all_to_all x1, waiting for transfers between devices, local(): terms = lax.all_to_all(term, ('seq', 'head'), split_axis=0, concat_axis=0)  5.84 us
    all_to_all x2, waiting for transfers between devices, exchange(): lax.all_to_all(x, 'seq', split_axis=0, concat_axis=0, axis_index_groups=o...  4 us
    all_to_all x1, starting transfers between devices, local(): terms = lax.all_to_all(term, ('seq', 'head'), split_axis=0, concat_axis=0)  3.39 us
    ppermute x1, starting transfers between devices, local(): back = lax.ppermute(edge, 'seq', down)  3.31 us
    ppermute x1, starting transfers between devices, local(): before = lax.ppermute(edge, 'seq', up)  2.99 us
    pallas_call x1, Pallas kernels, local(): call(global_kernel, [own, shaped((groups * n, width), F32), shaped((pairs...  1.89 us
    pallas_call x1, Pallas kernels, local(): pl.pallas_call(pool_kernel, out_shape=[shaped((groups, n, width), BF16),...  1.85 us
  transfers between devices with their start and end apart: 5, of which 4 were waited for; matrix products, arithmetic and copies ran while one was open for 0% of the time, Pallas kernels for 10%

profile of v8, /device:TPU:0, one launch (start us, length us, event | category | flops | bytes accessed | tf_op | source)
XLA Modules:
  0.0 41.4 jit_solution(1222192917513269772)
XLA Ops:
  0.6 1.9 %shard_map.92 = (bf16[16,8,192]{2,1,0:T(8,128)(2,1)}, bf16[192,384]{1,0:T(8,128)(2,1)S(1)}, bf16[192,256]{1,0:T(8,128)(2,1)S(1)}, bf16[192,256]{1,0:T(8,128)(2,1...) custom-call(bf16[192,256]{1,0:T(8,128)(2,1)} %bitcast.17, ...), custom_call_target="tpu_custom_call" | custom-call | tf_op jit(solution)/shard_map/pallas_call | solution.py:307
  2.5 3.0 %collective-permute-start = (bf16[192,384]{1,0:T(8,128)(2,1)S(1)}, bf16[192,384]{1,0:T(8,128)(2,1)S(1)}, u32[]{:S(2)}, u32[]{:S(2)}) collective-permute-start(bf16[192,384]{1,0:T(8,128)(2,1)S(1)} %get-tuple-element.41), channel_id=1, source_target_pairs={{0,2},{2,4},{4,6},{6,8},{8,10},{10,12},{12,14},{14,16},{16,18},{18... | collective-permute-start | bytes 442376 | tf_op jit(solution)/shard_map/ppermute | solution.py:315
  5.5 6.4 %all-to-all-start = ((bf16[16,8,192]{2,1,0:T(8,128)(2,1)}), bf16[16,8,192]{2,1,0:T(8,128)(2,1)S(1)}, u32[]{:S(2)}, u32[]{:S(2)}) async-start(bf16[16,8,192]{2,1,0:T(8,128)(2,1)} %get-tuple-element.45), calls=%async_computation | async-start | bytes 131072 | tf_op jit(solution)/shard_map/all_to_all | solution.py:304
  11.9 1.4 %collective-permute-done.before_ref = bf16[192,384]{1,0:T(8,128)(2,1)S(1)} collective-permute-done((bf16[192,384]{1,0:T(8,128)(2,1)S(1)}, bf16[192,384]{1,0:T(8,128)(2,1)S(1)}, u32[]{:S(2)}, u32[]{:S(2)}) %collective-permute-start) | collective-permute-done | bytes 147488 | tf_op jit(solution)/shard_map/ppermute | solution.py:315
  13.3 1.1 %shard_map.93 = (f32[2,256,384]{2,1,0:T(8,128)S(1)}, f32[2,1,384]{2,1,0:T(1,128)S(1)}, f32[2,1,384]{2,1,0:T(1,128)S(1)}, bf16[192,256]{1,0:T(8,128)(2,1)S(1)}, b...) custom-call(s32[1]{0:T(128)} %bitcast.first_ref, ...), custom_call_target="tpu_custom_call" | custom-call | tf_op jit(solution)/shard_map/pallas_call | solution.py:318
  14.4 2.7 %all-to-all-done = bf16[16,8,192]{2,1,0:T(8,128)(2,1)S(1)} async-done(((bf16[16,8,192]{2,1,0:T(8,128)(2,1)}), bf16[16,8,192]{2,1,0:T(8,128)(2,1)S(1)}, u32[]{:S(2)}, u32[]{:S(2)}) %all-to-all-start) | async-done | bytes 49184 | tf_op jit(solution)/shard_map/all_to_all | solution.py:304
  17.2 1.9 %shard_map.94 = (bf16[192,256]{1,0:T(8,128)(2,1)S(1)}, f32[128,192]{1,0:T(8,128)}, bf16[2,128,384]{2,1,0:T(8,128)(2,1)S(1)}, f32[2,1,384]{2,1,0:T(1,128)S(1)}, f32[2,1,384]{2,1,0:T(1,128)S(1)}) custom-call(bf16[192,256]{1,0:T(8,128)(2,1)S(1)} %get-tuple-element.42.qx_ref, bf16[192,256]{1,0:T(8,128)(2,1)S(1)} %get-tuple-element.43.gx_ref, ...), custom_call_target="tpu_custom_call" | custom-call | tf_op jit(solution)/shard_map/pallas_call | solution.py:325
  19.1 4.9 %all-to-all-start.1 = ((f32[16,8,192]{2,1,0:T(8,128)}), f32[16,8,192]{2,1,0:T(8,128)S(1)}, u32[]{:S(2)}, u32[]{:S(2)}) async-start(f32[16,8,192]{2,1,0:T(8,128)} %bitcast.7), calls=%async_computation.1 | async-start | bytes 262144 | tf_op jit(solution)/shard_map/all_to_all | solution.py:304
  24.0 0.9 %shard_map.95 = (bf16[192,256]{1,0:T(8,128)(2,1)S(1)}, f32[192,256]{1,0:T(8,128)S(1)}, f32[192,256]{1,0:T(8,128)S(1)}, bf16[192,384]{1,0:T(8,128)(2,1)S(1)}) custom-call(bf16[192,256]{1,0:T(8,128)(2,1)S(1)} %get-tuple-element.42.qx_ref, bf16[192,256]{1,0:T(8,128)(2,1)S(1)} %get-tuple-element.43.gx_ref, bf16[192,384]{1,0:T(8,128)(2,1)S(1)} %get-tuple-element.50.kt_ref, ...), custom_call_target="tpu_custom_call" | custom-call | tf_op jit(solution)/shard_map/pallas_call | solution.py:331
  24.9 3.3 %collective-permute-start.1 = (bf16[192,384]{1,0:T(8,128)(2,1)S(1)}, bf16[192,384]{1,0:T(8,128)(2,1)S(1)}, u32[]{:S(2)}, u32[]{:S(2)}) collective-permute-start(bf16[192,384]{1,0:T(8,128)(2,1)S(1)} %get-tuple-element.62), channel_id=1, source_target_pairs={{2,0},{4,2},{6,4},{8,6},{10,8},{12,10},{14,12},{16,14},{18,16},{20... | collective-permute-start | bytes 442376 | tf_op jit(solution)/shard_map/ppermute | solution.py:334
  28.2 1.3 %all-to-all-done.1.parts_ref = f32[16,8,192]{2,1,0:T(8,128)S(1)} async-done(((f32[16,8,192]{2,1,0:T(8,128)}), f32[16,8,192]{2,1,0:T(8,128)S(1)}, u32[]{:S(2)}, u32[]{:S(2)}) %all-to-all-start.1) | async-done | bytes 98336 | tf_op jit(solution)/shard_map/all_to_all | solution.py:304
  29.5 0.8 %shard_map.96 = (f32[8,192]{1,0:T(8,128)S(1)}, f32[32,64]{1,0:T(8,128)}) custom-call(f32[16,8,192]{2,1,0:T(8,128)S(1)} %all-to-all-done.1.parts_ref, bf16[192,256]{1,0:T(8,128)(2,1)S(1)} %get-tuple-element.38.k_ref, bf16[192,256]{1,0:T(8,128)(2,1)S(1)} %get-tuple-element.39.v_ref), custom_call_target="tpu_custom_call" | custom-call | tf_op jit(solution)/shard_map/pallas_call | solution.py:336
  30.3 3.4 %all-to-all-start.2 = ((f32[32,1,64]{2,1,0:T(1,128)}), f32[32,1,64]{2,1,0:T(1,128)S(1)}, u32[]{:S(2)}, u32[]{:S(2)}) async-start(f32[32,1,64]{2,1,0:T(1,128)} %bitcast.13), calls=%async_computation.2 | async-start | bytes 32768 | tf_op jit(solution)/shard_map/all_to_all | solution.py:339
  33.7 0.0 collective-permute-done.1.back_ref
  33.7 1.3 %shard_map.97 = (bf16[192,256]{1,0:T(8,128)(2,1)}, bf16[192,256]{1,0:T(8,128)(2,1)}, bf16[192,256]{1,0:T(8,128)(2,1)}, bf16[192,256]{1,0:T(8,128)(2,1)}) custom-call(f32[8,192]{1,0:T(8,128)S(1)} %get-tuple-element.58.owned_ref, f32[192,256]{1,0:T(8,128)S(1)} %get-tuple-element.59.kg_ref, f32[192,256]{1,0:T(8,128)S(1)} %get-tuple-element.60.vg_ref, ...), custom_call_target="tpu_custom_call" | custom-call | tf_op jit(solution)/shard_map/pallas_call | solution.py:340
  35.0 5.8 %all-to-all-done.2 = f32[32,1,64]{2,1,0:T(1,128)S(1)} async-done(((f32[32,1,64]{2,1,0:T(1,128)}), f32[32,1,64]{2,1,0:T(1,128)S(1)}, u32[]{:S(2)}, u32[]{:S(2)}) %all-to-all-start.2) | async-done | bytes 8224 | tf_op jit(solution)/shard_map/all_to_all | solution.py:339
  40.9 0.6 %reduce_sum.9 = f32[64]{0:T(128)} reduce(f32[32,1,64]{2,1,0:T(1,128)S(1)} %all-to-all-done.2, f32[]{:T(128)} %constant.9.clone.1), dimensions={0,1}, to_apply=%region_0.0 | reduce | flops 1984 | bytes 8452 | tf_op jit(solution)/shard_map/reduce_sum | solution.py:343
Async XLA Ops:
  2.5 10.8 %collective-permute-start = (bf16[192,384]{1,0:T(8,128)(2,1)S(1)}, bf16[192,384]{1,0:T(8,128)(2,1)S(1)}, u32[]{:S(2)}, u32[]{:S(2)}) collective-permute-start(bf16[192,384]{1,0:T(8,128)(2,1)S(1)} %get-tuple-element.41), channel_id=1, source_target_pairs={{0,2},{2,4},{4,6},{6,8},{8,10},{10,12},{12,14},{14,16},{16,18},{18... | collective-permute-start | bytes 442376 | tf_op jit(solution)/shard_map/ppermute | solution.py:315
  5.5 11.7 %all-to-all-start = ((bf16[16,8,192]{2,1,0:T(8,128)(2,1)}), bf16[16,8,192]{2,1,0:T(8,128)(2,1)S(1)}, u32[]{:S(2)}, u32[]{:S(2)}) async-start(bf16[16,8,192]{2,1,0:T(8,128)(2,1)} %get-tuple-element.45), calls=%async_computation | async-start | bytes 131072 | tf_op jit(solution)/shard_map/all_to_all | solution.py:304
  19.1 10.4 %all-to-all-start.1 = ((f32[16,8,192]{2,1,0:T(8,128)}), f32[16,8,192]{2,1,0:T(8,128)S(1)}, u32[]{:S(2)}, u32[]{:S(2)}) async-start(f32[16,8,192]{2,1,0:T(8,128)} %bitcast.7), calls=%async_computation.1 | async-start | bytes 262144 | tf_op jit(solution)/shard_map/all_to_all | solution.py:304
  24.9 8.8 %collective-permute-start.1 = (bf16[192,384]{1,0:T(8,128)(2,1)S(1)}, bf16[192,384]{1,0:T(8,128)(2,1)S(1)}, u32[]{:S(2)}, u32[]{:S(2)}) collective-permute-start(bf16[192,384]{1,0:T(8,128)(2,1)S(1)} %get-tuple-element.62), channel_id=1, source_target_pairs={{2,0},{4,2},{6,4},{8,6},{10,8},{12,10},{14,12},{16,14},{18,16},{20... | collective-permute-start | bytes 442376 | tf_op jit(solution)/shard_map/ppermute | solution.py:334
  30.3 10.5 %all-to-all-start.2 = ((f32[32,1,64]{2,1,0:T(1,128)}), f32[32,1,64]{2,1,0:T(1,128)S(1)}, u32[]{:S(2)}, u32[]{:S(2)}) async-start(f32[32,1,64]{2,1,0:T(1,128)} %bitcast.13), calls=%async_computation.2 | async-start | bytes 32768 | tf_op jit(solution)/shard_map/all_to_all | solution.py:339

commit v9 on v8

--- a/solution.py
+++ b/solution.py
@@ -172,7 +172,8 @@
     rows = rows_ref[...]
     values_g = value_rows(rows)
     values_gt = values_g.T
-    part = jnp.zeros(part_ref.shape, F32)
+    part_k = jnp.zeros(part_ref.shape, F32)
+    part_v = jnp.zeros(part_ref.shape, F32)
     for p in range(qx_ref.shape[1] // PAIR):
         own = slice(p * PAIR, (p + 1) * PAIR)
         g = gx_ref[:, own]
@@ -185,22 +186,28 @@
         inverse = 1.0 / (total_ref[p] * factor + total_of(s))
         factor = factor * inverse
         w = s * inverse
+        wb = w.astype(BF16)
         probs = (exp_ref[p] * factor).astype(BF16)
-        att = mm(vt_ref[:, p * PAIR : (p + 2) * PAIR], probs) + mm(values_gt, w.astype(BF16))
-        att = own_head(att).astype(BF16)
+        near = slice(p * PAIR, (p + 2) * PAIR)
+        att = []
+        for h in range(qx_ref.shape[0] // HEAD_DIM):
+            f, c = slice(h * HEAD_DIM, (h + 1) * HEAD_DIM), slice(h * PAIR, (h + 1) * PAIR)
+            att.append(mm(vt_ref[f, near], probs[:, c]) + mm(values_gt[f], wb[:, c]))
+        att = jnp.concatenate(att, axis=0).astype(BF16)
         att_ref[:, own] = att
         delta = head_sums(g.astype(F32) * att.astype(F32)) * SCALE
         ds = (w * (mm(values_g, gm) - delta)).astype(BF16)
-        part += mm_nt(ds, qm) + mm_nt(pltpu.roll(w, SUM_DEV, 0).astype(BF16), gm)
+        part_k += mm_nt(ds, qm)
+        part_v += mm_nt(wb, gm)
         ds_ref[p] = ds
         factor_ref[p] = factor
         delta_ref[p] = delta
-    part_ref[...] = part * (1.0 / SCALE)
+    part_ref[...] = (part_k + pltpu.roll(part_v, SUM_DEV, 0)) * (1.0 / SCALE)
 
 
 def gradient_kernel(
     qx_ref, gx_ref, kt_ref, vx_ref, rows_ref, exp_ref, att_ref, ds_ref, factor_ref, delta_ref,
-    qg_ref, kg_ref, vg_ref, back_ref,
+    att_out_ref, qg_out_ref, kg_ref, vg_ref, back_ref,
 ):
     width, tok = kg_ref.shape
     pairs = tok // PAIR
@@ -213,15 +220,16 @@
         w = exp_ref[p] * factor_ref[p]
         ds = (w * (mm(vx_ref[near], gm) - delta_ref[p])).astype(BF16)
         qg = own_head(mm(kt_ref[:, near], ds) + mm(rows_t, ds_ref[p])).astype(BF16)
-        qg_ref[:, own] = qg
         kg = mm_nt(qm, ds) * (1.0 / SCALE)
         vg = mm_nt(gm, w.astype(BF16)) * (1.0 / SCALE)
         return qg, kg, vg
 
     grads = [pair(p) for p in range(pairs)]
-    back_ref[:, 2 * PAIR :] = jnp.concatenate(
-        [att_ref[:, :BLOCK], grads[0][0][:, :BLOCK]], axis=1
-    )
+    qg = jnp.concatenate([qg for qg, _, _ in grads], axis=1)
+    att = att_ref[...]
+    back_ref[:, 2 * PAIR :] = jnp.concatenate([att[:, :BLOCK], qg[:, :BLOCK]], axis=1)
+    for x, ref in ((att, att_out_ref), (qg, qg_out_ref)):
+        ref[...] = jnp.concatenate([x[:, BLOCK:], x[:, :BLOCK]], axis=1)
     for at, i, ref in ((0, 1, kg_ref), (PAIR, 2, vg_ref)):
         back_ref[:, at : at + PAIR] = grads[0][i][:, :PAIR].astype(BF16)
         for p in range(pairs - 1):
@@ -247,24 +255,53 @@
     term_ref[...] = jnp.broadcast_to(term, term_ref.shape)
 
 
+def sum_kernel(terms_ref, sum_ref):
+    sum_ref[...] = jnp.sum(terms_ref[...], axis=0, keepdims=True)
+
+
+def outer(rows, weights):
+    n = rows.shape[0]
+    a, b = pieces(rows), pieces(weights)
+    a = [a[i * n : (i + 1) * n] for i in (0, 0, 1, 0, 1, 2)]
+    b = [b[i * n : (i + 1) * n] for i in (0, 1, 0, 2, 1, 0)]
+    return mm_tn(jnp.concatenate(a, axis=0), jnp.concatenate(b, axis=0))
+
+
 def finish_kernel(
-    owned_ref, kg_ref, vg_ref, w_ref, back_ref, attx_ref, qgx_ref,
-    key_ref, value_ref, att_ref, qg_ref,
+    owned_ref, kg_ref, vg_ref, w_ref, back_ref, atts_ref, qgs_ref, pool_ref,
+    key_out, value_out, att_out, qg_out, pool_out, key_ref, value_ref, att_ref, qg_ref, sem,
 ):
+    copies = []
+
+    def send(ref, out):
+        copies.append(pltpu.make_async_copy(ref, out, sem.at[len(copies)]))
+        copies[-1].start()
+
     tok = kg_ref.shape[1]
-    columns = owned_ref[...].T
-    w = w_ref[...]
-    for first, at, grad_ref, out_ref in ((0, 0, kg_ref, key_ref), (SUM_DEV, PAIR, vg_ref, value_ref)):
-        pooled = jnp.concatenate(
-            [columns[:, first + j : first + j + 1] * w for j in range(SUM_DEV)], axis=1
-        )
-        total = grad_ref[...] + pooled
-        out_ref[:, : tok - PAIR] = total[:, : tok - PAIR].astype(BF16)
-        total = total[:, tok - PAIR :] + back_ref[:, at : at + PAIR].astype(F32)
-        out_ref[:, tok - PAIR :] = total.astype(BF16)
-    for at, x_ref, out_ref in ((0, attx_ref, att_ref), (BLOCK, qgx_ref, qg_ref)):
+    low, high = slice(0, tok - PAIR), slice(tok - PAIR, tok)
+    send(pool_ref, pool_out)
+    for at, x_ref, ref, out in (
+        (0, atts_ref, att_ref, att_out),
+        (BLOCK, qgs_ref, qg_ref, qg_out),
+    ):
+        send(x_ref.at[:, low], out.at[:, low])
         edge = back_ref[:, 2 * PAIR + at : 2 * PAIR + at + BLOCK]
-        out_ref[...] = jnp.concatenate([x_ref[:, BLOCK:], edge], axis=1)
+        ref[...] = jnp.concatenate([x_ref[:, tok - PAIR : tok - BLOCK], edge], axis=1)
+        send(ref, out.at[:, high])
+    owned = owned_ref[...]
+    w = jnp.concatenate([w_ref[...]] * SUM_DEV, axis=1)
+    w = jnp.broadcast_to(w, (owned.shape[0], tok))
+    for first, at, grad_ref, ref, out in (
+        (0, 0, kg_ref, key_ref, key_out),
+        (SUM_DEV, PAIR, vg_ref, value_ref, value_out),
+    ):
+        weights = jnp.where(segment_mask(first, w.shape[0], tok, w_ref.shape[1]), w, 0.0)
+        total = grad_ref[...] + outer(owned, weights)
+        ref[:, low] = total[:, low].astype(BF16)
+        ref[:, high] = (total[:, high] + back_ref[:, at : at + PAIR].astype(F32)).astype(BF16)
+        send(ref, out)
+    for copy in copies:
+        copy.wait()
 
 
 def shaped(shape, dtype):
@@ -297,7 +334,8 @@
     stat = shaped((pairs, 1, lanes), F32)
     up = [(i, (i + 1) % groups) for i in range(groups)]
     down = [(j, i) for i, j in up]
-    order = [[(i + groups // 2) % groups for i in range(groups)]]
+    quarter = groups // 4
+    order = [[part * quarter + i for part in (2, 3, 1, 0) for i in range(quarter)]]
 
     def exchange(x):
         x = x.reshape(groups, n, width)
@@ -328,19 +366,29 @@
         7,
     )(qx, gx, vt, rows, exps, top, total)
     parts = exchange(part)
-    qg_x, key_part, value_part, edge = call(gradient_kernel, [own, grad, grad, halo], 10)(
+    att_own, qg_own, key_part, value_part, edge = call(
+        gradient_kernel, [own, own, grad, grad, halo], 10
+    )(
         qx, gx, kt, vx, rows, exps, att_x, ds, factor, delta
     )
     back = lax.ppermute(edge, "seq", down)
-    parts, qg_x = lax.optimization_barrier((parts, qg_x))
+    parts, qg_own = lax.optimization_barrier((parts, qg_own))
     owned, term = call(owned_kernel, [shaped((n, width), F32), shaped((everyone, seg), F32)], 3)(
         parts, k, v
     )
     terms = lax.all_to_all(term, ("seq", "head"), split_axis=0, concat_axis=0)
-    key_grad, value_grad, attended, query_grad = call(finish_kernel, [own] * 4, 7)(
-        owned, key_part, value_part, weight_row, back, att_x, qg_x
-    )
-    return (attended.T, query_grad.T, key_grad.T, value_grad.T, terms.sum(0))
+    (pool_sum,) = call(sum_kernel, [shaped((1, seg), F32)], 1)(terms)
+    key_grad, value_grad, attended, query_grad, pool_grad = pl.pallas_call(
+        finish_kernel,
+        out_shape=[own] * 4 + [shaped((1, seg), F32)],
+        in_specs=[VMEM] * 8,
+        out_specs=[pl.BlockSpec(memory_space=pltpu.HBM)] * 5,
+        scratch_shapes=[pltpu.VMEM((width, tok), BF16)] * 2
+        + [pltpu.VMEM((width, PAIR), BF16)] * 2
+        + [pltpu.SemaphoreType.DMA((7,))],
+        compiler_params=PARAMS,
+    )(owned, key_part, value_part, weight_row, back, att_own, qg_own, pool_sum)
+    return (attended.T, query_grad.T, key_grad.T, value_grad.T, pool_grad.reshape(seg))
 
 
 def solution(mesh):

time: 41.7 us -> 41 us (0.983)
  blocking collectives: 0 us -> 9.9 us
  waiting for transfers between devices: 11.3 us -> 5.79 us
  starting transfers between devices: 21 us -> 17.4 us
  Pallas kernels: 7.92 us -> 6.92 us
  other arithmetic: 0.56 us -> 0 us
    all_to_all x0 -> x1, blocking collectives: none -> 9.9 us  [local(): terms = lax.all_to_all(term, ('seq', 'head'), split_axis=0, concat_axis=0)]
    all_to_all x1 -> x0, waiting for transfers between devices: 5.84 us -> none  [local(): terms = lax.all_to_all(term, ('seq', 'head'), split_axis=0, concat_axis=0)]
    all_to_all x1 -> x0, starting transfers between devices: 3.39 us -> none  [local(): terms = lax.all_to_all(term, ('seq', 'head'), split_axis=0, concat_axis=0)]
    pallas_call x1, Pallas kernels: 0.84 us -> 0.23 us  [local(): call(owned_kernel, [shaped((n, width), F32), shaped((everyone, seg), F32)...]
    reduce_sum x1 -> x0, other arithmetic: 0.56 us -> none  [local(): return (attended.T, query_grad.T, key_grad.T, value_grad.T, terms.sum(0))]
    pallas_call x2 -> x3, Pallas kernels: 2.24 us -> 1.95 us  [the longest x1 1 us: local(): pl.pallas_call(finish_kernel, out_shape=[own] * 4 + [shaped((1, seg), F32...]
  transfers between devices with their start and end apart: 5 -> 4, of which waited for: 4 -> 3; matrix products, arithmetic and copies ran while one was open for 0% -> 0% of each run, Pallas kernels for 10% -> 6%
where the time goes in v9:
time: 41 us; the launch traced here: 40.7 us
  starting transfers between devices  17.4 us (42%)
  blocking collectives  9.9 us (24%)
  Pallas kernels  6.92 us (17%)
  waiting for transfers between devices  5.79 us (14%)
  between operations  0.66 us (2%)
    all_to_all x2, starting transfers between devices, exchange(): lax.all_to_all(x, 'seq', split_axis=0, concat_axis=0, axis_index_groups=o...  11.2 us
    all_to_all x1, blocking collectives, local(): terms = lax.all_to_all(term, ('seq', 'head'), split_axis=0, concat_axis=0)  9.9 us
    all_to_all x2, waiting for transfers between devices, exchange(): lax.all_to_all(x, 'seq', split_axis=0, concat_axis=0, axis_index_groups=o...  4.36 us
    ppermute x1, starting transfers between devices, local(): back = lax.ppermute(edge, 'seq', down)  3.28 us
    ppermute x1, starting transfers between devices, local(): before = lax.ppermute(edge, 'seq', up)  2.99 us
    pallas_call x1, Pallas kernels, local(): pl.pallas_call(pool_kernel, out_shape=[shaped((groups, n, width), BF16),...  1.85 us
    pallas_call x1, Pallas kernels, local(): call(global_kernel, [own, shaped((groups * n, width), F32), shaped((pairs...  1.78 us
    ppermute x1, waiting for transfers between devices, local(): before = lax.ppermute(edge, 'seq', up)  1.43 us
  transfers between devices with their start and end apart: 4, of which 3 were waited for; matrix products, arithmetic and copies ran while one was open for 0% of the time, Pallas kernels for 6%

profile of v9, /device:TPU:0, one launch (start us, length us, event | category | flops | bytes accessed | tf_op | source)
XLA Modules:
  0.0 40.7 jit_solution(7759661538055427481)
XLA Ops:
  0.6 1.9 %shard_map.92 = (bf16[16,8,192]{2,1,0:T(8,128)(2,1)}, bf16[192,384]{1,0:T(8,128)(2,1)S(1)}, bf16[192,256]{1,0:T(8,128)(2,1)S(1)}, bf16[192,256]{1,0:T(8,128)(2,1...) custom-call(bf16[192,256]{1,0:T(8,128)(2,1)} %bitcast.21, ...), custom_call_target="tpu_custom_call" | custom-call | tf_op jit(solution)/shard_map/pallas_call | solution.py:345
  2.5 3.0 %collective-permute-start = (bf16[192,384]{1,0:T(8,128)(2,1)S(1)}, bf16[192,384]{1,0:T(8,128)(2,1)S(1)}, u32[]{:S(2)}, u32[]{:S(2)}) collective-permute-start(bf16[192,384]{1,0:T(8,128)(2,1)S(1)} %get-tuple-element.43), channel_id=1, source_target_pairs={{0,2},{2,4},{4,6},{6,8},{8,10},{10,12},{12,14},{14,16},{16,18},{18... | collective-permute-start | bytes 442376 | tf_op jit(solution)/shard_map/ppermute | solution.py:353
  5.5 6.4 %all-to-all-start = ((bf16[16,8,192]{2,1,0:T(8,128)(2,1)}), bf16[16,8,192]{2,1,0:T(8,128)(2,1)S(1)}, u32[]{:S(2)}, u32[]{:S(2)}) async-start(bf16[16,8,192]{2,1,0:T(8,128)(2,1)} %get-tuple-element.47), calls=%async_computation | async-start | bytes 131072 | tf_op jit(solution)/shard_map/all_to_all | solution.py:342
  11.9 1.4 %collective-permute-done.before_ref = bf16[192,384]{1,0:T(8,128)(2,1)S(1)} collective-permute-done((bf16[192,384]{1,0:T(8,128)(2,1)S(1)}, bf16[192,384]{1,0:T(8,128)(2,1)S(1)}, u32[]{:S(2)}, u32[]{:S(2)}) %collective-permute-start) | collective-permute-done | bytes 147488 | tf_op jit(solution)/shard_map/ppermute | solution.py:353
  13.3 1.1 %shard_map.93 = (f32[2,256,384]{2,1,0:T(8,128)S(1)}, f32[2,1,384]{2,1,0:T(1,128)S(1)}, f32[2,1,384]{2,1,0:T(1,128)S(1)}, bf16[192,256]{1,0:T(8,128)(2,1)S(1)}, b...) custom-call(s32[1]{0:T(128)} %bitcast.first_ref, ...), custom_call_target="tpu_custom_call" | custom-call | tf_op jit(solution)/shard_map/pallas_call | solution.py:356
  14.4 2.8 %all-to-all-done = bf16[16,8,192]{2,1,0:T(8,128)(2,1)S(1)} async-done(((bf16[16,8,192]{2,1,0:T(8,128)(2,1)}), bf16[16,8,192]{2,1,0:T(8,128)(2,1)S(1)}, u32[]{:S(2)}, u32[]{:S(2)}) %all-to-all-start) | async-done | bytes 49184 | tf_op jit(solution)/shard_map/all_to_all | solution.py:342
  17.3 1.8 %shard_map.94 = (bf16[192,256]{1,0:T(8,128)(2,1)S(1)}, f32[128,192]{1,0:T(8,128)}, bf16[2,128,384]{2,1,0:T(8,128)(2,1)S(1)}, f32[2,1,384]{2,1,0:T(1,128)S(1)}, f32[2,1,384]{2,1,0:T(1,128)S(1)}) custom-call(bf16[192,256]{1,0:T(8,128)(2,1)S(1)} %get-tuple-element.44.qx_ref, bf16[192,256]{1,0:T(8,128)(2,1)S(1)} %get-tuple-element.45.gx_ref, ...), custom_call_target="tpu_custom_call" | custom-call | tf_op jit(solution)/shard_map/pallas_call | solution.py:363
  19.0 4.8 %all-to-all-start.1 = ((f32[16,8,192]{2,1,0:T(8,128)}), f32[16,8,192]{2,1,0:T(8,128)S(1)}, u32[]{:S(2)}, u32[]{:S(2)}) async-start(f32[16,8,192]{2,1,0:T(8,128)} %bitcast.7), calls=%async_computation.1 | async-start | bytes 262144 | tf_op jit(solution)/shard_map/all_to_all | solution.py:342
  23.8 0.9 %shard_map.95 = (bf16[192,256]{1,0:T(8,128)(2,1)S(1)}, bf16[192,256]{1,0:T(8,128)(2,1)S(1)}, f32[192,256]{1,0:T(8,128)S(1)}, f32[192,256]{1,0:T(8,128)S(1)}, bf16[192,384]{1,0:T(8,128)(2,1)S(1)}) custom-call(bf16[192,256]{1,0:T(8,128)(2,1)S(1)} %get-tuple-element.44.qx_ref, bf16[192,256]{1,0:T(8,128)(2,1)S(1)} %get-tuple-element.45.gx_ref, ...), custom_call_target="tpu_custom_call" | custom-call | tf_op jit(solution)/shard_map/pallas_call | solution.py:369
  24.7 3.3 %collective-permute-start.1 = (bf16[192,384]{1,0:T(8,128)(2,1)S(1)}, bf16[192,384]{1,0:T(8,128)(2,1)S(1)}, u32[]{:S(2)}, u32[]{:S(2)}) collective-permute-start(bf16[192,384]{1,0:T(8,128)(2,1)S(1)} %get-tuple-element.64), channel_id=1, source_target_pairs={{2,0},{4,2},{6,4},{8,6},{10,8},{12,10},{14,12},{16,14},{18,16},{20... | collective-permute-start | bytes 442376 | tf_op jit(solution)/shard_map/ppermute | solution.py:374
  28.0 1.5 %all-to-all-done.1.parts_ref = f32[16,8,192]{2,1,0:T(8,128)S(1)} async-done(((f32[16,8,192]{2,1,0:T(8,128)}), f32[16,8,192]{2,1,0:T(8,128)S(1)}, u32[]{:S(2)}, u32[]{:S(2)}) %all-to-all-start.1) | async-done | bytes 98336 | tf_op jit(solution)/shard_map/all_to_all | solution.py:342
  29.6 0.2 shard_map.96
  29.8 9.9 %all_to_all.21 = f32[32,1,64]{2,1,0:T(1,128)S(1)} all-to-all(f32[32,1,64]{2,1,0:T(1,128)S(1)} %bitcast.20), channel_id=1, replica_groups=mesh['seq'=16,'head'=2] {'seq','head'}, dimensions={0} | all-to-all | bytes 16384 | tf_op jit(solution)/shard_map/all_to_all | solution.py:379
  39.7 0.0 collective-permute-done.1.back_ref
  39.7 1.0 %shard_map.98 = (bf16[192,256]{1,0:T(8,128)(2,1)}, bf16[192,256]{1,0:T(8,128)(2,1)}, bf16[192,256]{1,0:T(8,128)(2,1)}, bf16[192,256]{1,0:T(8,128)(2,1)}, f32[1,64]{1,0:T(1,128)}) custom-call(f32[8,192]{1,0:T(8,128)S(1)} %get-tuple-element.60.owned_ref, f32[192,256]{1,0:T(8,128)S(1)} %get-tuple-element.61.kg_ref, f32[192,256]{1,0:T(8,128)S(1)} %get-tuple-element.62.vg_ref, ...), custom_call_target="tpu_custom_call" | custom-call | tf_op jit(solution)/shard_map/pallas_call | solution.py:381
  (1 shorter events, 0.0 us)
Async XLA Ops:
  2.5 10.8 %collective-permute-start = (bf16[192,384]{1,0:T(8,128)(2,1)S(1)}, bf16[192,384]{1,0:T(8,128)(2,1)S(1)}, u32[]{:S(2)}, u32[]{:S(2)}) collective-permute-start(bf16[192,384]{1,0:T(8,128)(2,1)S(1)} %get-tuple-element.43), channel_id=1, source_target_pairs={{0,2},{2,4},{4,6},{6,8},{8,10},{10,12},{12,14},{14,16},{16,18},{18... | collective-permute-start | bytes 442376 | tf_op jit(solution)/shard_map/ppermute | solution.py:353
  5.5 11.8 %all-to-all-start = ((bf16[16,8,192]{2,1,0:T(8,128)(2,1)}), bf16[16,8,192]{2,1,0:T(8,128)(2,1)S(1)}, u32[]{:S(2)}, u32[]{:S(2)}) async-start(bf16[16,8,192]{2,1,0:T(8,128)(2,1)} %get-tuple-element.47), calls=%async_computation | async-start | bytes 131072 | tf_op jit(solution)/shard_map/all_to_all | solution.py:342
  19.0 10.5 %all-to-all-start.1 = ((f32[16,8,192]{2,1,0:T(8,128)}), f32[16,8,192]{2,1,0:T(8,128)S(1)}, u32[]{:S(2)}, u32[]{:S(2)}) async-start(f32[16,8,192]{2,1,0:T(8,128)} %bitcast.7), calls=%async_computation.1 | async-start | bytes 262144 | tf_op jit(solution)/shard_map/all_to_all | solution.py:342
  24.7 15.0 %collective-permute-start.1 = (bf16[192,384]{1,0:T(8,128)(2,1)S(1)}, bf16[192,384]{1,0:T(8,128)(2,1)S(1)}, u32[]{:S(2)}, u32[]{:S(2)}) collective-permute-start(bf16[192,384]{1,0:T(8,128)(2,1)S(1)} %get-tuple-element.64), channel_id=1, source_target_pairs={{2,0},{4,2},{6,4},{8,6},{10,8},{12,10},{14,12},{16,14},{18,16},{20... | collective-permute-start | bytes 442376 | tf_op jit(solution)/shard_map/ppermute | solution.py:374

commit v10 on v9

--- a/solution.py
+++ b/solution.py
@@ -334,8 +334,8 @@
     stat = shaped((pairs, 1, lanes), F32)
     up = [(i, (i + 1) % groups) for i in range(groups)]
     down = [(j, i) for i, j in up]
-    quarter = groups // 4
-    order = [[part * quarter + i for part in (2, 3, 1, 0) for i in range(quarter)]]
+    half = groups // 2
+    order = [[*range(half, groups), *range(half)[::-1]]]
 
     def exchange(x):
         x = x.reshape(groups, n, width)

time: 41 us -> 40.7 us (level)
  waiting for transfers between devices: 5.79 us -> 5.03 us
    all_to_all x2, waiting for transfers between devices: 4.36 us -> 3.6 us  [exchange(): lax.all_to_all(x, 'seq', split_axis=0, concat_axis=0, axis_index_groups=o...]
    all_to_all x1, blocking collectives: 9.9 us -> 10.3 us  [local(): terms = lax.all_to_all(term, ('seq', 'head'), split_axis=0, concat_axis=0)]
where the time goes in v10:
time: 40.7 us; the launch traced here: 40.4 us
  starting transfers between devices  17.4 us (43%)
  blocking collectives  10.3 us (25%)
  Pallas kernels  6.92 us (17%)
  waiting for transfers between devices  5.03 us (12%)
  between operations  0.66 us (2%)
    all_to_all x2, starting transfers between devices, exchange(): lax.all_to_all(x, 'seq', split_axis=0, concat_axis=0, axis_index_groups=o...  11.2 us
    all_to_all x1, blocking collectives, local(): terms = lax.all_to_all(term, ('seq', 'head'), split_axis=0, concat_axis=0)  10.3 us
    all_to_all x2, waiting for transfers between devices, exchange(): lax.all_to_all(x, 'seq', split_axis=0, concat_axis=0, axis_index_groups=o...  3.6 us
    ppermute x1, starting transfers between devices, local(): back = lax.ppermute(edge, 'seq', down)  3.26 us
    ppermute x1, starting transfers between devices, local(): before = lax.ppermute(edge, 'seq', up)  2.99 us
    pallas_call x1, Pallas kernels, local(): pl.pallas_call(pool_kernel, out_shape=[shaped((groups, n, width), BF16),...  1.85 us
    pallas_call x1, Pallas kernels, local(): call(global_kernel, [own, shaped((groups * n, width), F32), shaped((pairs...  1.78 us
    ppermute x1, waiting for transfers between devices, local(): before = lax.ppermute(edge, 'seq', up)  1.42 us
  transfers between devices with their start and end apart: 4, of which 3 were waited for; matrix products, arithmetic and copies ran while one was open for 0% of the time, Pallas kernels for 6%

profile of v10, /device:TPU:0, one launch (start us, length us, event | category | flops | bytes accessed | tf_op | source)
XLA Modules:
  0.0 40.4 jit_solution(684791410762468966)
XLA Ops:
  0.6 1.9 %shard_map.92 = (bf16[16,8,192]{2,1,0:T(8,128)(2,1)}, bf16[192,384]{1,0:T(8,128)(2,1)S(1)}, bf16[192,256]{1,0:T(8,128)(2,1)S(1)}, bf16[192,256]{1,0:T(8,128)(2,1...) custom-call(bf16[192,256]{1,0:T(8,128)(2,1)} %bitcast.21, ...), custom_call_target="tpu_custom_call" | custom-call | tf_op jit(solution)/shard_map/pallas_call | solution.py:345
  2.5 3.0 %collective-permute-start = (bf16[192,384]{1,0:T(8,128)(2,1)S(1)}, bf16[192,384]{1,0:T(8,128)(2,1)S(1)}, u32[]{:S(2)}, u32[]{:S(2)}) collective-permute-start(bf16[192,384]{1,0:T(8,128)(2,1)S(1)} %get-tuple-element.43), channel_id=1, source_target_pairs={{0,2},{2,4},{4,6},{6,8},{8,10},{10,12},{12,14},{14,16},{16,18},{18... | collective-permute-start | bytes 442376 | tf_op jit(solution)/shard_map/ppermute | solution.py:353
  5.5 6.4 %all-to-all-start = ((bf16[16,8,192]{2,1,0:T(8,128)(2,1)}), bf16[16,8,192]{2,1,0:T(8,128)(2,1)S(1)}, u32[]{:S(2)}, u32[]{:S(2)}) async-start(bf16[16,8,192]{2,1,0:T(8,128)(2,1)} %get-tuple-element.47), calls=%async_computation | async-start | bytes 131072 | tf_op jit(solution)/shard_map/all_to_all | solution.py:342
  11.9 1.4 %collective-permute-done.before_ref = bf16[192,384]{1,0:T(8,128)(2,1)S(1)} collective-permute-done((bf16[192,384]{1,0:T(8,128)(2,1)S(1)}, bf16[192,384]{1,0:T(8,128)(2,1)S(1)}, u32[]{:S(2)}, u32[]{:S(2)}) %collective-permute-start) | collective-permute-done | bytes 147488 | tf_op jit(solution)/shard_map/ppermute | solution.py:353
  13.3 1.1 %shard_map.93 = (f32[2,256,384]{2,1,0:T(8,128)S(1)}, f32[2,1,384]{2,1,0:T(1,128)S(1)}, f32[2,1,384]{2,1,0:T(1,128)S(1)}, bf16[192,256]{1,0:T(8,128)(2,1)S(1)}, b...) custom-call(s32[1]{0:T(128)} %bitcast.first_ref, ...), custom_call_target="tpu_custom_call" | custom-call | tf_op jit(solution)/shard_map/pallas_call | solution.py:356
  14.4 2.6 %all-to-all-done = bf16[16,8,192]{2,1,0:T(8,128)(2,1)S(1)} async-done(((bf16[16,8,192]{2,1,0:T(8,128)(2,1)}), bf16[16,8,192]{2,1,0:T(8,128)(2,1)S(1)}, u32[]{:S(2)}, u32[]{:S(2)}) %all-to-all-start) | async-done | bytes 49184 | tf_op jit(solution)/shard_map/all_to_all | solution.py:342
  17.0 1.8 %shard_map.94 = (bf16[192,256]{1,0:T(8,128)(2,1)S(1)}, f32[128,192]{1,0:T(8,128)}, bf16[2,128,384]{2,1,0:T(8,128)(2,1)S(1)}, f32[2,1,384]{2,1,0:T(1,128)S(1)}, f32[2,1,384]{2,1,0:T(1,128)S(1)}) custom-call(bf16[192,256]{1,0:T(8,128)(2,1)S(1)} %get-tuple-element.44.qx_ref, bf16[192,256]{1,0:T(8,128)(2,1)S(1)} %get-tuple-element.45.gx_ref, ...), custom_call_target="tpu_custom_call" | custom-call | tf_op jit(solution)/shard_map/pallas_call | solution.py:363
  18.8 4.8 %all-to-all-start.1 = ((f32[16,8,192]{2,1,0:T(8,128)}), f32[16,8,192]{2,1,0:T(8,128)S(1)}, u32[]{:S(2)}, u32[]{:S(2)}) async-start(f32[16,8,192]{2,1,0:T(8,128)} %bitcast.7), calls=%async_computation.1 | async-start | bytes 262144 | tf_op jit(solution)/shard_map/all_to_all | solution.py:342
  23.6 0.9 %shard_map.95 = (bf16[192,256]{1,0:T(8,128)(2,1)S(1)}, bf16[192,256]{1,0:T(8,128)(2,1)S(1)}, f32[192,256]{1,0:T(8,128)S(1)}, f32[192,256]{1,0:T(8,128)S(1)}, bf16[192,384]{1,0:T(8,128)(2,1)S(1)}) custom-call(bf16[192,256]{1,0:T(8,128)(2,1)S(1)} %get-tuple-element.44.qx_ref, bf16[192,256]{1,0:T(8,128)(2,1)S(1)} %get-tuple-element.45.gx_ref, ...), custom_call_target="tpu_custom_call" | custom-call | tf_op jit(solution)/shard_map/pallas_call | solution.py:369
  24.5 3.3 %collective-permute-start.1 = (bf16[192,384]{1,0:T(8,128)(2,1)S(1)}, bf16[192,384]{1,0:T(8,128)(2,1)S(1)}, u32[]{:S(2)}, u32[]{:S(2)}) collective-permute-start(bf16[192,384]{1,0:T(8,128)(2,1)S(1)} %get-tuple-element.64), channel_id=1, source_target_pairs={{2,0},{4,2},{6,4},{8,6},{10,8},{12,10},{14,12},{16,14},{18,16},{20... | collective-permute-start | bytes 442376 | tf_op jit(solution)/shard_map/ppermute | solution.py:374
  27.8 1.0 %all-to-all-done.1.parts_ref = f32[16,8,192]{2,1,0:T(8,128)S(1)} async-done(((f32[16,8,192]{2,1,0:T(8,128)}), f32[16,8,192]{2,1,0:T(8,128)S(1)}, u32[]{:S(2)}, u32[]{:S(2)}) %all-to-all-start.1) | async-done | bytes 98336 | tf_op jit(solution)/shard_map/all_to_all | solution.py:342
  28.8 0.2 shard_map.96
  29.0 10.3 %all_to_all.21 = f32[32,1,64]{2,1,0:T(1,128)S(1)} all-to-all(f32[32,1,64]{2,1,0:T(1,128)S(1)} %bitcast.20), channel_id=1, replica_groups=mesh['seq'=16,'head'=2] {'seq','head'}, dimensions={0} | all-to-all | bytes 16384 | tf_op jit(solution)/shard_map/all_to_all | solution.py:379
  39.4 0.0 collective-permute-done.1.back_ref
  39.4 1.0 %shard_map.98 = (bf16[192,256]{1,0:T(8,128)(2,1)}, bf16[192,256]{1,0:T(8,128)(2,1)}, bf16[192,256]{1,0:T(8,128)(2,1)}, bf16[192,256]{1,0:T(8,128)(2,1)}, f32[1,64]{1,0:T(1,128)}) custom-call(f32[8,192]{1,0:T(8,128)S(1)} %get-tuple-element.60.owned_ref, f32[192,256]{1,0:T(8,128)S(1)} %get-tuple-element.61.kg_ref, f32[192,256]{1,0:T(8,128)S(1)} %get-tuple-element.62.vg_ref, ...), custom_call_target="tpu_custom_call" | custom-call | tf_op jit(solution)/shard_map/pallas_call | solution.py:381
  (1 shorter events, 0.0 us)
Async XLA Ops:
  2.5 10.8 %collective-permute-start = (bf16[192,384]{1,0:T(8,128)(2,1)S(1)}, bf16[192,384]{1,0:T(8,128)(2,1)S(1)}, u32[]{:S(2)}, u32[]{:S(2)}) collective-permute-start(bf16[192,384]{1,0:T(8,128)(2,1)S(1)} %get-tuple-element.43), channel_id=1, source_target_pairs={{0,2},{2,4},{4,6},{6,8},{8,10},{10,12},{12,14},{14,16},{16,18},{18... | collective-permute-start | bytes 442376 | tf_op jit(solution)/shard_map/ppermute | solution.py:353
  5.5 11.5 %all-to-all-start = ((bf16[16,8,192]{2,1,0:T(8,128)(2,1)}), bf16[16,8,192]{2,1,0:T(8,128)(2,1)S(1)}, u32[]{:S(2)}, u32[]{:S(2)}) async-start(bf16[16,8,192]{2,1,0:T(8,128)(2,1)} %get-tuple-element.47), calls=%async_computation | async-start | bytes 131072 | tf_op jit(solution)/shard_map/all_to_all | solution.py:342
  18.8 10.0 %all-to-all-start.1 = ((f32[16,8,192]{2,1,0:T(8,128)}), f32[16,8,192]{2,1,0:T(8,128)S(1)}, u32[]{:S(2)}, u32[]{:S(2)}) async-start(f32[16,8,192]{2,1,0:T(8,128)} %bitcast.7), calls=%async_computation.1 | async-start | bytes 262144 | tf_op jit(solution)/shard_map/all_to_all | solution.py:342
  24.5 14.8 %collective-permute-start.1 = (bf16[192,384]{1,0:T(8,128)(2,1)S(1)}, bf16[192,384]{1,0:T(8,128)(2,1)S(1)}, u32[]{:S(2)}, u32[]{:S(2)}) collective-permute-start(bf16[192,384]{1,0:T(8,128)(2,1)S(1)} %get-tuple-element.64), channel_id=1, source_target_pairs={{2,0},{4,2},{6,4},{8,6},{10,8},{12,10},{14,12},{16,14},{18,16},{20... | collective-permute-start | bytes 442376 | tf_op jit(solution)/shard_map/ppermute | solution.py:374

commit v11 on v10

--- a/solution.py
+++ b/solution.py
@@ -170,39 +170,52 @@
     att_ref, part_ref, ds_ref, factor_ref, delta_ref,
 ):
     rows = rows_ref[...]
+    width = qx_ref.shape[0]
+    pairs = range(qx_ref.shape[1] // PAIR)
+    own = [slice(p * PAIR, (p + 1) * PAIR) for p in pairs]
+    qm = [by_head(qx_ref[:, own[p]]) for p in pairs]
+    s = global_scores(rows, jnp.concatenate(qm, axis=1))
+    lanes = qm[0].shape[1]
+    s = [s[:, p * lanes : (p + 1) * lanes] for p in pairs]
     values_g = value_rows(rows)
     values_gt = values_g.T
-    part_k = jnp.zeros(part_ref.shape, F32)
-    part_v = jnp.zeros(part_ref.shape, F32)
-    for p in range(qx_ref.shape[1] // PAIR):
-        own = slice(p * PAIR, (p + 1) * PAIR)
-        g = gx_ref[:, own]
-        qm, gm = by_head(qx_ref[:, own]), by_head(g)
-        s = global_scores(rows, qm)
-        local_top = top_ref[p]
-        top = jnp.maximum(local_top, top_of(s))
-        s = jnp.exp(s - top)
-        factor = jnp.exp(local_top - top)
-        inverse = 1.0 / (total_ref[p] * factor + total_of(s))
-        factor = factor * inverse
-        w = s * inverse
-        wb = w.astype(BF16)
-        probs = (exp_ref[p] * factor).astype(BF16)
-        near = slice(p * PAIR, (p + 2) * PAIR)
-        att = []
-        for h in range(qx_ref.shape[0] // HEAD_DIM):
-            f, c = slice(h * HEAD_DIM, (h + 1) * HEAD_DIM), slice(h * PAIR, (h + 1) * PAIR)
-            att.append(mm(vt_ref[f, near], probs[:, c]) + mm(values_gt[f], wb[:, c]))
-        att = jnp.concatenate(att, axis=0).astype(BF16)
-        att_ref[:, own] = att
-        delta = head_sums(g.astype(F32) * att.astype(F32)) * SCALE
-        ds = (w * (mm(values_g, gm) - delta)).astype(BF16)
-        part_k += mm_nt(ds, qm)
-        part_v += mm_nt(wb, gm)
-        ds_ref[p] = ds
-        factor_ref[p] = factor
-        delta_ref[p] = delta
+    gm = [by_head(gx_ref[:, own[p]]) for p in pairs]
+    top = [jnp.maximum(top_ref[p], top_of(s[p])) for p in pairs]
+    s = [jnp.exp(s[p] - top[p]) for p in pairs]
+    factor = [jnp.exp(top_ref[p] - top[p]) for p in pairs]
+    inverse = [1.0 / (total_ref[p] * factor[p] + total_of(s[p])) for p in pairs]
+    factor = [factor[p] * inverse[p] for p in pairs]
+    w = [s[p] * inverse[p] for p in pairs]
+    wb = [w[p].astype(BF16) for p in pairs]
+    probs = [(exp_ref[p] * factor[p]).astype(BF16) for p in pairs]
+    heads = range(width // HEAD_DIM)
+    f = [slice(h * HEAD_DIM, (h + 1) * HEAD_DIM) for h in heads]
+    c = [slice(h * PAIR, (h + 1) * PAIR) for h in heads]
+    att = [
+        jnp.concatenate(
+            [
+                mm(vt_ref[f[h], p * PAIR : (p + 2) * PAIR], probs[p][:, c[h]])
+                + mm(values_gt[f[h]], wb[p][:, c[h]])
+                for h in heads
+            ],
+            axis=0,
+        ).astype(BF16)
+        for p in pairs
+    ]
+    dprob = mm(values_g, jnp.concatenate(gm, axis=1))
+    dprob = [dprob[:, p * lanes : (p + 1) * lanes] for p in pairs]
+    part_v = mm_nt(jnp.concatenate(wb, axis=1), jnp.concatenate(gm, axis=1))
+    delta = [
+        head_sums(gx_ref[:, own[p]].astype(F32) * att[p].astype(F32)) * SCALE for p in pairs
+    ]
+    ds = [(w[p] * (dprob[p] - delta[p])).astype(BF16) for p in pairs]
+    part_k = mm_nt(jnp.concatenate(ds, axis=1), jnp.concatenate(qm, axis=1))
     part_ref[...] = (part_k + pltpu.roll(part_v, SUM_DEV, 0)) * (1.0 / SCALE)
+    for p in pairs:
+        att_ref[:, own[p]] = att[p]
+        ds_ref[p] = ds[p]
+        factor_ref[p] = factor[p]
+        delta_ref[p] = delta[p]
 
 
 def gradient_kernel(

time: 40.7 us -> 40.3 us (level)
  no operation moved by 1% of the time
where the time goes in v11:
time: 40.3 us; the launch traced here: 40 us
  starting transfers between devices  17.4 us (43%)
  blocking collectives  10.3 us (26%)
  Pallas kernels  6.57 us (16%)
  waiting for transfers between devices  5.02 us (12%)
  between operations  0.66 us (2%)
    all_to_all x2, starting transfers between devices, exchange(): lax.all_to_all(x, 'seq', split_axis=0, concat_axis=0, axis_index_groups=o...  11.2 us
    all_to_all x1, blocking collectives, local(): terms = lax.all_to_all(term, ('seq', 'head'), split_axis=0, concat_axis=0)  10.3 us
    all_to_all x2, waiting for transfers between devices, exchange(): lax.all_to_all(x, 'seq', split_axis=0, concat_axis=0, axis_index_groups=o...  3.6 us
    ppermute x1, starting transfers between devices, local(): back = lax.ppermute(edge, 'seq', down)  3.25 us
    ppermute x1, starting transfers between devices, local(): before = lax.ppermute(edge, 'seq', up)  2.99 us
    pallas_call x1, Pallas kernels, local(): pl.pallas_call(pool_kernel, out_shape=[shaped((groups, n, width), BF16),...  1.85 us
    ppermute x1, waiting for transfers between devices, local(): before = lax.ppermute(edge, 'seq', up)  1.42 us
    pallas_call x1, Pallas kernels, local(): call(global_kernel, [own, shaped((groups * n, width), F32), shaped((pairs...  1.41 us
  transfers between devices with their start and end apart: 4, of which 3 were waited for; matrix products, arithmetic and copies ran while one was open for 0% of the time, Pallas kernels for 6%

profile of v11, /device:TPU:0, one launch (start us, length us, event | category | flops | bytes accessed | tf_op | source)
XLA Modules:
  0.0 40.0 jit_solution(8403640155010209401)
XLA Ops:
  0.6 1.9 %shard_map.92 = (bf16[16,8,192]{2,1,0:T(8,128)(2,1)}, bf16[192,384]{1,0:T(8,128)(2,1)S(1)}, bf16[192,256]{1,0:T(8,128)(2,1)S(1)}, bf16[192,256]{1,0:T(8,128)(2,1...) custom-call(bf16[192,256]{1,0:T(8,128)(2,1)} %bitcast.21, ...), custom_call_target="tpu_custom_call" | custom-call | tf_op jit(solution)/shard_map/pallas_call | solution.py:358
  2.5 3.0 %collective-permute-start = (bf16[192,384]{1,0:T(8,128)(2,1)S(1)}, bf16[192,384]{1,0:T(8,128)(2,1)S(1)}, u32[]{:S(2)}, u32[]{:S(2)}) collective-permute-start(bf16[192,384]{1,0:T(8,128)(2,1)S(1)} %get-tuple-element.43), channel_id=1, source_target_pairs={{0,2},{2,4},{4,6},{6,8},{8,10},{10,12},{12,14},{14,16},{16,18},{18... | collective-permute-start | bytes 442376 | tf_op jit(solution)/shard_map/ppermute | solution.py:366
  5.5 6.4 %all-to-all-start = ((bf16[16,8,192]{2,1,0:T(8,128)(2,1)}), bf16[16,8,192]{2,1,0:T(8,128)(2,1)S(1)}, u32[]{:S(2)}, u32[]{:S(2)}) async-start(bf16[16,8,192]{2,1,0:T(8,128)(2,1)} %get-tuple-element.47), calls=%async_computation | async-start | bytes 131072 | tf_op jit(solution)/shard_map/all_to_all | solution.py:355
  11.9 1.4 %collective-permute-done.before_ref = bf16[192,384]{1,0:T(8,128)(2,1)S(1)} collective-permute-done((bf16[192,384]{1,0:T(8,128)(2,1)S(1)}, bf16[192,384]{1,0:T(8,128)(2,1)S(1)}, u32[]{:S(2)}, u32[]{:S(2)}) %collective-permute-start) | collective-permute-done | bytes 147488 | tf_op jit(solution)/shard_map/ppermute | solution.py:366
  13.3 1.1 %shard_map.93 = (f32[2,256,384]{2,1,0:T(8,128)S(1)}, f32[2,1,384]{2,1,0:T(1,128)S(1)}, f32[2,1,384]{2,1,0:T(1,128)S(1)}, bf16[192,256]{1,0:T(8,128)(2,1)S(1)}, b...) custom-call(s32[1]{0:T(128)} %bitcast.first_ref, ...), custom_call_target="tpu_custom_call" | custom-call | tf_op jit(solution)/shard_map/pallas_call | solution.py:369
  14.4 2.6 %all-to-all-done = bf16[16,8,192]{2,1,0:T(8,128)(2,1)S(1)} async-done(((bf16[16,8,192]{2,1,0:T(8,128)(2,1)}), bf16[16,8,192]{2,1,0:T(8,128)(2,1)S(1)}, u32[]{:S(2)}, u32[]{:S(2)}) %all-to-all-start) | async-done | bytes 49184 | tf_op jit(solution)/shard_map/all_to_all | solution.py:355
  17.0 1.4 %shard_map.94 = (bf16[192,256]{1,0:T(8,128)(2,1)S(1)}, f32[128,192]{1,0:T(8,128)}, bf16[2,128,384]{2,1,0:T(8,128)(2,1)S(1)}, f32[2,1,384]{2,1,0:T(1,128)S(1)}, f32[2,1,384]{2,1,0:T(1,128)S(1)}) custom-call(bf16[192,256]{1,0:T(8,128)(2,1)S(1)} %get-tuple-element.44.qx_ref, bf16[192,256]{1,0:T(8,128)(2,1)S(1)} %get-tuple-element.45.gx_ref, ...), custom_call_target="tpu_custom_call" | custom-call | tf_op jit(solution)/shard_map/pallas_call | solution.py:376
  18.4 4.8 %all-to-all-start.1 = ((f32[16,8,192]{2,1,0:T(8,128)}), f32[16,8,192]{2,1,0:T(8,128)S(1)}, u32[]{:S(2)}, u32[]{:S(2)}) async-start(f32[16,8,192]{2,1,0:T(8,128)} %bitcast.7), calls=%async_computation.1 | async-start | bytes 262144 | tf_op jit(solution)/shard_map/all_to_all | solution.py:355
  23.2 1.0 %shard_map.95 = (bf16[192,256]{1,0:T(8,128)(2,1)S(1)}, bf16[192,256]{1,0:T(8,128)(2,1)S(1)}, f32[192,256]{1,0:T(8,128)S(1)}, f32[192,256]{1,0:T(8,128)S(1)}, bf16[192,384]{1,0:T(8,128)(2,1)S(1)}) custom-call(bf16[192,256]{1,0:T(8,128)(2,1)S(1)} %get-tuple-element.44.qx_ref, bf16[192,256]{1,0:T(8,128)(2,1)S(1)} %get-tuple-element.45.gx_ref, ...), custom_call_target="tpu_custom_call" | custom-call | tf_op jit(solution)/shard_map/pallas_call | solution.py:382
  24.2 3.2 %collective-permute-start.1 = (bf16[192,384]{1,0:T(8,128)(2,1)S(1)}, bf16[192,384]{1,0:T(8,128)(2,1)S(1)}, u32[]{:S(2)}, u32[]{:S(2)}) collective-permute-start(bf16[192,384]{1,0:T(8,128)(2,1)S(1)} %get-tuple-element.64), channel_id=1, source_target_pairs={{2,0},{4,2},{6,4},{8,6},{10,8},{12,10},{14,12},{16,14},{18,16},{20... | collective-permute-start | bytes 442376 | tf_op jit(solution)/shard_map/ppermute | solution.py:387
  27.4 1.0 %all-to-all-done.1.parts_ref = f32[16,8,192]{2,1,0:T(8,128)S(1)} async-done(((f32[16,8,192]{2,1,0:T(8,128)}), f32[16,8,192]{2,1,0:T(8,128)S(1)}, u32[]{:S(2)}, u32[]{:S(2)}) %all-to-all-start.1) | async-done | bytes 98336 | tf_op jit(solution)/shard_map/all_to_all | solution.py:355
  28.4 0.2 shard_map.96
  28.7 10.3 %all_to_all.21 = f32[32,1,64]{2,1,0:T(1,128)S(1)} all-to-all(f32[32,1,64]{2,1,0:T(1,128)S(1)} %bitcast.20), channel_id=1, replica_groups=mesh['seq'=16,'head'=2] {'seq','head'}, dimensions={0} | all-to-all | bytes 16384 | tf_op jit(solution)/shard_map/all_to_all | solution.py:392
  39.0 0.0 collective-permute-done.1.back_ref
  39.0 1.0 %shard_map.98 = (bf16[192,256]{1,0:T(8,128)(2,1)}, bf16[192,256]{1,0:T(8,128)(2,1)}, bf16[192,256]{1,0:T(8,128)(2,1)}, bf16[192,256]{1,0:T(8,128)(2,1)}, f32[1,64]{1,0:T(1,128)}) custom-call(f32[8,192]{1,0:T(8,128)S(1)} %get-tuple-element.60.owned_ref, f32[192,256]{1,0:T(8,128)S(1)} %get-tuple-element.61.kg_ref, f32[192,256]{1,0:T(8,128)S(1)} %get-tuple-element.62.vg_ref, ...), custom_call_target="tpu_custom_call" | custom-call | tf_op jit(solution)/shard_map/pallas_call | solution.py:394
  (1 shorter events, 0.0 us)
Async XLA Ops:
  2.5 10.8 %collective-permute-start = (bf16[192,384]{1,0:T(8,128)(2,1)S(1)}, bf16[192,384]{1,0:T(8,128)(2,1)S(1)}, u32[]{:S(2)}, u32[]{:S(2)}) collective-permute-start(bf16[192,384]{1,0:T(8,128)(2,1)S(1)} %get-tuple-element.43), channel_id=1, source_target_pairs={{0,2},{2,4},{4,6},{6,8},{8,10},{10,12},{12,14},{14,16},{16,18},{18... | collective-permute-start | bytes 442376 | tf_op jit(solution)/shard_map/ppermute | solution.py:366
  5.5 11.5 %all-to-all-start = ((bf16[16,8,192]{2,1,0:T(8,128)(2,1)}), bf16[16,8,192]{2,1,0:T(8,128)(2,1)S(1)}, u32[]{:S(2)}, u32[]{:S(2)}) async-start(bf16[16,8,192]{2,1,0:T(8,128)(2,1)} %get-tuple-element.47), calls=%async_computation | async-start | bytes 131072 | tf_op jit(solution)/shard_map/all_to_all | solution.py:355
  18.4 10.0 %all-to-all-start.1 = ((f32[16,8,192]{2,1,0:T(8,128)}), f32[16,8,192]{2,1,0:T(8,128)S(1)}, u32[]{:S(2)}, u32[]{:S(2)}) async-start(f32[16,8,192]{2,1,0:T(8,128)} %bitcast.7), calls=%async_computation.1 | async-start | bytes 262144 | tf_op jit(solution)/shard_map/all_to_all | solution.py:355
  24.2 14.8 %collective-permute-start.1 = (bf16[192,384]{1,0:T(8,128)(2,1)S(1)}, bf16[192,384]{1,0:T(8,128)(2,1)S(1)}, u32[]{:S(2)}, u32[]{:S(2)}) collective-permute-start(bf16[192,384]{1,0:T(8,128)(2,1)S(1)} %get-tuple-element.64), channel_id=1, source_target_pairs={{2,0},{4,2},{6,4},{8,6},{10,8},{12,10},{14,12},{16,14},{18,16},{20... | collective-permute-start | bytes 442376 | tf_op jit(solution)/shard_map/ppermute | solution.py:387

commit v12 on v11

--- a/solution.py
+++ b/solution.py
@@ -250,9 +250,16 @@
         ref[:, tok - PAIR :] = grads[-1][i][:, PAIR:]
 
 
-def owned_kernel(parts_ref, k_ref, v_ref, owned_ref, term_ref):
+def outer(rows, weights):
+    n = rows.shape[0]
+    a, b = pieces(rows), pieces(weights)
+    a = [a[i * n : (i + 1) * n] for i in (0, 0, 1, 0, 1, 2)]
+    b = [b[i * n : (i + 1) * n] for i in (0, 1, 0, 2, 1, 0)]
+    return mm_tn(jnp.concatenate(a, axis=0), jnp.concatenate(b, axis=0))
+
+
+def owned_kernel(parts_ref, k_ref, v_ref, w_ref, term_ref, kp_ref, vp_ref):
     owned = jnp.sum(parts_ref[...], axis=0)
-    owned_ref[...] = owned
     split = pieces(owned)
     n = 2 * SUM_DEV
     seg = k_ref.shape[1] // SUM_DEV
@@ -266,22 +273,19 @@
     for j in range(1, SUM_DEV):
         term += total[:, j * seg : (j + 1) * seg]
     term_ref[...] = jnp.broadcast_to(term, term_ref.shape)
+    tok = k_ref.shape[1]
+    w = jnp.concatenate([w_ref[...]] * SUM_DEV, axis=1)
+    w = jnp.broadcast_to(w, (n, tok))
+    for first, ref in ((0, kp_ref), (SUM_DEV, vp_ref)):
+        ref[...] = outer(owned, jnp.where(segment_mask(first, n, tok, seg), w, 0.0))
 
 
 def sum_kernel(terms_ref, sum_ref):
     sum_ref[...] = jnp.sum(terms_ref[...], axis=0, keepdims=True)
 
 
-def outer(rows, weights):
-    n = rows.shape[0]
-    a, b = pieces(rows), pieces(weights)
-    a = [a[i * n : (i + 1) * n] for i in (0, 0, 1, 0, 1, 2)]
-    b = [b[i * n : (i + 1) * n] for i in (0, 1, 0, 2, 1, 0)]
-    return mm_tn(jnp.concatenate(a, axis=0), jnp.concatenate(b, axis=0))
-
-
 def finish_kernel(
-    owned_ref, kg_ref, vg_ref, w_ref, back_ref, atts_ref, qgs_ref, pool_ref,
+    kp_ref, vp_ref, kg_ref, vg_ref, back_ref, atts_ref, qgs_ref, pool_ref,
     key_out, value_out, att_out, qg_out, pool_out, key_ref, value_ref, att_ref, qg_ref, sem,
 ):
     copies = []
@@ -301,15 +305,11 @@
         edge = back_ref[:, 2 * PAIR + at : 2 * PAIR + at + BLOCK]
         ref[...] = jnp.concatenate([x_ref[:, tok - PAIR : tok - BLOCK], edge], axis=1)
         send(ref, out.at[:, high])
-    owned = owned_ref[...]
-    w = jnp.concatenate([w_ref[...]] * SUM_DEV, axis=1)
-    w = jnp.broadcast_to(w, (owned.shape[0], tok))
-    for first, at, grad_ref, ref, out in (
-        (0, 0, kg_ref, key_ref, key_out),
-        (SUM_DEV, PAIR, vg_ref, value_ref, value_out),
+    for at, pooled_ref, grad_ref, ref, out in (
+        (0, kp_ref, kg_ref, key_ref, key_out),
+        (PAIR, vp_ref, vg_ref, value_ref, value_out),
     ):
-        weights = jnp.where(segment_mask(first, w.shape[0], tok, w_ref.shape[1]), w, 0.0)
-        total = grad_ref[...] + outer(owned, weights)
+        total = grad_ref[...] + pooled_ref[...]
         ref[:, low] = total[:, low].astype(BF16)
         ref[:, high] = (total[:, high] + back_ref[:, at : at + PAIR].astype(F32)).astype(BF16)
         send(ref, out)
@@ -386,9 +386,9 @@
     )
     back = lax.ppermute(edge, "seq", down)
     parts, qg_own = lax.optimization_barrier((parts, qg_own))
-    owned, term = call(owned_kernel, [shaped((n, width), F32), shaped((everyone, seg), F32)], 3)(
-        parts, k, v
-    )
+    term, key_pooled, value_pooled = call(
+        owned_kernel, [shaped((everyone, seg), F32), grad, grad], 4
+    )(parts, k, v, weight_row)
     terms = lax.all_to_all(term, ("seq", "head"), split_axis=0, concat_axis=0)
     (pool_sum,) = call(sum_kernel, [shaped((1, seg), F32)], 1)(terms)
     key_grad, value_grad, attended, query_grad, pool_grad = pl.pallas_call(
@@ -400,7 +400,7 @@
         + [pltpu.VMEM((width, PAIR), BF16)] * 2
         + [pltpu.SemaphoreType.DMA((7,))],
         compiler_params=PARAMS,
-    )(owned, key_part, value_part, weight_row, back, att_own, qg_own, pool_sum)
+    )(key_pooled, value_pooled, key_part, value_part, back, att_own, qg_own, pool_sum)
     return (attended.T, query_grad.T, key_grad.T, value_grad.T, pool_grad.reshape(seg))
 
 

time: 40.3 us -> 40.2 us (level)
  no operation moved by 1% of the time
where the time goes in v12:
time: 40.2 us; the launch traced here: 39.9 us
  starting transfers between devices  17.4 us (43%)
  blocking collectives  10.3 us (26%)
  Pallas kernels  6.47 us (16%)
  waiting for transfers between devices  5.02 us (12%)
  between operations  0.67 us (2%)
    all_to_all x2, starting transfers between devices, exchange(): lax.all_to_all(x, 'seq', split_axis=0, concat_axis=0, axis_index_groups=o...  11.2 us
    all_to_all x1, blocking collectives, local(): terms = lax.all_to_all(term, ('seq', 'head'), split_axis=0, concat_axis=0)  10.3 us
    all_to_all x2, waiting for transfers between devices, exchange(): lax.all_to_all(x, 'seq', split_axis=0, concat_axis=0, axis_index_groups=o...  3.6 us
    ppermute x1, starting transfers between devices, local(): back = lax.ppermute(edge, 'seq', down)  3.25 us
    ppermute x1, starting transfers between devices, local(): before = lax.ppermute(edge, 'seq', up)  2.99 us
    pallas_call x1, Pallas kernels, local(): pl.pallas_call(pool_kernel, out_shape=[shaped((groups, n, width), BF16),...  1.85 us
    ppermute x1, waiting for transfers between devices, local(): before = lax.ppermute(edge, 'seq', up)  1.42 us
    pallas_call x1, Pallas kernels, local(): call(global_kernel, [own, shaped((groups * n, width), F32), shaped((pairs...  1.41 us
  transfers between devices with their start and end apart: 4, of which 3 were waited for; matrix products, arithmetic and copies ran while one was open for 0% of the time, Pallas kernels for 6%

profile of v12, /device:TPU:0, one launch (start us, length us, event | category | flops | bytes accessed | tf_op | source)
XLA Modules:
  0.0 39.9 jit_solution(18324359042157289450)
XLA Ops:
  0.6 1.9 %shard_map.92 = (bf16[16,8,192]{2,1,0:T(8,128)(2,1)}, bf16[192,384]{1,0:T(8,128)(2,1)S(1)}, bf16[192,256]{1,0:T(8,128)(2,1)S(1)}, bf16[192,256]{1,0:T(8,128)(2,1...) custom-call(bf16[192,256]{1,0:T(8,128)(2,1)} %bitcast.21, ...), custom_call_target="tpu_custom_call" | custom-call | tf_op jit(solution)/shard_map/pallas_call | solution.py:358
  2.5 3.0 %collective-permute-start = (bf16[192,384]{1,0:T(8,128)(2,1)S(1)}, bf16[192,384]{1,0:T(8,128)(2,1)S(1)}, u32[]{:S(2)}, u32[]{:S(2)}) collective-permute-start(bf16[192,384]{1,0:T(8,128)(2,1)S(1)} %get-tuple-element.44), channel_id=1, source_target_pairs={{0,2},{2,4},{4,6},{6,8},{8,10},{10,12},{12,14},{14,16},{16,18},{18... | collective-permute-start | bytes 442376 | tf_op jit(solution)/shard_map/ppermute | solution.py:366
  5.5 6.4 %all-to-all-start = ((bf16[16,8,192]{2,1,0:T(8,128)(2,1)}), bf16[16,8,192]{2,1,0:T(8,128)(2,1)S(1)}, u32[]{:S(2)}, u32[]{:S(2)}) async-start(bf16[16,8,192]{2,1,0:T(8,128)(2,1)} %get-tuple-element.48), calls=%async_computation | async-start | bytes 131072 | tf_op jit(solution)/shard_map/all_to_all | solution.py:355
  11.9 1.4 %collective-permute-done.before_ref = bf16[192,384]{1,0:T(8,128)(2,1)S(1)} collective-permute-done((bf16[192,384]{1,0:T(8,128)(2,1)S(1)}, bf16[192,384]{1,0:T(8,128)(2,1)S(1)}, u32[]{:S(2)}, u32[]{:S(2)}) %collective-permute-start) | collective-permute-done | bytes 147488 | tf_op jit(solution)/shard_map/ppermute | solution.py:366
  13.3 1.1 %shard_map.93 = (f32[2,256,384]{2,1,0:T(8,128)S(1)}, f32[2,1,384]{2,1,0:T(1,128)S(1)}, f32[2,1,384]{2,1,0:T(1,128)S(1)}, bf16[192,256]{1,0:T(8,128)(2,1)S(1)}, b...) custom-call(s32[1]{0:T(128)} %bitcast.first_ref, ...), custom_call_target="tpu_custom_call" | custom-call | tf_op jit(solution)/shard_map/pallas_call | solution.py:369
  14.4 2.6 %all-to-all-done = bf16[16,8,192]{2,1,0:T(8,128)(2,1)S(1)} async-done(((bf16[16,8,192]{2,1,0:T(8,128)(2,1)}), bf16[16,8,192]{2,1,0:T(8,128)(2,1)S(1)}, u32[]{:S(2)}, u32[]{:S(2)}) %all-to-all-start) | async-done | bytes 49184 | tf_op jit(solution)/shard_map/all_to_all | solution.py:355
  17.0 1.4 %shard_map.94 = (bf16[192,256]{1,0:T(8,128)(2,1)S(1)}, f32[128,192]{1,0:T(8,128)}, bf16[2,128,384]{2,1,0:T(8,128)(2,1)S(1)}, f32[2,1,384]{2,1,0:T(1,128)S(1)}, f32[2,1,384]{2,1,0:T(1,128)S(1)}) custom-call(bf16[192,256]{1,0:T(8,128)(2,1)S(1)} %get-tuple-element.45.qx_ref, bf16[192,256]{1,0:T(8,128)(2,1)S(1)} %get-tuple-element.46.gx_ref, ...), custom_call_target="tpu_custom_call" | custom-call | tf_op jit(solution)/shard_map/pallas_call | solution.py:376
  18.4 4.8 %all-to-all-start.1 = ((f32[16,8,192]{2,1,0:T(8,128)}), f32[16,8,192]{2,1,0:T(8,128)S(1)}, u32[]{:S(2)}, u32[]{:S(2)}) async-start(f32[16,8,192]{2,1,0:T(8,128)} %bitcast.7), calls=%async_computation.1 | async-start | bytes 262144 | tf_op jit(solution)/shard_map/all_to_all | solution.py:355
  23.2 1.0 %shard_map.95 = (bf16[192,256]{1,0:T(8,128)(2,1)S(1)}, bf16[192,256]{1,0:T(8,128)(2,1)S(1)}, f32[192,256]{1,0:T(8,128)S(1)}, f32[192,256]{1,0:T(8,128)S(1)}, bf16[192,384]{1,0:T(8,128)(2,1)S(1)}) custom-call(bf16[192,256]{1,0:T(8,128)(2,1)S(1)} %get-tuple-element.45.qx_ref, bf16[192,256]{1,0:T(8,128)(2,1)S(1)} %get-tuple-element.46.gx_ref, ...), custom_call_target="tpu_custom_call" | custom-call | tf_op jit(solution)/shard_map/pallas_call | solution.py:382
  24.2 3.2 %collective-permute-start.1 = (bf16[192,384]{1,0:T(8,128)(2,1)S(1)}, bf16[192,384]{1,0:T(8,128)(2,1)S(1)}, u32[]{:S(2)}, u32[]{:S(2)}) collective-permute-start(bf16[192,384]{1,0:T(8,128)(2,1)S(1)} %get-tuple-element.66), channel_id=1, source_target_pairs={{2,0},{4,2},{6,4},{8,6},{10,8},{12,10},{14,12},{16,14},{18,16},{20... | collective-permute-start | bytes 442376 | tf_op jit(solution)/shard_map/ppermute | solution.py:387
  27.4 1.0 %all-to-all-done.1.parts_ref = f32[16,8,192]{2,1,0:T(8,128)S(1)} async-done(((f32[16,8,192]{2,1,0:T(8,128)}), f32[16,8,192]{2,1,0:T(8,128)S(1)}, u32[]{:S(2)}, u32[]{:S(2)}) %all-to-all-start.1) | async-done | bytes 98336 | tf_op jit(solution)/shard_map/all_to_all | solution.py:355
  28.4 0.3 shard_map.96
  28.7 10.3 %all_to_all.21 = f32[32,1,64]{2,1,0:T(1,128)S(1)} all-to-all(f32[32,1,64]{2,1,0:T(1,128)S(1)} %bitcast.20), channel_id=1, replica_groups=mesh['seq'=16,'head'=2] {'seq','head'}, dimensions={0} | all-to-all | bytes 16384 | tf_op jit(solution)/shard_map/all_to_all | solution.py:392
  39.0 0.0 collective-permute-done.1.back_ref
  39.0 0.9 %shard_map.98 = (bf16[192,256]{1,0:T(8,128)(2,1)}, bf16[192,256]{1,0:T(8,128)(2,1)}, bf16[192,256]{1,0:T(8,128)(2,1)}, bf16[192,256]{1,0:T(8,128)(2,1)}, f32[1,64]{1,0:T(1,128)}) custom-call(f32[192,256]{1,0:T(8,128)S(1)} %get-tuple-element.62.kp_ref, f32[192,256]{1,0:T(8,128)S(1)} %get-tuple-element.63.vp_ref, f32[192,256]{1,0:T(8,128)S(1)} %get-tuple-element.64.kg_ref, ...), custom_call_target="tpu_custom_call" | custom-call | tf_op jit(solution)/shard_map/pallas_call | solution.py:394
  (1 shorter events, 0.0 us)
Async XLA Ops:
  2.5 10.8 %collective-permute-start = (bf16[192,384]{1,0:T(8,128)(2,1)S(1)}, bf16[192,384]{1,0:T(8,128)(2,1)S(1)}, u32[]{:S(2)}, u32[]{:S(2)}) collective-permute-start(bf16[192,384]{1,0:T(8,128)(2,1)S(1)} %get-tuple-element.44), channel_id=1, source_target_pairs={{0,2},{2,4},{4,6},{6,8},{8,10},{10,12},{12,14},{14,16},{16,18},{18... | collective-permute-start | bytes 442376 | tf_op jit(solution)/shard_map/ppermute | solution.py:366
  5.5 11.5 %all-to-all-start = ((bf16[16,8,192]{2,1,0:T(8,128)(2,1)}), bf16[16,8,192]{2,1,0:T(8,128)(2,1)S(1)}, u32[]{:S(2)}, u32[]{:S(2)}) async-start(bf16[16,8,192]{2,1,0:T(8,128)(2,1)} %get-tuple-element.48), calls=%async_computation | async-start | bytes 131072 | tf_op jit(solution)/shard_map/all_to_all | solution.py:355
  18.4 10.0 %all-to-all-start.1 = ((f32[16,8,192]{2,1,0:T(8,128)}), f32[16,8,192]{2,1,0:T(8,128)S(1)}, u32[]{:S(2)}, u32[]{:S(2)}) async-start(f32[16,8,192]{2,1,0:T(8,128)} %bitcast.7), calls=%async_computation.1 | async-start | bytes 262144 | tf_op jit(solution)/shard_map/all_to_all | solution.py:355
  24.2 14.9 %collective-permute-start.1 = (bf16[192,384]{1,0:T(8,128)(2,1)S(1)}, bf16[192,384]{1,0:T(8,128)(2,1)S(1)}, u32[]{:S(2)}, u32[]{:S(2)}) collective-permute-start(bf16[192,384]{1,0:T(8,128)(2,1)S(1)} %get-tuple-element.66), channel_id=1, source_target_pairs={{2,0},{4,2},{6,4},{8,6},{10,8},{12,10},{14,12},{16,14},{18,16},{20... | collective-permute-start | bytes 442376 | tf_op jit(solution)/shard_map/ppermute | solution.py:387

commit v13 on v12

--- a/solution.py
+++ b/solution.py
@@ -14,7 +14,6 @@
 SCALE = HEAD_DIM ** (-0.5)
 LOW = -1e30
 VMEM = pl.BlockSpec(memory_space=pltpu.VMEM)
-SMEM = pl.BlockSpec(memory_space=pltpu.SMEM)
 PARAMS = pltpu.CompilerParams(vmem_limit_bytes=40 * 1024 * 1024)
 F32 = jnp.float32
 BF16 = jnp.bfloat16
@@ -133,9 +132,18 @@
     return pltpu.roll(rows.astype(F32), rows.shape[0] - SUM_DEV, 0).astype(BF16)
 
 
-def local_kernel(
-    first_ref, q_ref, k_ref, v_ref, g_ref, before_ref,
-    exp_ref, top_ref, total_ref, qx_ref, gx_ref, kx_ref, vx_ref, kt_ref, vt_ref,
+def rows_kernel(rows_ref, values_ref, values_t_ref, keys_t_ref):
+    rows = rows_ref[...]
+    values = value_rows(rows)
+    values_ref[...] = values
+    values_t_ref[...] = values.T
+    keys_t_ref[...] = rows.T
+
+
+def attention_kernel(
+    q_ref, k_ref, v_ref, g_ref, before_ref, rows_ref, values_ref, values_t_ref,
+    weight_ref, qx_ref, gx_ref, vx_ref, kt_ref, att_ref, part_ref, ds_ref, delta_ref,
+    kx_ref, vt_ref,
 ):
     width, tok = q_ref.shape
     for at, t_ref, x_ref, own_ref in ((0, kt_ref, kx_ref, k_ref), (PAIR, vt_ref, vx_ref, v_ref)):
@@ -148,46 +156,35 @@
             [before_ref[:, at : at + BLOCK], own_ref[:, : tok - BLOCK]], axis=1
         )
     second = second_half(width // HEAD_DIM * PAIR)
-    is_first = first_ref[0] == 1
-    for p in range(tok // PAIR):
-        s = mm(kx_ref[p * PAIR : (p + 2) * PAIR], by_head(qx_ref[:, p * PAIR : (p + 1) * PAIR]))
+    is_first = lax.axis_index("seq") == 0
+    pairs = range(tok // PAIR)
+    own = [slice(p * PAIR, (p + 1) * PAIR) for p in pairs]
+    qm = [by_head(qx_ref[:, own[p]]) for p in pairs]
+    local = []
+    for p in pairs:
+        s = mm(kx_ref[p * PAIR : (p + 2) * PAIR], qm[p])
         parts = [s[b * BLOCK : (b + 1) * BLOCK] for b in range(4)]
         parts[0] += jnp.where(second, LOW, 0.0)
         if p == 0:
             parts[1] += jnp.where(jnp.logical_and(is_first, second), LOW, 0.0)
             parts[2] += jnp.where(jnp.logical_and(is_first, jnp.logical_not(second)), LOW, 0.0)
         parts[3] += jnp.where(second, 0.0, LOW)
-        s = jnp.concatenate(parts, axis=0)
-        top = top_of(s)
-        s = jnp.exp(s - top)
-        exp_ref[p] = s
-        top_ref[p] = top
-        total_ref[p] = total_of(s)
-
-
-def global_kernel(
-    qx_ref, gx_ref, vt_ref, rows_ref, exp_ref, top_ref, total_ref,
-    att_ref, part_ref, ds_ref, factor_ref, delta_ref,
-):
+        local.append(jnp.concatenate(parts, axis=0))
     rows = rows_ref[...]
-    width = qx_ref.shape[0]
-    pairs = range(qx_ref.shape[1] // PAIR)
-    own = [slice(p * PAIR, (p + 1) * PAIR) for p in pairs]
-    qm = [by_head(qx_ref[:, own[p]]) for p in pairs]
     s = global_scores(rows, jnp.concatenate(qm, axis=1))
     lanes = qm[0].shape[1]
     s = [s[:, p * lanes : (p + 1) * lanes] for p in pairs]
-    values_g = value_rows(rows)
-    values_gt = values_g.T
+    values_g = values_ref[...]
+    values_gt = values_t_ref[...]
     gm = [by_head(gx_ref[:, own[p]]) for p in pairs]
-    top = [jnp.maximum(top_ref[p], top_of(s[p])) for p in pairs]
+    top = [jnp.maximum(top_of(local[p]), top_of(s[p])) for p in pairs]
+    local = [jnp.exp(local[p] - top[p]) for p in pairs]
     s = [jnp.exp(s[p] - top[p]) for p in pairs]
-    factor = [jnp.exp(top_ref[p] - top[p]) for p in pairs]
-    inverse = [1.0 / (total_ref[p] * factor[p] + total_of(s[p])) for p in pairs]
-    factor = [factor[p] * inverse[p] for p in pairs]
+    inverse = [1.0 / (total_of(local[p]) + total_of(s[p])) for p in pairs]
+    local = [local[p] * inverse[p] for p in pairs]
     w = [s[p] * inverse[p] for p in pairs]
     wb = [w[p].astype(BF16) for p in pairs]
-    probs = [(exp_ref[p] * factor[p]).astype(BF16) for p in pairs]
+    probs = [local[p].astype(BF16) for p in pairs]
     heads = range(width // HEAD_DIM)
     f = [slice(h * HEAD_DIM, (h + 1) * HEAD_DIM) for h in heads]
     c = [slice(h * PAIR, (h + 1) * PAIR) for h in heads]
@@ -214,23 +211,23 @@
     for p in pairs:
         att_ref[:, own[p]] = att[p]
         ds_ref[p] = ds[p]
-        factor_ref[p] = factor[p]
+        weight_ref[p] = local[p]
         delta_ref[p] = delta[p]
 
 
 def gradient_kernel(
-    qx_ref, gx_ref, kt_ref, vx_ref, rows_ref, exp_ref, att_ref, ds_ref, factor_ref, delta_ref,
+    qx_ref, gx_ref, kt_ref, vx_ref, keys_gt_ref, weight_ref, att_ref, ds_ref, delta_ref,
     att_out_ref, qg_out_ref, kg_ref, vg_ref, back_ref,
 ):
     width, tok = kg_ref.shape
     pairs = tok // PAIR
-    rows_t = rows_ref[...].T
+    rows_t = keys_gt_ref[...]
 
     def pair(p):
         own = slice(p * PAIR, (p + 1) * PAIR)
         near = slice(p * PAIR, (p + 2) * PAIR)
         qm, gm = by_head(qx_ref[:, own]), by_head(gx_ref[:, own])
-        w = exp_ref[p] * factor_ref[p]
+        w = weight_ref[p]
         ds = (w * (mm(vx_ref[near], gm) - delta_ref[p])).astype(BF16)
         qg = own_head(mm(kt_ref[:, near], ds) + mm(rows_t, ds_ref[p])).astype(BF16)
         kg = mm_nt(qm, ds) * (1.0 / SCALE)
@@ -321,19 +318,19 @@
     return jax.ShapeDtypeStruct(shape, dtype)
 
 
-def call(kernel, outs, count, first=VMEM):
+def call(kernel, outs, count, scratch=()):
     return pl.pallas_call(
         kernel,
         out_shape=outs,
-        in_specs=[first] + [VMEM] * (count - 1),
+        in_specs=[VMEM] * count,
         out_specs=[VMEM] * len(outs),
+        scratch_shapes=list(scratch),
         compiler_params=PARAMS,
     )
 
 
 def local(queries, key_states, value_states, pool_weight, out_grad):
     tok, width = queries.shape
-    group_index = lax.axis_index("seq")
     groups = lax.axis_size("seq")
     everyone = groups * lax.axis_size("head")
     n = 2 * SUM_DEV
@@ -365,24 +362,24 @@
     )(*[pltpu.with_memory_space_constraint(x, pltpu.HBM) for x in arguments])
     before = lax.ppermute(edge, "seq", up)
     rows = exchange(summary).reshape(groups * n, width)
-    is_first = (group_index == 0).astype(jnp.int32).reshape(1)
-    exps, top, total, qx, gx, kx, vx, kt, vt = call(
-        local_kernel,
-        [shaped((pairs, 2 * PAIR, lanes), F32), stat, stat, own, own, keys, keys, keys_t, keys_t],
-        6,
-        SMEM,
-    )(is_first, q, k, v, g, before)
-
-    att_x, part, ds, factor, delta = call(
-        global_kernel,
-        [own, shaped((groups * n, width), F32), shaped((pairs, groups * n, lanes), BF16), stat, stat],
-        7,
-    )(qx, gx, vt, rows, exps, top, total)
+    values_g, values_gt, keys_gt = call(
+        rows_kernel,
+        [shaped((groups * n, width), BF16)] + [shaped((width, groups * n), BF16)] * 2,
+        1,
+    )(rows)
+    keys_gt, before = lax.optimization_barrier((keys_gt, before))
+    w, qx, gx, vx, kt, att_x, part, ds, delta = call(
+        attention_kernel,
+        [shaped((pairs, 2 * PAIR, lanes), F32), own, own, keys, keys_t, own]
+        + [shaped((groups * n, width), F32), shaped((pairs, groups * n, lanes), BF16), stat],
+        8,
+        [pltpu.VMEM(keys.shape, BF16), pltpu.VMEM(keys_t.shape, BF16)],
+    )(q, k, v, g, before, rows, values_g, values_gt)
     parts = exchange(part)
     att_own, qg_own, key_part, value_part, edge = call(
-        gradient_kernel, [own, own, grad, grad, halo], 10
+        gradient_kernel, [own, own, grad, grad, halo], 9
     )(
-        qx, gx, kt, vx, rows, exps, att_x, ds, factor, delta
+        qx, gx, kt, vx, keys_gt, w, att_x, ds, delta
     )
     back = lax.ppermute(edge, "seq", down)
     parts, qg_own = lax.optimization_barrier((parts, qg_own))

time: 40.2 us -> 39.9 us (level)
  blocking collectives: 10.3 us -> 21.7 us
  starting transfers between devices: 17.4 us -> 11 us
  waiting for transfers between devices: 5.02 us -> 1.01 us
  Pallas kernels: 6.47 us -> 5.28 us
    all_to_all x0 -> x1, blocking collectives: none -> 11.3 us  [exchange(): lax.all_to_all(x, 'seq', split_axis=0, concat_axis=0, axis_index_groups=o...]
    all_to_all x2 -> x1, starting transfers between devices: 11.2 us -> 4.77 us  [exchange(): lax.all_to_all(x, 'seq', split_axis=0, concat_axis=0, axis_index_groups=o...]
    all_to_all x2 -> x1, waiting for transfers between devices: 3.6 us -> 1.01 us  [exchange(): lax.all_to_all(x, 'seq', split_axis=0, concat_axis=0, axis_index_groups=o...]
    ppermute x1, waiting for transfers between devices: 1.42 us -> 0.01 us  [local(): before = lax.ppermute(edge, 'seq', up)]
    pallas_call x3, Pallas kernels: 3.47 us -> 2.83 us  [the longest x1 1.81 us: local(): call(attention_kernel, [shaped((pairs, 2 * PAIR, lanes), F32), own, own,...]
    pallas_call x1, Pallas kernels: 1.85 us -> 1.31 us  [local(): pl.pallas_call(pool_kernel, out_shape=[shaped((groups, n, width), BF16),...]
  transfers between devices with their start and end apart: 4 -> 3, of which waited for: 3 -> 1; matrix products, arithmetic and copies ran while one was open for 0% -> 0% of each run, Pallas kernels for 6% -> 3%
where the time goes in v13:
time: 39.9 us; the launch traced here: 39.6 us
  blocking collectives  21.7 us (54%)
  starting transfers between devices  11 us (28%)
  Pallas kernels  5.28 us (13%)
  waiting for transfers between devices  1.01 us (3%)
  between operations  0.68 us (2%)
    all_to_all x1, blocking collectives, exchange(): lax.all_to_all(x, 'seq', split_axis=0, concat_axis=0, axis_index_groups=o...  11.3 us
    all_to_all x1, blocking collectives, local(): terms = lax.all_to_all(term, ('seq', 'head'), split_axis=0, concat_axis=0)  10.3 us
    all_to_all x1, starting transfers between devices, exchange(): lax.all_to_all(x, 'seq', split_axis=0, concat_axis=0, axis_index_groups=o...  4.77 us
    ppermute x1, starting transfers between devices, local(): back = lax.ppermute(edge, 'seq', down)  3.26 us
    ppermute x1, starting transfers between devices, local(): before = lax.ppermute(edge, 'seq', up)  2.99 us
    pallas_call x1, Pallas kernels, local(): call(attention_kernel, [shaped((pairs, 2 * PAIR, lanes), F32), own, own,...  1.81 us
    pallas_call x1, Pallas kernels, local(): pl.pallas_call(pool_kernel, out_shape=[shaped((groups, n, width), BF16),...  1.31 us
    all_to_all x1, waiting for transfers between devices, exchange(): lax.all_to_all(x, 'seq', split_axis=0, concat_axis=0, axis_index_groups=o...  1.01 us
  transfers between devices with their start and end apart: 3, of which 1 were waited for; matrix products, arithmetic and copies ran while one was open for 0% of the time, Pallas kernels for 3%

profile of v13, /device:TPU:0, one launch (start us, length us, event | category | flops | bytes accessed | tf_op | source)
XLA Modules:
  0.0 39.6 jit_solution(1677748146428554763)
XLA Ops:
  0.6 1.3 %shard_map.92 = (bf16[16,8,192]{2,1,0:T(8,128)(2,1)S(1)}, bf16[192,384]{1,0:T(8,128)(2,1)S(1)}, bf16[192,256]{1,0:T(8,128)(2,1)S(1)}, bf16[192,256]{1,0:T(8,128)...) custom-call(bf16[192,256]{1,0:T(8,128)(2,1)} %bitcast.20, ...), custom_call_target="tpu_custom_call" | custom-call | tf_op jit(solution)/shard_map/pallas_call | solution.py:355
  1.9 3.0 %collective-permute-start = (bf16[192,384]{1,0:T(8,128)(2,1)S(1)}, bf16[192,384]{1,0:T(8,128)(2,1)S(1)}, u32[]{:S(2)}, u32[]{:S(2)}) collective-permute-start(bf16[192,384]{1,0:T(8,128)(2,1)S(1)} %get-tuple-element.47), channel_id=1, source_target_pairs={{0,2},{2,4},{4,6},{6,8},{8,10},{10,12},{12,14},{14,16},{16,18},{18... | collective-permute-start | bytes 442376 | tf_op jit(solution)/shard_map/ppermute | solution.py:363
  4.9 11.3 %all_to_all.21 = bf16[16,8,192]{2,1,0:T(8,128)(2,1)S(1)} all-to-all(bf16[16,8,192]{2,1,0:T(8,128)(2,1)S(1)} %get-tuple-element.45), channel_id=1, replica_groups={{16,18,20,22,24,26,28,30,14,12,10,8,6,4,2,0},{17,19,21,23,25,27,29,31,1..., dimensions={0} | all-to-all | bytes 98304 | tf_op jit(solution)/shard_map/all_to_all | solution.py:352
  16.3 0.1 shard_map.93
  16.3 0.0 collective-permute-done.before_ref
  16.4 1.8 %shard_map.94 = (f32[2,256,384]{2,1,0:T(8,128)S(1)}, bf16[192,256]{1,0:T(8,128)(2,1)S(1)}, bf16[192,256]{1,0:T(8,128)(2,1)S(1)}, bf16[384,192]{1,0:T(8,128)(2,1)...) custom-call(bf16[192,256]{1,0:T(8,128)(2,1)S(1)} %get-tuple-element., ...), custom_call_target="tpu_custom_call" | custom-call | tf_op jit(solution)/shard_map/pallas_call | solution.py:371
  18.2 4.8 %all-to-all-start.1 = ((f32[16,8,192]{2,1,0:T(8,128)}), f32[16,8,192]{2,1,0:T(8,128)S(1)}, u32[]{:S(2)}, u32[]{:S(2)}) async-start(f32[16,8,192]{2,1,0:T(8,128)} %bitcast.6), calls=%async_computation.1 | async-start | bytes 262144 | tf_op jit(solution)/shard_map/all_to_all | solution.py:352
  22.9 0.9 %shard_map.95 = (bf16[192,256]{1,0:T(8,128)(2,1)S(1)}, bf16[192,256]{1,0:T(8,128)(2,1)S(1)}, f32[192,256]{1,0:T(8,128)S(1)}, f32[192,256]{1,0:T(8,128)S(1)}, bf16[192,384]{1,0:T(8,128)(2,1)S(1)}) custom-call(bf16[192,256]{1,0:T(8,128)(2,1)S(1)} %get-tuple-element.52.qx_ref, bf16[192,256]{1,0:T(8,128)(2,1)S(1)} %get-tuple-element.53.gx_ref, ...), custom_call_target="tpu_custom_call" | custom-call | tf_op jit(solution)/shard_map/pallas_call | solution.py:379
  23.9 3.3 %collective-permute-start.1 = (bf16[192,384]{1,0:T(8,128)(2,1)S(1)}, bf16[192,384]{1,0:T(8,128)(2,1)S(1)}, u32[]{:S(2)}, u32[]{:S(2)}) collective-permute-start(bf16[192,384]{1,0:T(8,128)(2,1)S(1)} %get-tuple-element.68), channel_id=1, source_target_pairs={{2,0},{4,2},{6,4},{8,6},{10,8},{12,10},{14,12},{16,14},{18,16},{20... | collective-permute-start | bytes 442376 | tf_op jit(solution)/shard_map/ppermute | solution.py:384
  27.1 1.0 %all-to-all-done.1.parts_ref = f32[16,8,192]{2,1,0:T(8,128)S(1)} async-done(((f32[16,8,192]{2,1,0:T(8,128)}), f32[16,8,192]{2,1,0:T(8,128)S(1)}, u32[]{:S(2)}, u32[]{:S(2)}) %all-to-all-start.1) | async-done | bytes 98336 | tf_op jit(solution)/shard_map/all_to_all | solution.py:352
  28.2 0.3 shard_map.96
  28.4 10.3 %all_to_all.22 = f32[32,1,64]{2,1,0:T(1,128)S(1)} all-to-all(f32[32,1,64]{2,1,0:T(1,128)S(1)} %bitcast.19), channel_id=1, replica_groups=mesh['seq'=16,'head'=2] {'seq','head'}, dimensions={0} | all-to-all | bytes 16384 | tf_op jit(solution)/shard_map/all_to_all | solution.py:389
  38.8 0.0 collective-permute-done.1.back_ref
  38.8 0.9 %shard_map.98 = (bf16[192,256]{1,0:T(8,128)(2,1)}, bf16[192,256]{1,0:T(8,128)(2,1)}, bf16[192,256]{1,0:T(8,128)(2,1)}, bf16[192,256]{1,0:T(8,128)(2,1)}, f32[1,64]{1,0:T(1,128)}) custom-call(f32[192,256]{1,0:T(8,128)S(1)} %get-tuple-element.64.kp_ref, f32[192,256]{1,0:T(8,128)S(1)} %get-tuple-element.65.vp_ref, f32[192,256]{1,0:T(8,128)S(1)} %get-tuple-element.66.kg_ref, ...), custom_call_target="tpu_custom_call" | custom-call | tf_op jit(solution)/shard_map/pallas_call | solution.py:391
  (1 shorter events, 0.0 us)
Async XLA Ops:
  1.9 14.4 %collective-permute-start = (bf16[192,384]{1,0:T(8,128)(2,1)S(1)}, bf16[192,384]{1,0:T(8,128)(2,1)S(1)}, u32[]{:S(2)}, u32[]{:S(2)}) collective-permute-start(bf16[192,384]{1,0:T(8,128)(2,1)S(1)} %get-tuple-element.47), channel_id=1, source_target_pairs={{0,2},{2,4},{4,6},{6,8},{8,10},{10,12},{12,14},{14,16},{16,18},{18... | collective-permute-start | bytes 442376 | tf_op jit(solution)/shard_map/ppermute | solution.py:363
  18.2 10.0 %all-to-all-start.1 = ((f32[16,8,192]{2,1,0:T(8,128)}), f32[16,8,192]{2,1,0:T(8,128)S(1)}, u32[]{:S(2)}, u32[]{:S(2)}) async-start(f32[16,8,192]{2,1,0:T(8,128)} %bitcast.6), calls=%async_computation.1 | async-start | bytes 262144 | tf_op jit(solution)/shard_map/all_to_all | solution.py:352
  23.9 14.9 %collective-permute-start.1 = (bf16[192,384]{1,0:T(8,128)(2,1)S(1)}, bf16[192,384]{1,0:T(8,128)(2,1)S(1)}, u32[]{:S(2)}, u32[]{:S(2)}) collective-permute-start(bf16[192,384]{1,0:T(8,128)(2,1)S(1)} %get-tuple-element.68), channel_id=1, source_target_pairs={{2,0},{4,2},{6,4},{8,6},{10,8},{12,10},{14,12},{16,14},{18,16},{20... | collective-permute-start | bytes 442376 | tf_op jit(solution)/shard_map/ppermute | solution.py:384

commit v14 on v13

--- a/solution.py
+++ b/solution.py
@@ -146,30 +146,13 @@
     kx_ref, vt_ref,
 ):
     width, tok = q_ref.shape
-    for at, t_ref, x_ref, own_ref in ((0, kt_ref, kx_ref, k_ref), (PAIR, vt_ref, vx_ref, v_ref)):
-        t_ref[:, :PAIR] = before_ref[:, at : at + PAIR]
-        t_ref[:, PAIR:] = own_ref[...]
-        x_ref[:PAIR] = before_ref[:, at : at + PAIR].T
-        x_ref[PAIR:] = own_ref[...].T
     for at, x_ref, own_ref in ((2 * PAIR, qx_ref, q_ref), (2 * PAIR + BLOCK, gx_ref, g_ref)):
         x_ref[...] = jnp.concatenate(
             [before_ref[:, at : at + BLOCK], own_ref[:, : tok - BLOCK]], axis=1
         )
-    second = second_half(width // HEAD_DIM * PAIR)
-    is_first = lax.axis_index("seq") == 0
     pairs = range(tok // PAIR)
     own = [slice(p * PAIR, (p + 1) * PAIR) for p in pairs]
     qm = [by_head(qx_ref[:, own[p]]) for p in pairs]
-    local = []
-    for p in pairs:
-        s = mm(kx_ref[p * PAIR : (p + 2) * PAIR], qm[p])
-        parts = [s[b * BLOCK : (b + 1) * BLOCK] for b in range(4)]
-        parts[0] += jnp.where(second, LOW, 0.0)
-        if p == 0:
-            parts[1] += jnp.where(jnp.logical_and(is_first, second), LOW, 0.0)
-            parts[2] += jnp.where(jnp.logical_and(is_first, jnp.logical_not(second)), LOW, 0.0)
-        parts[3] += jnp.where(second, 0.0, LOW)
-        local.append(jnp.concatenate(parts, axis=0))
     rows = rows_ref[...]
     s = global_scores(rows, jnp.concatenate(qm, axis=1))
     lanes = qm[0].shape[1]
@@ -177,6 +160,23 @@
     values_g = values_ref[...]
     values_gt = values_t_ref[...]
     gm = [by_head(gx_ref[:, own[p]]) for p in pairs]
+    for at, t_ref, x_ref, own_ref in ((0, kt_ref, kx_ref, k_ref), (PAIR, vt_ref, vx_ref, v_ref)):
+        t_ref[:, :PAIR] = before_ref[:, at : at + PAIR]
+        t_ref[:, PAIR:] = own_ref[...]
+        x_ref[:PAIR] = before_ref[:, at : at + PAIR].T
+        x_ref[PAIR:] = own_ref[...].T
+    second = second_half(width // HEAD_DIM * PAIR)
+    is_first = lax.axis_index("seq") == 0
+    local = []
+    for p in pairs:
+        scores = mm(kx_ref[p * PAIR : (p + 2) * PAIR], qm[p])
+        parts = [scores[b * BLOCK : (b + 1) * BLOCK] for b in range(4)]
+        parts[0] += jnp.where(second, LOW, 0.0)
+        if p == 0:
+            parts[1] += jnp.where(jnp.logical_and(is_first, second), LOW, 0.0)
+            parts[2] += jnp.where(jnp.logical_and(is_first, jnp.logical_not(second)), LOW, 0.0)
+        parts[3] += jnp.where(second, 0.0, LOW)
+        local.append(jnp.concatenate(parts, axis=0))
     top = [jnp.maximum(top_of(local[p]), top_of(s[p])) for p in pairs]
     local = [jnp.exp(local[p] - top[p]) for p in pairs]
     s = [jnp.exp(s[p] - top[p]) for p in pairs]

time: 39.9 us -> 39.9 us (level)
  no operation moved by 1% of the time
where the time goes in v14:
time: 39.9 us; the launch traced here: 39.6 us
  blocking collectives  21.7 us (54%)
  starting transfers between devices  11 us (28%)
  Pallas kernels  5.21 us (13%)
  waiting for transfers between devices  1.01 us (3%)
  between operations  0.68 us (2%)
    all_to_all x1, blocking collectives, exchange(): lax.all_to_all(x, 'seq', split_axis=0, concat_axis=0, axis_index_groups=o...  11.3 us
    all_to_all x1, blocking collectives, local(): terms = lax.all_to_all(term, ('seq', 'head'), split_axis=0, concat_axis=0)  10.3 us
    all_to_all x1, starting transfers between devices, exchange(): lax.all_to_all(x, 'seq', split_axis=0, concat_axis=0, axis_index_groups=o...  4.77 us
    ppermute x1, starting transfers between devices, local(): back = lax.ppermute(edge, 'seq', down)  3.26 us
    ppermute x1, starting transfers between devices, local(): before = lax.ppermute(edge, 'seq', up)  2.99 us
    pallas_call x1, Pallas kernels, local(): call(attention_kernel, [shaped((pairs, 2 * PAIR, lanes), F32), own, own,...  1.74 us
    pallas_call x1, Pallas kernels, local(): pl.pallas_call(pool_kernel, out_shape=[shaped((groups, n, width), BF16),...  1.31 us
    all_to_all x1, waiting for transfers between devices, exchange(): lax.all_to_all(x, 'seq', split_axis=0, concat_axis=0, axis_index_groups=o...  1.01 us
  transfers between devices with their start and end apart: 3, of which 1 were waited for; matrix products, arithmetic and copies ran while one was open for 0% of the time, Pallas kernels for 3%

profile of v14, /device:TPU:0, one launch (start us, length us, event | category | flops | bytes accessed | tf_op | source)
XLA Modules:
  0.0 39.6 jit_solution(17811495737297147446)
XLA Ops:
  0.6 1.3 %shard_map.92 = (bf16[16,8,192]{2,1,0:T(8,128)(2,1)S(1)}, bf16[192,384]{1,0:T(8,128)(2,1)S(1)}, bf16[192,256]{1,0:T(8,128)(2,1)S(1)}, bf16[192,256]{1,0:T(8,128)...) custom-call(bf16[192,256]{1,0:T(8,128)(2,1)} %bitcast.20, ...), custom_call_target="tpu_custom_call" | custom-call | tf_op jit(solution)/shard_map/pallas_call | solution.py:355
  1.9 3.0 %collective-permute-start = (bf16[192,384]{1,0:T(8,128)(2,1)S(1)}, bf16[192,384]{1,0:T(8,128)(2,1)S(1)}, u32[]{:S(2)}, u32[]{:S(2)}) collective-permute-start(bf16[192,384]{1,0:T(8,128)(2,1)S(1)} %get-tuple-element.47), channel_id=1, source_target_pairs={{0,2},{2,4},{4,6},{6,8},{8,10},{10,12},{12,14},{14,16},{16,18},{18... | collective-permute-start | bytes 442376 | tf_op jit(solution)/shard_map/ppermute | solution.py:363
  4.9 11.3 %all_to_all.21 = bf16[16,8,192]{2,1,0:T(8,128)(2,1)S(1)} all-to-all(bf16[16,8,192]{2,1,0:T(8,128)(2,1)S(1)} %get-tuple-element.45), channel_id=1, replica_groups={{16,18,20,22,24,26,28,30,14,12,10,8,6,4,2,0},{17,19,21,23,25,27,29,31,1..., dimensions={0} | all-to-all | bytes 98304 | tf_op jit(solution)/shard_map/all_to_all | solution.py:352
  16.3 0.1 shard_map.93
  16.3 0.0 collective-permute-done.before_ref
  16.4 1.7 %shard_map.94 = (f32[2,256,384]{2,1,0:T(8,128)S(1)}, bf16[192,256]{1,0:T(8,128)(2,1)S(1)}, bf16[192,256]{1,0:T(8,128)(2,1)S(1)}, bf16[384,192]{1,0:T(8,128)(2,1)...) custom-call(bf16[192,256]{1,0:T(8,128)(2,1)S(1)} %get-tuple-element., ...), custom_call_target="tpu_custom_call" | custom-call | tf_op jit(solution)/shard_map/pallas_call | solution.py:371
  18.1 4.8 %all-to-all-start.1 = ((f32[16,8,192]{2,1,0:T(8,128)}), f32[16,8,192]{2,1,0:T(8,128)S(1)}, u32[]{:S(2)}, u32[]{:S(2)}) async-start(f32[16,8,192]{2,1,0:T(8,128)} %bitcast.6), calls=%async_computation.1 | async-start | bytes 262144 | tf_op jit(solution)/shard_map/all_to_all | solution.py:352
  22.9 0.9 %shard_map.95 = (bf16[192,256]{1,0:T(8,128)(2,1)S(1)}, bf16[192,256]{1,0:T(8,128)(2,1)S(1)}, f32[192,256]{1,0:T(8,128)S(1)}, f32[192,256]{1,0:T(8,128)S(1)}, bf16[192,384]{1,0:T(8,128)(2,1)S(1)}) custom-call(bf16[192,256]{1,0:T(8,128)(2,1)S(1)} %get-tuple-element.52.qx_ref, bf16[192,256]{1,0:T(8,128)(2,1)S(1)} %get-tuple-element.53.gx_ref, ...), custom_call_target="tpu_custom_call" | custom-call | tf_op jit(solution)/shard_map/pallas_call | solution.py:379
  23.8 3.3 %collective-permute-start.1 = (bf16[192,384]{1,0:T(8,128)(2,1)S(1)}, bf16[192,384]{1,0:T(8,128)(2,1)S(1)}, u32[]{:S(2)}, u32[]{:S(2)}) collective-permute-start(bf16[192,384]{1,0:T(8,128)(2,1)S(1)} %get-tuple-element.68), channel_id=1, source_target_pairs={{2,0},{4,2},{6,4},{8,6},{10,8},{12,10},{14,12},{16,14},{18,16},{20... | collective-permute-start | bytes 442376 | tf_op jit(solution)/shard_map/ppermute | solution.py:384
  27.1 1.0 %all-to-all-done.1.parts_ref = f32[16,8,192]{2,1,0:T(8,128)S(1)} async-done(((f32[16,8,192]{2,1,0:T(8,128)}), f32[16,8,192]{2,1,0:T(8,128)S(1)}, u32[]{:S(2)}, u32[]{:S(2)}) %all-to-all-start.1) | async-done | bytes 98336 | tf_op jit(solution)/shard_map/all_to_all | solution.py:352
  28.1 0.3 shard_map.96
  28.3 10.3 %all_to_all.22 = f32[32,1,64]{2,1,0:T(1,128)S(1)} all-to-all(f32[32,1,64]{2,1,0:T(1,128)S(1)} %bitcast.19), channel_id=1, replica_groups=mesh['seq'=16,'head'=2] {'seq','head'}, dimensions={0} | all-to-all | bytes 16384 | tf_op jit(solution)/shard_map/all_to_all | solution.py:389
  38.7 0.0 collective-permute-done.1.back_ref
  38.7 0.9 %shard_map.98 = (bf16[192,256]{1,0:T(8,128)(2,1)}, bf16[192,256]{1,0:T(8,128)(2,1)}, bf16[192,256]{1,0:T(8,128)(2,1)}, bf16[192,256]{1,0:T(8,128)(2,1)}, f32[1,64]{1,0:T(1,128)}) custom-call(f32[192,256]{1,0:T(8,128)S(1)} %get-tuple-element.64.kp_ref, f32[192,256]{1,0:T(8,128)S(1)} %get-tuple-element.65.vp_ref, f32[192,256]{1,0:T(8,128)S(1)} %get-tuple-element.66.kg_ref, ...), custom_call_target="tpu_custom_call" | custom-call | tf_op jit(solution)/shard_map/pallas_call | solution.py:391
  (1 shorter events, 0.0 us)
Async XLA Ops:
  1.9 14.4 %collective-permute-start = (bf16[192,384]{1,0:T(8,128)(2,1)S(1)}, bf16[192,384]{1,0:T(8,128)(2,1)S(1)}, u32[]{:S(2)}, u32[]{:S(2)}) collective-permute-start(bf16[192,384]{1,0:T(8,128)(2,1)S(1)} %get-tuple-element.47), channel_id=1, source_target_pairs={{0,2},{2,4},{4,6},{6,8},{8,10},{10,12},{12,14},{14,16},{16,18},{18... | collective-permute-start | bytes 442376 | tf_op jit(solution)/shard_map/ppermute | solution.py:363
  18.1 10.0 %all-to-all-start.1 = ((f32[16,8,192]{2,1,0:T(8,128)}), f32[16,8,192]{2,1,0:T(8,128)S(1)}, u32[]{:S(2)}, u32[]{:S(2)}) async-start(f32[16,8,192]{2,1,0:T(8,128)} %bitcast.6), calls=%async_computation.1 | async-start | bytes 262144 | tf_op jit(solution)/shard_map/all_to_all | solution.py:352
  23.8 14.9 %collective-permute-start.1 = (bf16[192,384]{1,0:T(8,128)(2,1)S(1)}, bf16[192,384]{1,0:T(8,128)(2,1)S(1)}, u32[]{:S(2)}, u32[]{:S(2)}) collective-permute-start(bf16[192,384]{1,0:T(8,128)(2,1)S(1)} %get-tuple-element.68), channel_id=1, source_target_pairs={{2,0},{4,2},{6,4},{8,6},{10,8},{12,10},{14,12},{16,14},{18,16},{20... | collective-permute-start | bytes 442376 | tf_op jit(solution)/shard_map/ppermute | solution.py:384

commit v15 on v14

--- a/solution.py
+++ b/solution.py
@@ -54,17 +54,18 @@
     ]
     for i in (4, 1, 2, 0, 3):
         copies[i].start()
-    for i in (4, 1, 2):
-        copies[i].wait()
+    copies[4].wait()
     seg = w_ref.shape[1]
     n = 2 * SUM_DEV
     w = jnp.concatenate([w_ref[...]] * SUM_DEV, axis=1)
     w = jnp.broadcast_to(w, (n, w.shape[1]))
-    pooled = jnp.zeros((n, k_ref.shape[0]), F32)
-    for first, ref in ((0, k_ref), (SUM_DEV, v_ref)):
-        weights = jnp.where(segment_mask(first, w.shape[0], w.shape[1], seg), w, 0.0)
-        parts = mm_nt(pieces(weights), ref[...])
-        pooled += parts[:n] + parts[n : 2 * n] + parts[2 * n :]
+    weights = [
+        pieces(jnp.where(segment_mask(first, n, w.shape[1], seg), w, 0.0)) for first in (0, SUM_DEV)
+    ]
+    copies[1].wait()
+    copies[2].wait()
+    pooled = mm_nt(weights[0], k_ref[...]) + mm_nt(weights[1], v_ref[...])
+    pooled = pooled[:n] + pooled[n : 2 * n] + pooled[2 * n :]
     rows_ref[...] = jnp.broadcast_to(pooled.astype(BF16)[None], rows_ref.shape)
     copies[0].wait()
     copies[3].wait()

time: 39.9 us -> 39.8 us (level)
  no operation moved by 1% of the time
where the time goes in v15:
time: 39.8 us; the launch traced here: 39.6 us
  blocking collectives  21.7 us (55%)
  starting transfers between devices  11 us (28%)
  Pallas kernels  5.19 us (13%)
  waiting for transfers between devices  1.01 us (3%)
  between operations  0.68 us (2%)
    all_to_all x1, blocking collectives, exchange(): lax.all_to_all(x, 'seq', split_axis=0, concat_axis=0, axis_index_groups=o...  11.3 us
    all_to_all x1, blocking collectives, local(): terms = lax.all_to_all(term, ('seq', 'head'), split_axis=0, concat_axis=0)  10.3 us
    all_to_all x1, starting transfers between devices, exchange(): lax.all_to_all(x, 'seq', split_axis=0, concat_axis=0, axis_index_groups=o...  4.77 us
    ppermute x1, starting transfers between devices, local(): back = lax.ppermute(edge, 'seq', down)  3.26 us
    ppermute x1, starting transfers between devices, local(): before = lax.ppermute(edge, 'seq', up)  2.99 us
    pallas_call x1, Pallas kernels, local(): call(attention_kernel, [shaped((pairs, 2 * PAIR, lanes), F32), own, own,...  1.74 us
    pallas_call x1, Pallas kernels, local(): pl.pallas_call(pool_kernel, out_shape=[shaped((groups, n, width), BF16),...  1.28 us
    all_to_all x1, waiting for transfers between devices, exchange(): lax.all_to_all(x, 'seq', split_axis=0, concat_axis=0, axis_index_groups=o...  1.01 us
  transfers between devices with their start and end apart: 3, of which 1 were waited for; matrix products, arithmetic and copies ran while one was open for 0% of the time, Pallas kernels for 3%

profile of v15, /device:TPU:0, one launch (start us, length us, event | category | flops | bytes accessed | tf_op | source)
XLA Modules:
  0.0 39.6 jit_solution(973483404737745840)
XLA Ops:
  0.6 1.3 %shard_map.92 = (bf16[16,8,192]{2,1,0:T(8,128)(2,1)S(1)}, bf16[192,384]{1,0:T(8,128)(2,1)S(1)}, bf16[192,256]{1,0:T(8,128)(2,1)S(1)}, bf16[192,256]{1,0:T(8,128)...) custom-call(bf16[192,256]{1,0:T(8,128)(2,1)} %bitcast.20, ...), custom_call_target="tpu_custom_call" | custom-call | tf_op jit(solution)/shard_map/pallas_call | solution.py:356
  1.9 3.0 %collective-permute-start = (bf16[192,384]{1,0:T(8,128)(2,1)S(1)}, bf16[192,384]{1,0:T(8,128)(2,1)S(1)}, u32[]{:S(2)}, u32[]{:S(2)}) collective-permute-start(bf16[192,384]{1,0:T(8,128)(2,1)S(1)} %get-tuple-element.47), channel_id=1, source_target_pairs={{0,2},{2,4},{4,6},{6,8},{8,10},{10,12},{12,14},{14,16},{16,18},{18... | collective-permute-start | bytes 442376 | tf_op jit(solution)/shard_map/ppermute | solution.py:364
  4.9 11.3 %all_to_all.21 = bf16[16,8,192]{2,1,0:T(8,128)(2,1)S(1)} all-to-all(bf16[16,8,192]{2,1,0:T(8,128)(2,1)S(1)} %get-tuple-element.45), channel_id=1, replica_groups={{16,18,20,22,24,26,28,30,14,12,10,8,6,4,2,0},{17,19,21,23,25,27,29,31,1..., dimensions={0} | all-to-all | bytes 98304 | tf_op jit(solution)/shard_map/all_to_all | solution.py:353
  16.2 0.1 shard_map.93
  16.3 0.0 collective-permute-done.before_ref
  16.3 1.7 %shard_map.94 = (f32[2,256,384]{2,1,0:T(8,128)S(1)}, bf16[192,256]{1,0:T(8,128)(2,1)S(1)}, bf16[192,256]{1,0:T(8,128)(2,1)S(1)}, bf16[384,192]{1,0:T(8,128)(2,1)...) custom-call(bf16[192,256]{1,0:T(8,128)(2,1)S(1)} %get-tuple-element., ...), custom_call_target="tpu_custom_call" | custom-call | tf_op jit(solution)/shard_map/pallas_call | solution.py:372
  18.1 4.8 %all-to-all-start.1 = ((f32[16,8,192]{2,1,0:T(8,128)}), f32[16,8,192]{2,1,0:T(8,128)S(1)}, u32[]{:S(2)}, u32[]{:S(2)}) async-start(f32[16,8,192]{2,1,0:T(8,128)} %bitcast.6), calls=%async_computation.1 | async-start | bytes 262144 | tf_op jit(solution)/shard_map/all_to_all | solution.py:353
  22.8 0.9 %shard_map.95 = (bf16[192,256]{1,0:T(8,128)(2,1)S(1)}, bf16[192,256]{1,0:T(8,128)(2,1)S(1)}, f32[192,256]{1,0:T(8,128)S(1)}, f32[192,256]{1,0:T(8,128)S(1)}, bf16[192,384]{1,0:T(8,128)(2,1)S(1)}) custom-call(bf16[192,256]{1,0:T(8,128)(2,1)S(1)} %get-tuple-element.52.qx_ref, bf16[192,256]{1,0:T(8,128)(2,1)S(1)} %get-tuple-element.53.gx_ref, ...), custom_call_target="tpu_custom_call" | custom-call | tf_op jit(solution)/shard_map/pallas_call | solution.py:380
  23.8 3.3 %collective-permute-start.1 = (bf16[192,384]{1,0:T(8,128)(2,1)S(1)}, bf16[192,384]{1,0:T(8,128)(2,1)S(1)}, u32[]{:S(2)}, u32[]{:S(2)}) collective-permute-start(bf16[192,384]{1,0:T(8,128)(2,1)S(1)} %get-tuple-element.68), channel_id=1, source_target_pairs={{2,0},{4,2},{6,4},{8,6},{10,8},{12,10},{14,12},{16,14},{18,16},{20... | collective-permute-start | bytes 442376 | tf_op jit(solution)/shard_map/ppermute | solution.py:385
  27.1 1.0 %all-to-all-done.1.parts_ref = f32[16,8,192]{2,1,0:T(8,128)S(1)} async-done(((f32[16,8,192]{2,1,0:T(8,128)}), f32[16,8,192]{2,1,0:T(8,128)S(1)}, u32[]{:S(2)}, u32[]{:S(2)}) %all-to-all-start.1) | async-done | bytes 98336 | tf_op jit(solution)/shard_map/all_to_all | solution.py:353
  28.1 0.3 shard_map.96
  28.3 10.3 %all_to_all.22 = f32[32,1,64]{2,1,0:T(1,128)S(1)} all-to-all(f32[32,1,64]{2,1,0:T(1,128)S(1)} %bitcast.19), channel_id=1, replica_groups=mesh['seq'=16,'head'=2] {'seq','head'}, dimensions={0} | all-to-all | bytes 16384 | tf_op jit(solution)/shard_map/all_to_all | solution.py:390
  38.7 0.0 collective-permute-done.1.back_ref
  38.7 0.9 %shard_map.98 = (bf16[192,256]{1,0:T(8,128)(2,1)}, bf16[192,256]{1,0:T(8,128)(2,1)}, bf16[192,256]{1,0:T(8,128)(2,1)}, bf16[192,256]{1,0:T(8,128)(2,1)}, f32[1,64]{1,0:T(1,128)}) custom-call(f32[192,256]{1,0:T(8,128)S(1)} %get-tuple-element.64.kp_ref, f32[192,256]{1,0:T(8,128)S(1)} %get-tuple-element.65.vp_ref, f32[192,256]{1,0:T(8,128)S(1)} %get-tuple-element.66.kg_ref, ...), custom_call_target="tpu_custom_call" | custom-call | tf_op jit(solution)/shard_map/pallas_call | solution.py:392
  (1 shorter events, 0.0 us)
Async XLA Ops:
  1.9 14.4 %collective-permute-start = (bf16[192,384]{1,0:T(8,128)(2,1)S(1)}, bf16[192,384]{1,0:T(8,128)(2,1)S(1)}, u32[]{:S(2)}, u32[]{:S(2)}) collective-permute-start(bf16[192,384]{1,0:T(8,128)(2,1)S(1)} %get-tuple-element.47), channel_id=1, source_target_pairs={{0,2},{2,4},{4,6},{6,8},{8,10},{10,12},{12,14},{14,16},{16,18},{18... | collective-permute-start | bytes 442376 | tf_op jit(solution)/shard_map/ppermute | solution.py:364
  18.1 10.0 %all-to-all-start.1 = ((f32[16,8,192]{2,1,0:T(8,128)}), f32[16,8,192]{2,1,0:T(8,128)S(1)}, u32[]{:S(2)}, u32[]{:S(2)}) async-start(f32[16,8,192]{2,1,0:T(8,128)} %bitcast.6), calls=%async_computation.1 | async-start | bytes 262144 | tf_op jit(solution)/shard_map/all_to_all | solution.py:353
  23.8 14.9 %collective-permute-start.1 = (bf16[192,384]{1,0:T(8,128)(2,1)S(1)}, bf16[192,384]{1,0:T(8,128)(2,1)S(1)}, u32[]{:S(2)}, u32[]{:S(2)}) collective-permute-start(bf16[192,384]{1,0:T(8,128)(2,1)S(1)} %get-tuple-element.68), channel_id=1, source_target_pairs={{2,0},{4,2},{6,4},{8,6},{10,8},{12,10},{14,12},{16,14},{18,16},{20... | collective-permute-start | bytes 442376 | tf_op jit(solution)/shard_map/ppermute | solution.py:385
